TPU v7x, 128 devices: a whole 4x4x4 slice. The times are simulated.
128 devices in a mesh: gx: 4 (over z), gy: 4 (over y), gz: 8 (over x, core).
Axes of the slice: x: 4, y: 4, z: 4, core: 2. Of those that a mesh axis runs over, the one named last changes fastest.
Arguments:
- rhs_old: float32 [512, 196608], P(None, ('gx', 'gy', 'gz'))
- diagonal_old: float32 [512, 196608], P(None, ('gx', 'gy', 'gz')), may hold values from 0.02 to 2
- new_owner: int32 [196608], P(('gx', 'gy', 'gz')), may hold values from -1 to 127, as said below
- face_source: int32 [6, 131072], P(None, ('gx', 'gy', 'gz')), may hold values from 0 to 6656, as said below
- send_layers: int32 [2, 32768], P(None, ('gx', 'gy', 'gz')), may hold values from 0 to 6143, as said below
- block_inverse: float32 [512, 512], replicated
Outputs:
- solution: float32 [512, 131072], P(None, ('gx', 'gy', 'gz'))
- residual: float32 [512, 131072], P(None, ('gx', 'gy', 'gz'))
Inputs may be any that keep to these rules, and one draw needn't show every extreme that they name: `new_owner`: A device's 1536 slots hold, in order, the blocks it hands to device e - 1, those it keeps, those it hands to device e + 1, then empty slots (-1). It hands at most 256 to each neighbour; device 0 hands none down, the last device none up, device 1 hands exactly 256 down and device 0 exactly 256 up; every device ends with exactly 1024 blocks. `face_source`: A device reads at most 256 layers through the codes of each neighbour, each such code at most once; device 1 reads all 256 from device 0, device 0 all 256 from device 1; device 0 reads none from below, the last device none from above. The layer named for face g is always face g xor 1 of its block. `send_layers`: entries are local layer codes g * 1024 + k; entries that no face_source code reads are arbitrary layers.
All inputs are finite; a program needn't handle non-finite values.
Results may differ from a plain program's by a relative error of at most 0.00014.
Values sent between devices are 32-bit elements; how exact they have to be, the bound alone decides.
No kernel may reach another device: no remote copies, remote signals or barrier semaphores. Data moves between devices by JAX's collectives and lax.ppermute only.
A program may use at most 128 MiB of HBM per device.

v0:
```python
import jax
import jax.numpy as jnp
from jax import lax
from jax.sharding import PartitionSpec as P

BE = 8
BCELLS = 512
FACE = 64
BDEV = 1024
MOVE = 256
HMAX = 256
ITERS = 2


def shifted(value, axis, steps):
    count = lax.axis_size(axis)
    initial, last = (max(0, -steps), min(count, count - steps))
    return lax.ppermute(value, axis, [(source, source + steps) for source in range(initial, last)])


def split_faces(field):
    columns = field.shape[1]
    volume = field.reshape(BE, BE, BE, columns)
    return [
        volume[0].reshape(FACE, columns),
        volume[BE - 1].reshape(FACE, columns),
        volume[:, 0].reshape(FACE, columns),
        volume[:, BE - 1].reshape(FACE, columns),
        volume[:, :, 0].reshape(FACE, columns),
        volume[:, :, BE - 1].reshape(FACE, columns),
    ]


def apply_operator(field, diagonal, outside):
    columns = field.shape[1]
    volume = field.reshape(BE, BE, BE, columns)
    beside = jnp.concatenate([outside[0].reshape(1, BE, BE, columns), volume[:-1]], axis=0)
    beside = beside + jnp.concatenate([volume[1:], outside[1].reshape(1, BE, BE, columns)], axis=0)
    beside = beside + jnp.concatenate(
        [outside[2].reshape(BE, 1, BE, columns), volume[:, :-1]], axis=1
    )
    beside = beside + jnp.concatenate(
        [volume[:, 1:], outside[3].reshape(BE, 1, BE, columns)], axis=1
    )
    beside = beside + jnp.concatenate(
        [outside[4].reshape(BE, BE, 1, columns), volume[:, :, :-1]], axis=2
    )
    beside = beside + jnp.concatenate(
        [volume[:, :, 1:], outside[5].reshape(BE, BE, 1, columns)], axis=2
    )
    return (6.0 + diagonal) * field - beside.reshape(field.shape)


def select_dot(values, selector):
    return jnp.dot(
        values, selector, precision=lax.Precision.HIGHEST, preferred_element_type=jnp.float32
    )


def per_device(rhs_old, diagonal_old, new_owner, face_source, send_layers, block_inverse):

    def precondition(field):
        return jnp.dot(
            block_inverse,
            field,
            precision=lax.Precision.HIGHEST,
            preferred_element_type=jnp.float32,
        )

    my_rank = lax.axis_index(("gx", "gy", "gz"))
    filled = new_owner >= 0
    head = jnp.sum(((new_owner == my_rank - 1) & filled).astype(jnp.int32))
    stay = jnp.sum((new_owner == my_rank).astype(jnp.int32))
    tail = jnp.sum(((new_owner == my_rank + 1) & filled).astype(jnp.int32))
    stacked = jnp.stack([rhs_old, diagonal_old])
    layers_count = stacked.shape[0]
    lower_part = stacked[:, :, :MOVE]
    upper_part = lax.dynamic_slice_in_dim(stacked, head + stay, MOVE, 2)
    from_upper = shifted(lower_part, ("gx", "gy", "gz"), -1)
    from_lower, tail_prev = shifted((upper_part, tail.reshape(1)), ("gx", "gy", "gz"), 1)
    before_count = tail_prev[0]
    column = jnp.arange(BDEV, dtype=jnp.int32)[None, None, :]
    lower_wide = jnp.concatenate(
        [from_lower, jnp.zeros((layers_count, BCELLS, BDEV - MOVE), jnp.float32)], axis=2
    )
    own_padded = jnp.concatenate(
        [jnp.zeros((layers_count, BCELLS, MOVE), jnp.float32), stacked], axis=2
    )
    own_wide = lax.dynamic_slice_in_dim(own_padded, MOVE + head - before_count, BDEV, 2)
    upper_padded = jnp.concatenate(
        [jnp.zeros((layers_count, BCELLS, BDEV), jnp.float32), from_upper], axis=2
    )
    upper_wide = lax.dynamic_slice_in_dim(upper_padded, BDEV - before_count - stay, BDEV, 2)
    moved = jnp.where(
        column < before_count,
        lower_wide,
        jnp.where(column < before_count + stay, own_wide, upper_wide),
    )
    rhs = moved[0]
    diagonal = moved[1]
    first_search = precondition(rhs)
    send_codes = send_layers.reshape(-1)
    block_rows = jnp.arange(BDEV, dtype=jnp.int32)[:, None]
    halo_rows = jnp.arange(2 * HMAX, dtype=jnp.int32)[:, None]

    def operate(field):
        faces = split_faces(field)
        packed = jnp.zeros((FACE, 2 * HMAX), jnp.float32)
        for which in range(6):
            chooser = (send_codes[None, :] == which * BDEV + block_rows).astype(jnp.float32)
            packed = packed + select_dot(faces[which], chooser)
        from_above = shifted(packed[:, :HMAX], ("gx", "gy", "gz"), -1)
        from_below = shifted(packed[:, HMAX:], ("gx", "gy", "gz"), 1)
        remote = jnp.concatenate([from_below, from_above], axis=1)
        outside = []
        for which in range(6):
            codes = face_source[which][None, :]
            partner = which ^ 1
            local_pick = (codes == partner * BDEV + block_rows).astype(jnp.float32)
            remote_pick = (codes == 6 * BDEV + halo_rows).astype(jnp.float32)
            outside.append(select_dot(faces[partner], local_pick) + select_dot(remote, remote_pick))
        return apply_operator(field, diagonal, outside)

    solution = jnp.zeros_like(rhs)
    residual = rhs
    rho = lax.psum(jnp.sum(rhs * residual), ("gx", "gy", "gz"))
    direction = residual
    along = jnp.zeros_like(rhs)
    alpha = jnp.float32(1.0)
    omega = jnp.float32(1.0)
    rho_next = rho
    for step in range(ITERS):
        if step > 0:
            beta = rho_next / rho * (alpha / omega)
            rho = rho_next
            direction = residual + beta * (direction - omega * along)
        search = first_search if step == 0 else precondition(direction)
        along = operate(search)
        alpha = rho / lax.psum(jnp.sum(rhs * along), ("gx", "gy", "gz"))
        middle = residual - alpha * along
        middle_pre = precondition(middle)
        image = operate(middle_pre)
        stats = lax.psum((jnp.sum(image * middle), jnp.sum(image * image)), ("gx", "gy", "gz"))
        omega = stats[0] / stats[1]
        residual = middle - omega * image
        if step + 1 < ITERS:
            rho_next = lax.psum(jnp.sum(rhs * residual), ("gx", "gy", "gz"))
        solution = solution + alpha * search + omega * middle_pre
    return (solution, residual)


def solution(mesh):
    return jax.shard_map(
        per_device,
        mesh=mesh,
        in_specs=(
            P(None, ("gx", "gy", "gz")),
            P(None, ("gx", "gy", "gz")),
            P(("gx", "gy", "gz")),
            P(None, ("gx", "gy", "gz")),
            P(None, ("gx", "gy", "gz")),
            P(),
        ),
        out_specs=(P(None, ("gx", "gy", "gz")), P(None, ("gx", "gy", "gz"))),
        check_vma=False,
    )
```

profile of v0, /device:TPU:1, one launch (start us, length us, event | category | flops | bytes accessed | tf_op | source)
XLA Modules:
  0.0 570.2 jit_solution(2789913245630111823)
XLA Ops:
  2.1 4.5 collective-permute-start
  8.0 2.1 fusion.369
  12.0 3.4 collective-permute-start.2
  16.1 6.0 %pad_maximum_fusion = f32[2,512,1536]{2,1,0:T(8,128)} fusion(f32[1,512,1536]{2,1,0:T(8,128)} %bitcast.312, f32[1,512,1536]{2,1,0:T(8,128)} %bitcast.310), kind=kLoop, calls=%fused_computation.2 | loop fusion | flops 1572864 | bytes 12582912 | tf_op jit(solution)/shard_map/stack | solution.py:75
  26.1 2.1 collective-permute-done.2
  28.2 5.1 fusion.41
  33.3 3.5 fusion.204
  56.2 2.4 collective-permute-start.4
  58.6 3.1 collective-permute-done.4
  69.6 2.9 multiply_reduce_fusion.6
  72.5 74.7 %all-reduce.5 = (f32[]{:T(128)}, f32[]{:T(128)}) all-reduce(f32[]{:T(128)} %get-tuple-element.3, f32[]{:T(128)} %get-tuple-element.2), channel_id=1, replica_groups=mesh['gx'=4,'gy'=4,'gz'=8] {'gx','gy','gz'}, use_global_device_ids=true, to_apply=%region_4.5 | all-reduce | flops 2 | bytes 16 | tf_op jit(solution)/shard_map/psum | solution.py:126
  148.3 2.7 multiply_subtract_fusion.3
  151.0 3.5 fusion.534
  170.2 3.3 collective-permute-start.5
  177.1 3.6 collective-permute-done.6
  188.9 3.0 multiply_reduce_fusion.4
  191.9 69.3 %all-reduce.4 = (f32[]{:T(128)}, f32[]{:T(128)}) all-reduce(f32[]{:T(128)} %get-tuple-element.7, f32[]{:T(128)} %get-tuple-element.6), channel_id=1, replica_groups=mesh['gx'=4,'gy'=4,'gz'=8] {'gx','gy','gz'}, use_global_device_ids=true, to_apply=%region_8.9 | all-reduce | flops 2 | bytes 16 | tf_op jit(solution)/shard_map/psum | solution.py:143
  263.6 3.3 multiply_reduce_fusion.3
  268.1 64.3 %psum.60 = f32[]{:T(128)} all-reduce(f32[]{:T(128)} %multiply_reduce_fusion.3), channel_id=1, replica_groups=mesh['gx'=4,'gy'=4,'gz'=8] {'gx','gy','gz'}, use_global_device_ids=true, to_apply=%region_12.13 | all-reduce | flops 1 | bytes 8 | tf_op jit(solution)/shard_map/psum | solution.py:147
  333.6 6.9 %fusion.151 = f32[1024,512]{0,1:T(8,128)S(1)} fusion(f32[512,512]{1,0:T(8,128)S(1)} %copy-done, f32[512,1024]{1,0:T(8,128)} %get-tuple-element.19, f32[2,512,1024]{2,1,0:T(8,128)} %copy-done.1, f32[512,1024]{1,0:T(8,128)} %copy-done.8, f32[512,1024]{1,0:T(8,128)} %get-tuple-element.18, f32[]{:T(128)S(6)} %mul.110, f32[]{:T(128)S(6)} %div.19), kind=kOutput, calls=%fused_computation.175 | convolution fusion | flops 3224371200 | bytes 11534344 | tf_op jit(solution)/shard_map/dot_general | solution.py:63
  355.9 2.1 collective-permute-start.7
  359.6 2.4 collective-permute-start.8
  362.1 3.1 collective-permute-done.8
  376.1 70.1 %psum.61 = f32[]{:T(128)} all-reduce(f32[]{:T(128)} %multiply_reduce_fusion.2), channel_id=1, replica_groups=mesh['gx'=4,'gy'=4,'gz'=8] {'gx','gy','gz'}, use_global_device_ids=true, to_apply=%region_14.15 | all-reduce | flops 1 | bytes 8 | tf_op jit(solution)/shard_map/psum | solution.py:139
  447.3 4.7 multiply_subtract_fusion.1
  452.1 3.5 fusion.535
  475.1 2.4 collective-permute-start.10
  477.5 3.2 collective-permute-done.10
  486.7 2.0 fusion.150
  488.8 2.8 multiply_reduce_fusion
  491.6 69.9 %all-reduce.3 = (f32[]{:T(128)}, f32[]{:T(128)}) all-reduce(f32[]{:T(128)} %get-tuple-element.5, f32[]{:T(128)} %get-tuple-element.4), channel_id=1, replica_groups=mesh['gx'=4,'gy'=4,'gz'=8] {'gx','gy','gz'}, use_global_device_ids=true, to_apply=%region_16.17 | all-reduce | flops 2 | bytes 16 | tf_op jit(solution)/shard_map/psum | solution.py:143
  562.9 5.3 multiply_add_fusion
  (163 shorter events, 113.6 us)
Async XLA Ops:
  0.6 32.6 %copy-start = (f32[512,512]{1,0:T(8,128)S(1)}, f32[512,512]{1,0:T(8,128)}, u32[]{:S(2)}) copy-start(f32[512,512]{1,0:T(8,128)} %param.11) | copy-start | bytes 3145732
  2.1 20.0 %collective-permute-start = (s32[1]{0:T(128)}, s32[1]{0:T(128)}, u32[]{:S(2)}, u32[]{:S(2)}) collective-permute-start(s32[1]{0:T(128)} %bitcast), channel_id=1, source_target_pairs={{0,1},{1,2},{2,3},{3,4},{4,5},{5,6},{6,7},{7,8},{8,9},{9,10},{10,1... | collective-permute-start | bytes 20 | tf_op jit(solution)/shard_map/ppermute | solution.py:18
  7.9 8.1 %copy-start.14 = (s32[2,256]{1,0:T(2,128)S(1)}, s32[2,256]{1,0:T(2,128)}, u32[]{:S(2)}) copy-start(s32[2,256]{1,0:T(2,128)} %param.10) | copy-start | bytes 6148
  7.9 8.2 %copy-start.13 = (s32[6,1024]{1,0:T(8,128)S(1)}, s32[6,1024]{1,0:T(8,128)}, u32[]{:S(2)}) copy-start(s32[6,1024]{1,0:T(8,128)} %param.9) | copy-start | bytes 73732
  10.0 16.1 %collective-permute-start.1 = (f32[2,512,256]{2,1,0:T(8,128)S(1)}, f32[2,512,256]{2,1,0:T(8,128)}, u32[]{:S(2)}, u32[]{:S(2)}) collective-permute-start(f32[2,512,256]{2,1,0:T(8,128)S(1)} %get-tuple-element.20), channel_id=1, source_target_pairs={{0,1},{1,2},{2,3},{3,4},{4,5},{5,6},{6,7},{7,8},{8,9},{9,10},{10,1... | collective-permute-start | bytes 3145736 | tf_op jit(solution)/shard_map/ppermute | solution.py:18
  12.0 16.2 %collective-permute-start.2 = (f32[2,512,256]{2,1,0:T(8,128)S(1)}, f32[2,512,256]{2,1,0:T(8,128)}, u32[]{:S(2)}, u32[]{:S(2)}) collective-permute-start(f32[2,512,256]{2,1,0:T(8,128)S(1)} %get-tuple-element.21), channel_id=1, source_target_pairs={{1,0},{2,1},{3,2},{4,3},{5,4},{6,5},{7,6},{8,7},{9,8},{10,9},{11,1... | collective-permute-start | bytes 3145736 | tf_op jit(solution)/shard_map/ppermute | solution.py:18
  33.3 36.3 %copy-start.1 = (f32[2,512,1024]{2,1,0:T(8,128)}, f32[2,512,1024]{2,1,0:T(8,128)S(1)}, u32[]{:S(2)}) copy-start(f32[2,512,1024]{2,1,0:T(8,128)S(1)} %fusion.41) | copy-start | bytes 12582916
  36.8 32.8 %copy-start.5 = (f32[1024,512]{0,1:T(8,128)}, f32[1024,512]{0,1:T(8,128)S(1)}, u32[]{:S(2)}) copy-start(f32[1024,512]{0,1:T(8,128)S(1)} %fusion.204) | copy-start | bytes 6291460
  52.6 6.0 %collective-permute-start.3 = (f32[64,256]{1,0:T(8,128)S(1)}, f32[64,256]{1,0:T(8,128)S(1)}, u32[]{:S(2)}, u32[]{:S(2)}) collective-permute-start(f32[64,256]{1,0:T(8,128)S(1)} %get-tuple-element.61), channel_id=1, source_target_pairs={{0,1},{1,2},{2,3},{3,4},{4,5},{5,6},{6,7},{7,8},{8,9},{9,10},{10,1... | collective-permute-start | bytes 196616 | tf_op jit(solution)/shard_map/ppermute | solution.py:18
  56.2 5.6 collective-permute-start.4
  151.0 112.6 %copy-start.8 = (f32[512,1024]{1,0:T(8,128)}, f32[512,1024]{1,0:T(8,128)S(1)}, u32[]{:S(2)}) copy-start(f32[512,1024]{1,0:T(8,128)S(1)} %multiply_subtract_fusion.3) | copy-start | bytes 6291460
  154.5 34.0 %copy-start.6 = (f32[1024,512]{0,1:T(8,128)}, f32[1024,512]{0,1:T(8,128)S(1)}, u32[]{:S(2)}) copy-start(f32[1024,512]{0,1:T(8,128)S(1)} %fusion.534) | copy-start | bytes 6291460
  170.2 6.9 %collective-permute-start.5 = (f32[64,256]{1,0:T(8,128)S(1)}, f32[64,256]{1,0:T(8,128)S(1)}, u32[]{:S(2)}, u32[]{:S(2)}) collective-permute-start(f32[64,256]{1,0:T(8,128)S(1)} %get-tuple-element.59), channel_id=1, source_target_pairs={{0,1},{1,2},{2,3},{3,4},{4,5},{5,6},{6,7},{7,8},{8,9},{9,10},{10,1... | collective-permute-start | bytes 196616 | tf_op jit(solution)/shard_map/ppermute | solution.py:18
  175.1 5.6 collective-permute-start.6
  186.7 2.2 copy-start.2
  355.9 6.2 %collective-permute-start.7 = (f32[64,256]{1,0:T(8,128)S(1)}, f32[64,256]{1,0:T(8,128)S(1)}, u32[]{:S(2)}, u32[]{:S(2)}) collective-permute-start(f32[64,256]{1,0:T(8,128)S(1)} %get-tuple-element.57), channel_id=1, source_target_pairs={{0,1},{1,2},{2,3},{3,4},{4,5},{5,6},{6,7},{7,8},{8,9},{9,10},{10,1... | collective-permute-start | bytes 196616 | tf_op jit(solution)/shard_map/ppermute | solution.py:18
  359.6 5.6 collective-permute-start.8
  371.2 3.3 copy-start.3
  373.2 1.3 copy-start.11
  452.1 36.6 %copy-start.9 = (f32[512,1024]{1,0:T(8,128)}, f32[512,1024]{1,0:T(8,128)S(1)}, u32[]{:S(2)}) copy-start(f32[512,1024]{1,0:T(8,128)S(1)} %multiply_subtract_fusion.1) | copy-start | bytes 6291460
  455.6 33.1 %copy-start.7 = (f32[1024,512]{0,1:T(8,128)}, f32[1024,512]{0,1:T(8,128)S(1)}, u32[]{:S(2)}) copy-start(f32[1024,512]{0,1:T(8,128)S(1)} %fusion.535) | copy-start | bytes 6291460
  471.4 6.0 %collective-permute-start.9 = (f32[64,256]{1,0:T(8,128)S(1)}, f32[64,256]{1,0:T(8,128)S(1)}, u32[]{:S(2)}, u32[]{:S(2)}) collective-permute-start(f32[64,256]{1,0:T(8,128)S(1)} %get-tuple-element.55), channel_id=1, source_target_pairs={{0,1},{1,2},{2,3},{3,4},{4,5},{5,6},{6,7},{7,8},{8,9},{9,10},{10,1... | collective-permute-start | bytes 196616 | tf_op jit(solution)/shard_map/ppermute | solution.py:18
  475.1 5.6 collective-permute-start.10
  486.7 2.2 copy-start.4
  562.9 5.4 copy-start.10
  562.9 5.4 copy-start.12
where the time goes:
time: 581 us; the launch traced here: 570 us
  blocking collectives  348 us (60%)
  matrix products  101 us (17%)
  other arithmetic  51 us (9%)
  starting transfers between devices  28.2 us (5%)
  between operations  15.5 us (3%)
  waiting for transfers between devices  15.2 us (3%)
  local copies, waits for them, and re-layouts  11.7 us (2%)
    psum x2, blocking collectives, per_device(): lax.psum((jnp.sum(image * middle), jnp.sum(image * image)), ('gx', 'gy',...  139 us
    dot_general x72, matrix products, select_dot(): jnp.dot(values, selector, precision=lax.Precision.HIGHEST, preferred_elem...  83 us
    psum x1, blocking collectives, per_device(): rho = lax.psum(jnp.sum(rhs * residual), ('gx', 'gy', 'gz'))  74.7 us
    psum x1, blocking collectives, per_device(): alpha = rho / lax.psum(jnp.sum(rhs * along), ('gx', 'gy', 'gz'))  70.1 us
    psum x1, blocking collectives, per_device(): rho_next = lax.psum(jnp.sum(rhs * residual), ('gx', 'gy', 'gz'))  64.3 us
    ppermute x11, starting transfers between devices, shifted(): lax.ppermute(value, axis, [(source, source + steps) for source in range(i...  28.2 us
    dot_general x4, matrix products, precondition(): jnp.dot(block_inverse, field, precision=lax.Precision.HIGHEST, preferred_...  17.5 us
    ppermute x11, waiting for transfers between devices, shifted(): lax.ppermute(value, axis, [(source, source + steps) for source in range(i...  15.2 us
  transfers between devices with their start and end apart: 11, of which 5 were waited for; matrix products, arithmetic and copies ran while one was open for 3% of the time, Pallas kernels for 0%

commit v1 on v0

v1 whole, which is shorter than its diff:
```python
import functools

import jax
import jax.numpy as jnp
from jax import lax
from jax.experimental import pallas as pl
from jax.experimental.pallas import tpu as pltpu
from jax.sharding import PartitionSpec as P

BE = 8
BCELLS = 512
FACE = 64
BDEV = 1024
MOVE = 256
CAP = 1536
HMAX = 256
ITERS = 2
LANES = 128
SUB = 8
CHUNKS = BDEV // LANES
AXES = ("gx", "gy", "gz")
REMOTE = 6 * BDEV
BASIS = 2 * ITERS + 1
MIB = 1024 * 1024
F32 = jnp.float32

VMEM = pl.BlockSpec(memory_space=pltpu.VMEM)
SMEM = pl.BlockSpec(memory_space=pltpu.SMEM)


def shifted(value, steps):
    count = lax.axis_size(AXES)
    initial, last = (max(0, -steps), min(count, count - steps))
    return lax.ppermute(value, AXES, [(source, source + steps) for source in range(initial, last)])


def call(kernel, outs, args, in_specs, out_specs, scratch=(), limit=24, flops=0, bytes_accessed=0):
    return pl.pallas_call(
        kernel,
        out_shape=outs,
        in_specs=in_specs,
        out_specs=out_specs,
        scratch_shapes=list(scratch),
        compiler_params=pltpu.CompilerParams(vmem_limit_bytes=limit * MIB),
        cost_estimate=pl.CostEstimate(
            flops=flops, bytes_accessed=bytes_accessed, transcendentals=0
        ),
    )(*args)


def lane_iota(rows=SUB):
    return lax.broadcasted_iota(jnp.int32, (rows, LANES), 1)


def lanes(start):
    return pl.ds(pl.multiple_of(start, LANES), LANES)


def pick(values, index):
    return jnp.take_along_axis(values, index, axis=1, mode="promise_in_bounds")


def counts_kernel(rank_ref, owner_ref, counts_ref):
    rank = rank_ref[0]
    owner = owner_ref[...]
    filled = owner >= 0
    counts_ref[0] = jnp.sum(((owner == rank - 1) & filled).astype(jnp.int32))
    counts_ref[1] = jnp.sum((owner == rank).astype(jnp.int32))
    counts_ref[2] = jnp.sum(((owner == rank + 1) & filled).astype(jnp.int32))


def cut_kernel(counts_ref, old_ref, lower_ref, upper_ref):
    start = counts_ref[0] + counts_ref[1]
    tile = start >> 7
    shift = start & (LANES - 1)
    rows = 64

    def body(step, carry):
        at = pl.ds(pl.multiple_of(step * rows, rows), rows)
        lower_ref[at, :] = old_ref[at, 0:MOVE]
        first = lane_iota(rows) < LANES - shift
        turned = []
        for part in range(3):
            source = jnp.minimum(tile + part, CAP // LANES - 1) * LANES
            turned.append(pltpu.roll(old_ref[at, lanes(source)], (LANES - shift) & (LANES - 1), 1))
        upper_ref[at, 0:LANES] = jnp.where(first, turned[0], turned[1])
        upper_ref[at, LANES:MOVE] = jnp.where(first, turned[1], turned[2])
        return carry

    lax.fori_loop(0, BCELLS // rows, body, 0)
    upper_ref[BCELLS : BCELLS + SUB, :] = jnp.full((SUB, MOVE), counts_ref[2].astype(F32))


def assemble(counts_ref, before, old_ref, lower_ref, upper_ref, out_ref, turned_ref):
    head = counts_ref[0]
    stay = counts_ref[1]
    own_start = head - before
    own_tile = own_start >> 7
    own_shift = own_start & (LANES - 1)
    up_start = -(before + stay)
    up_tile = up_start >> 7
    up_shift = up_start & (LANES - 1)
    rows = 16

    def body(step, carry):
        start = pl.multiple_of(step * rows, rows)
        at = pl.ds(start, rows)
        lane = lane_iota(rows)
        for part in range(2):
            turned_ref[part] = pltpu.roll(
                upper_ref[at, part * LANES : (part + 1) * LANES],
                (LANES - up_shift) & (LANES - 1),
                1,
            )
        last = None
        for chunk in range(CHUNKS + 1):
            source = jnp.clip(own_tile + chunk, 0, CAP // LANES - 1) * LANES
            now = pltpu.roll(
                old_ref[at, lanes(source)], (LANES - own_shift) & (LANES - 1), 1
            )
            if chunk > 0:
                place = chunk - 1
                column = lane + place * LANES
                own = jnp.where(lane < LANES - own_shift, last, now)
                low_half = turned_ref[jnp.clip(up_tile + place, 0, 1)]
                high_half = turned_ref[jnp.clip(up_tile + place + 1, 0, 1)]
                above = jnp.where(lane < LANES - up_shift, low_half, high_half)
                value = jnp.where(column < before + stay, own, above)
                if place < MOVE // LANES:
                    below = lower_ref[at, place * LANES : (place + 1) * LANES]
                    value = jnp.where(column < before, below, value)
                out_ref[pl.ds(place * BCELLS + start, rows), :] = value
            last = now
        return carry

    lax.fori_loop(0, BCELLS // rows, body, 0)


def diagonal_kernel(counts_ref, before_ref, old_ref, lower_ref, upper_ref, out_ref, turned_ref):
    assemble(counts_ref, before_ref[0], old_ref, lower_ref, upper_ref, out_ref, turned_ref)


def prepare_kernel(inverse_ref, high_ref, low_ref, theta_ref):
    inverse = inverse_ref[...]
    size = jnp.abs(inverse)
    by_row = jnp.max(jnp.sum(size, axis=1, keepdims=True), axis=0, keepdims=True)
    by_column = jnp.max(jnp.sum(size, axis=0, keepdims=True), axis=1, keepdims=True)
    bound = 14.5 * jnp.sqrt(by_row) * jnp.sqrt(by_column)
    scale = jnp.full((1, 1), 0.5, F32)
    for power in (64, 32, 16, 8, 4, 2, 1):
        large = bound >= 2.0**power
        bound = jnp.where(large, bound * 2.0**-power, bound)
        scale = jnp.where(large, scale * 2.0**-power, scale)
    for power in (64, 32, 16, 8, 4, 2, 1):
        small = bound < 2.0**-power
        bound = jnp.where(small, bound * 2.0**power, bound)
        scale = jnp.where(small, scale * 2.0**power, scale)
    scaled = inverse * scale
    high = scaled.astype(jnp.bfloat16)
    high_ref[...] = high
    low_ref[...] = (scaled - high.astype(F32)).astype(jnp.bfloat16)
    row = lax.broadcasted_iota(jnp.int32, (BCELLS, BCELLS), 0)
    column = lax.broadcasted_iota(jnp.int32, (BCELLS, BCELLS), 1)
    theta_ref[0] = jnp.sum(jnp.where(row == column, scaled, 0.0)) * (6.5 / BCELLS)


def precondition(high_ref, low_ref, field_ref, out_ref):
    def body(step, carry):
        base = pl.multiple_of(step * (2 * BCELLS), 2 * BCELLS)
        halves = [pl.ds(base + half * BCELLS, BCELLS) for half in range(2)]
        field = jnp.concatenate([field_ref[half, :] for half in halves], axis=1)
        top = field.astype(jnp.bfloat16)
        rest = (field - top.astype(F32)).astype(jnp.bfloat16)
        high = high_ref[...]
        small = jnp.dot(high, rest, preferred_element_type=F32)
        small = small + jnp.dot(low_ref[...], top, preferred_element_type=F32)
        found = small + jnp.dot(high, top, preferred_element_type=F32)
        out_ref[halves[0], :] = found[:, :LANES]
        out_ref[halves[1], :] = found[:, LANES:]
        return carry

    lax.fori_loop(0, CHUNKS // 2, body, 0)


def split_ends(field_ref, first_ref, last_ref):
    first_ref[...] = field_ref[pl.ds(0, CHUNKS * FACE, stride=BE), :]
    last_ref[...] = field_ref[pl.ds(BE - 1, CHUNKS * FACE, stride=BE), :]


def layer_tile(field_ref, ends, which, part, chunk):
    if which >= 4:
        row = chunk * FACE + part * SUB
        return ends[which - 4][row : row + SUB, :]
    row = (part * BE, (BE - 1) * FACE + part * BE, part * FACE, part * FACE + (BE - 1) * BE)[which]
    row = row + chunk * BCELLS
    return field_ref[row : row + SUB, :]


def pack(field_ref, ends, send_ref, to_lower_ref, to_upper_ref):
    for row, out_ref in ((0, to_lower_ref), (1, to_upper_ref)):

        def body(step, carry, row=row, out_ref=out_ref):
            code = jnp.broadcast_to(send_ref[row : row + 1, lanes(step * LANES)], (SUB, LANES))
            lane = code & (LANES - 1)
            tile = code >> 7
            found = [jnp.zeros((SUB, LANES), F32) for _ in range(8)]
            for which in range(6):
                for source in range(CHUNKS):
                    here = tile == which * CHUNKS + source
                    for part in range(8):
                        values = layer_tile(field_ref, ends, which, part, source)
                        found[part] = jnp.where(here, pick(values, lane), found[part])
            base = pl.multiple_of(step * FACE, FACE)
            for part in range(8):
                out_ref[pl.ds(base + part * SUB, SUB), :] = found[part]
            return carry

        lax.fori_loop(0, HMAX // LANES, body, 0)


def put_layers(which, found, faces_ref, ends_ref):
    for part in range(8):
        if which < 4:
            base = which * FACE + part * SUB
            faces_ref[base : base + SUB, :] = found[part]
        else:
            ends_ref[pl.ds(part * FACE + (which - 4) * (BE - 1), SUB, stride=BE), :] = found[part]


def local_kernel(codes_ref, field_ref, out_ref, first_ref, last_ref, faces_ref, ends_ref):
    split_ends(field_ref, first_ref, last_ref)
    ends = (first_ref, last_ref)
    cell = lax.broadcasted_iota(jnp.int32, (SUB, LANES), 0)

    def body(step, carry):
        at = lanes(step * LANES)
        start = pl.multiple_of(step * BCELLS, BCELLS)
        for which in range(6):
            partner = which ^ 1
            code = jnp.broadcast_to(codes_ref[which : which + 1, at], (SUB, LANES))
            code = code - partner * BDEV
            lane = code & (LANES - 1)
            tile = code >> 7
            found = [jnp.zeros((SUB, LANES), F32) for _ in range(8)]
            for source in range(CHUNKS):
                here = tile == source
                for part in range(8):
                    values = layer_tile(field_ref, ends, partner, part, source)
                    found[part] = jnp.where(here, pick(values, lane), found[part])
            put_layers(which, found, faces_ref, ends_ref)

        def block(i, j):
            row = (i * BE + j) * BE
            return field_ref[pl.ds(start + row, SUB), :]

        def layer(which, part):
            base = which * FACE + part * SUB
            return faces_ref[base : base + SUB, :]

        for i in range(BE):
            for j in range(BE):
                row = (i * BE + j) * BE
                here = block(i, j)
                edge = ends_ref[row : row + SUB, :]
                beside = block(i - 1, j) if i > 0 else layer(0, j)
                beside = beside + (block(i + 1, j) if i < BE - 1 else layer(1, j))
                beside = beside + (block(i, j - 1) if j > 0 else layer(2, i))
                beside = beside + (block(i, j + 1) if j < BE - 1 else layer(3, i))
                beside = beside + jnp.where(cell == 0, edge, pltpu.roll(here, 1, 0))
                beside = beside + jnp.where(cell == BE - 1, edge, pltpu.roll(here, BE - 1, 0))
                out_ref[pl.ds(start + row, SUB), :] = 6.0 * here - beside
        return carry

    lax.fori_loop(0, CHUNKS, body, 0)


def finish(
    theta, codes_ref, below_ref, above_ref, diagonal_ref, field_ref, partial_ref, basis, out_ref,
    faces_ref, ends_ref, sums_ref
):
    cell = lax.broadcasted_iota(jnp.int32, (SUB, LANES), 0)
    is_end = (cell == 0) | (cell == BE - 1)
    sums_ref[...] = jnp.zeros_like(sums_ref)

    def body(step, carry):
        at = lanes(step * LANES)
        start = pl.multiple_of(step * BCELLS, BCELLS)
        for which in range(6):
            code = jnp.broadcast_to(codes_ref[which : which + 1, at], (SUB, LANES)) - REMOTE
            lane = code & (LANES - 1)
            tile = code >> 7
            found = [jnp.zeros((SUB, LANES), F32) for _ in range(8)]
            for source in range(2 * HMAX // LANES):
                here = tile == source
                from_ref = below_ref if source < HMAX // LANES else above_ref
                base = source % (HMAX // LANES) * FACE
                for part in range(8):
                    values = from_ref[base + part * SUB : base + (part + 1) * SUB, :]
                    found[part] = jnp.where(here, pick(values, lane), found[part])
            put_layers(which, found, faces_ref, ends_ref)

        def layer(which, part):
            base = which * FACE + part * SUB
            return faces_ref[base : base + SUB, :]

        sums = [jnp.zeros((SUB, LANES), F32) for _ in range(len(basis) + 1)]
        for i in range(BE):
            for j in range(BE):
                row = (i * BE + j) * BE
                rows = pl.ds(start + row, SUB)
                beside = jnp.where(is_end, ends_ref[row : row + SUB, :], 0.0)
                if i == 0:
                    beside = beside + layer(0, j)
                if i == BE - 1:
                    beside = beside + layer(1, j)
                if j == 0:
                    beside = beside + layer(2, i)
                if j == BE - 1:
                    beside = beside + layer(3, i)
                value = partial_ref[rows, :] + diagonal_ref[rows, :] * field_ref[rows, :]
                value = value - beside - theta * basis[-1][rows, :]
                out_ref[rows, :] = value
                for k, ref in enumerate(basis):
                    sums[k] = sums[k] + value * ref[rows, :]
                sums[-1] = sums[-1] + value * value
        for k, part in enumerate(sums):
            sums_ref[k] += part
        return carry

    lax.fori_loop(0, CHUNKS, body, 0)


def place_sums(sums_ref, count, gram_in, gram_out_ref, first):
    lane = lax.broadcasted_iota(jnp.int32, (SUB, LANES), 1)
    row = gram_in
    for k in range(count):
        row = row + jnp.where(lane == first + k, jnp.sum(sums_ref[k]), 0.0)
    gram_out_ref[...] = row


def first_kernel(
    counts_ref, before_ref, old_ref, lower_ref, upper_ref, high_ref, low_ref, send_ref,
    rhs_ref, field_ref, to_lower_ref, to_upper_ref, gram_ref,
    turned_ref, first_ref, last_ref, sums_ref,
):
    assemble(counts_ref, before_ref[0], old_ref, lower_ref, upper_ref, rhs_ref, turned_ref)
    precondition(high_ref, low_ref, rhs_ref, field_ref)
    split_ends(field_ref, first_ref, last_ref)
    pack(field_ref, (first_ref, last_ref), send_ref, to_lower_ref, to_upper_ref)
    sums_ref[...] = jnp.zeros_like(sums_ref)

    def body(step, carry):
        total = jnp.zeros((SUB, LANES), F32)
        start = pl.multiple_of(step * BCELLS, BCELLS)
        for row in range(0, BCELLS, SUB):
            value = rhs_ref[pl.ds(start + row, SUB), :]
            total = total + value * value
        sums_ref[0] += total
        return carry

    lax.fori_loop(0, CHUNKS, body, 0)
    place_sums(sums_ref, 1, jnp.zeros((SUB, LANES), F32), gram_ref, 0)


def next_kernel(known, more, *refs):
    theta_ref, codes_ref, below_ref, above_ref, diagonal_ref, field_ref, partial_ref = refs[:7]
    basis = refs[7 : 7 + known]
    gram_in_ref = refs[7 + known]
    at = 8 + known
    if more:
        high_ref, low_ref, send_ref = refs[at : at + 3]
        at += 3
        out_ref, gram_ref, next_ref, to_lower_ref, to_upper_ref = refs[at : at + 5]
        at += 5
    else:
        out_ref, gram_ref = refs[at : at + 2]
        at += 2
    faces_ref, ends_ref, sums_ref, first_ref, last_ref = refs[at:]
    finish(
        theta_ref[0], codes_ref, below_ref, above_ref, diagonal_ref, field_ref, partial_ref,
        basis, out_ref, faces_ref, ends_ref, sums_ref,
    )
    if more:
        precondition(high_ref, low_ref, out_ref, next_ref)
        split_ends(next_ref, first_ref, last_ref)
        pack(next_ref, (first_ref, last_ref), send_ref, to_lower_ref, to_upper_ref)
    place_sums(sums_ref, known + 1, gram_in_ref[...], gram_ref, known * (known + 1) // 2)


def recurrence(gram, theta):
    def dot(left, right):
        total = None
        for a, x in enumerate(left):
            if x is None:
                continue
            part = None
            for b, y in enumerate(right):
                if y is not None:
                    term = gram[max(a, b)][min(a, b)] * y
                    part = term if part is None else part + term
            total = x * part if total is None else total + x * part
        return total

    def add(left, right):
        return [
            y if x is None else x if y is None else x + y for x, y in zip(left, right)
        ]

    def times(factor, vector):
        return [None if x is None else factor * x for x in vector]

    def apply(vector):
        return add([None] + vector[:-1], times(theta, vector))

    one = jnp.ones_like(theta)
    shadow = [one] + [None] * (BASIS - 1)
    residual = shadow
    direction = residual
    rho = gram[0][0]
    rho_next = rho
    total = [None] * BASIS
    along = alpha = omega = None
    for step in range(ITERS):
        if step > 0:
            beta = (rho_next / rho) * (alpha / omega)
            rho = rho_next
            direction = add(residual, times(beta, add(direction, times(-omega, along))))
        along = apply(direction)
        alpha = rho / dot(shadow, along)
        middle = add(residual, times(-alpha, along))
        image = apply(middle)
        omega = dot(image, middle) / dot(image, image)
        total = add(total, add(times(alpha, direction), times(omega, middle)))
        residual = add(middle, times(-omega, image))
        rho_next = dot(shadow, residual)
    return total, residual


def last_kernel(theta_ref, gathered_ref, *refs):
    basis = refs[:BASIS]
    fields = refs[BASIS : 2 * BASIS - 1]
    solution_ref, residual_ref = refs[2 * BASIS - 1 :]
    row = jnp.sum(gathered_ref[...], axis=0, keepdims=True)
    lane = lax.broadcasted_iota(jnp.int32, (1, LANES), 1)

    def entry(k):
        return jnp.sum(jnp.where(lane == k, row, 0.0), axis=1, keepdims=True)

    gram = [[entry(a * (a + 1) // 2 + b) for b in range(a + 1)] for a in range(BASIS)]
    theta = jnp.full((1, 1), theta_ref[0])
    total, residual = recurrence(gram, theta)
    total = [None if x is None else jnp.broadcast_to(x, (SUB, LANES)) for x in total]
    residual = [jnp.broadcast_to(x, (SUB, LANES)) for x in residual]

    def body(step, carry):
        start = pl.multiple_of(step * SUB, SUB)
        for chunk in range(CHUNKS):
            rows = pl.ds(chunk * BCELLS + start, SUB)
            at = slice(chunk * LANES, (chunk + 1) * LANES)
            value = total[0] * fields[0][rows, :]
            for k in range(1, BASIS - 1):
                value = value + total[k] * fields[k][rows, :]
            solution_ref[pl.ds(start, SUB), at] = value
            value = residual[0] * basis[0][rows, :]
            for k in range(1, BASIS):
                value = value + residual[k] * basis[k][rows, :]
            residual_ref[pl.ds(start, SUB), at] = value
        return carry

    lax.fori_loop(0, BCELLS // SUB, body, 0)


def per_device(rhs_old, diagonal_old, new_owner, face_source, send_layers, block_inverse):
    field_type = jax.ShapeDtypeStruct((CHUNKS * BCELLS, LANES), F32)
    out_type = jax.ShapeDtypeStruct((BCELLS, BDEV), F32)
    halo_type = jax.ShapeDtypeStruct((HMAX // LANES * FACE, LANES), F32)
    gram_type = jax.ShapeDtypeStruct((SUB, LANES), F32)
    half_type = jax.ShapeDtypeStruct((BCELLS, BCELLS), jnp.bfloat16)
    lower_type = jax.ShapeDtypeStruct((BCELLS, MOVE), F32)
    upper_type = jax.ShapeDtypeStruct((BCELLS + SUB, MOVE), F32)
    turned = pltpu.VMEM((2, 16, LANES), F32)
    end_layers = [pltpu.VMEM((CHUNKS * FACE, LANES), F32)] * 2
    layers = [pltpu.VMEM((4 * FACE, LANES), F32), pltpu.VMEM((BCELLS, LANES), F32)]
    sums = pltpu.VMEM((BASIS, SUB, LANES), F32)

    rank = lax.axis_index(AXES).astype(jnp.int32).reshape(1)
    counts = call(
        counts_kernel,
        jax.ShapeDtypeStruct((3,), jnp.int32),
        (rank, new_owner.reshape(CAP // LANES, LANES)),
        [SMEM, VMEM],
        SMEM,
    )

    def cut(old):
        return call(
            cut_kernel, (lower_type, upper_type), (counts, old), [SMEM, VMEM], (VMEM, VMEM)
        )

    lower, upper = cut(rhs_old)
    rhs_above = shifted(lower, -1)
    rhs_below = shifted(upper, 1)
    lower, upper = cut(diagonal_old)
    diagonal_above = shifted(lower, -1)
    diagonal_below = shifted(upper, 1)
    high, low, theta = call(
        prepare_kernel,
        (half_type, half_type, jax.ShapeDtypeStruct((1,), F32)),
        (block_inverse,),
        [VMEM],
        (VMEM, VMEM, SMEM),
    )
    before = rhs_below[BCELLS, 0:1].astype(jnp.int32)
    rhs, field, to_lower, to_upper, gram = call(
        first_kernel,
        (field_type, field_type, halo_type, halo_type, gram_type),
        (counts, before, rhs_old, rhs_below, rhs_above, high, low, send_layers),
        [SMEM, SMEM] + [VMEM] * 6,
        (VMEM,) * 5,
        [turned] + end_layers + [sums],
        flops=10**9,
        bytes_accessed=8 * MIB,
    )
    diagonal = call(
        diagonal_kernel,
        field_type,
        (counts, before, diagonal_old, diagonal_below, diagonal_above),
        [SMEM, SMEM] + [VMEM] * 3,
        VMEM,
        [turned],
        bytes_accessed=6 * MIB,
    )
    basis = [rhs]
    fields = [field]
    for known in range(1, BASIS):
        above = shifted(to_lower, -1)
        below = shifted(to_upper, 1)
        partial = call(
            local_kernel,
            field_type,
            (face_source, field),
            [VMEM] * 2,
            VMEM,
            end_layers + layers,
            flops=10**9,
            bytes_accessed=4 * MIB,
        )
        more = known < BASIS - 1
        args = [theta, face_source, below, above, diagonal, field, partial] + basis + [gram]
        outs = [field_type, gram_type]
        if more:
            args += [high, low, send_layers]
            outs += [field_type, halo_type, halo_type]
        found = call(
            functools.partial(next_kernel, known, more),
            tuple(outs),
            tuple(args),
            [SMEM] + [VMEM] * (len(args) - 1),
            (VMEM,) * len(outs),
            layers + [sums] + end_layers,
            limit=32,
            flops=10**9,
            bytes_accessed=12 * MIB,
        )
        if more:
            value, gram, field, to_lower, to_upper = found
            fields.append(field)
        else:
            value, gram = found
        basis.append(value)
    gathered = lax.all_gather(gram[0:1], AXES, axis=0, tiled=True)
    return call(
        last_kernel,
        (out_type, out_type),
        (theta, gathered, *basis, *fields),
        [SMEM] + [VMEM] * (2 * BASIS),
        (VMEM, VMEM),
        limit=32,
    )


def solution(mesh):
    return jax.shard_map(
        per_device,
        mesh=mesh,
        in_specs=(
            P(None, AXES),
            P(None, AXES),
            P(AXES),
            P(None, AXES),
            P(None, AXES),
            P(),
        ),
        out_specs=(P(None, AXES), P(None, AXES)),
        check_vma=False,
    )
```

time: 581 us -> 165 us (0.28); the launches traced: 570 us -> 165 us
  blocking collectives: 348 us -> 55.3 us
  matrix products: 101 us -> 0 us
  Pallas kernels: 0 us -> 70.1 us
  other arithmetic: 51 us -> 0 us
  waiting for transfers between devices: 15.2 us -> 0.03 us
  between operations: 15.5 us -> 1.68 us
  local copies, waits for them, and re-layouts: 11.7 us -> 3.12 us
  starting transfers between devices: 28.2 us -> 34.6 us
    psum x5 -> x0, blocking collectives: 348 us -> none  [the longest x2 139 us: per_device(): lax.psum((jnp.sum(image * middle), jnp.sum(image * image)), ('gx', 'gy',...]
    dot_general x76 -> x0, matrix products: 101 us -> none  [the longest x72 83 us: select_dot(): jnp.dot(values, selector, precision=lax.Precision.HIGHEST, preferred_elem...]
    pallas_call x0 -> x15, Pallas kernels: none -> 70.1 us  [call(): pl.pallas_call(kernel, out_shape=outs, in_specs=in_specs, out_specs=out_s...]
    all_gather x0 -> x1, blocking collectives: none -> 55.3 us  [per_device(): gathered = lax.all_gather(gram[0:1], AXES, axis=0, tiled=True)]
    ppermute x11 -> x12, waiting for transfers between devices: 15.2 us -> 0.03 us  [shifted(): lax.ppermute(value, AXES, [(source, source + steps) for source in range(i...]
    reduce_sum x6 -> x0, other arithmetic: 15.1 us -> none  [the longest x2 5.78 us: per_device(): jnp.sum(image * image)]
    add x11 -> x0, other arithmetic: 13 us -> none  [the longest x4 7.61 us: apply_operator(): beside + jnp.concatenate([volume[:, :, 1:], outside[5].reshape(BE, BE, 1,...]
    sub x3 -> x0, other arithmetic: 9.18 us -> none  [the longest x2 7.39 us: per_device(): middle = residual - alpha * along]
  transfers between devices with their start and end apart: 11 -> 12, of which waited for: 5 -> 0; matrix products, arithmetic and copies ran while one was open for 3% -> 0% of each run, Pallas kernels for 0% -> 21%
where the time goes in v1:
time: 165 us
  Pallas kernels  70.1 us (42%)
  blocking collectives  55.3 us (34%)
  starting transfers between devices  34.6 us (21%)
  local copies, waits for them, and re-layouts  3.12 us (2%)
  between operations  1.68 us (1%)
    pallas_call x15, Pallas kernels, call(): pl.pallas_call(kernel, out_shape=outs, in_specs=in_specs, out_specs=out_s...  70.1 us
    all_gather x1, blocking collectives, per_device(): gathered = lax.all_gather(gram[0:1], AXES, axis=0, tiled=True)  55.3 us
    ppermute x12, starting transfers between devices, shifted(): lax.ppermute(value, AXES, [(source, source + steps) for source in range(i...  34.6 us
  transfers between devices with their start and end apart: 12, of which 0 were waited for; matrix products, arithmetic and copies ran while one was open for 0% of the time, Pallas kernels for 21%

profile of v1, /device:TPU:1, one launch (start us, length us, event | category | flops | bytes accessed | tf_op | source)
XLA Modules:
  0.0 164.9 jit_solution(17408205191785443119)
XLA Ops:
  0.6 0.7 copy-done.6
  1.3 0.7 shard_map.78.counts_ref
  2.1 1.9 %copy-done = f32[512,1536]{1,0:T(8,128)S(1)} copy-done((f32[512,1536]{1,0:T(8,128)S(1)}, f32[512,1536]{1,0:T(8,128)}, u32[]{:S(2)}) %copy-start) | copy-done | bytes 3145752
  4.0 1.3 shard_map.79
  5.3 0.0 copy-start.4
  5.3 4.6 %collective-permute-start = (f32[520,256]{1,0:T(8,128)S(1)}, f32[520,256]{1,0:T(8,128)S(1)}, u32[]{:S(2)}, u32[]{:S(2)}) collective-permute-start(f32[520,256]{1,0:T(8,128)S(1)} %get-tuple-element.32), channel_id=1, source_target_pairs={{0,1},{1,2},{2,3},{3,4},{4,5},{5,6},{6,7},{7,8},{8,9},{9,10},{10,1... | collective-permute-start | bytes 1597448 | tf_op jit(solution)/shard_map/ppermute | solution.py:34
  10.0 2.2 %collective-permute-start.1 = (f32[512,256]{1,0:T(8,128)S(1)}, f32[512,256]{1,0:T(8,128)S(1)}, u32[]{:S(2)}, u32[]{:S(2)}) collective-permute-start(f32[512,256]{1,0:T(8,128)S(1)} %get-tuple-element.33), channel_id=1, source_target_pairs={{1,0},{2,1},{3,2},{4,3},{5,4},{6,5},{7,6},{8,7},{9,8},{10,9},{11,1... | collective-permute-start | bytes 1572872 | tf_op jit(solution)/shard_map/ppermute | solution.py:34
  12.2 1.3 shard_map.81
  13.5 3.6 %collective-permute-start.4 = (f32[520,256]{1,0:T(8,128)S(1)}, f32[520,256]{1,0:T(8,128)S(1)}, u32[]{:S(2)}, u32[]{:S(2)}) collective-permute-start(f32[520,256]{1,0:T(8,128)S(1)} %get-tuple-element.38), channel_id=1, source_target_pairs={{0,1},{1,2},{2,3},{3,4},{4,5},{5,6},{6,7},{7,8},{8,9},{9,10},{10,1... | collective-permute-start | bytes 1597448 | tf_op jit(solution)/shard_map/ppermute | solution.py:34
  17.2 1.9 %collective-permute-start.5 = (f32[512,256]{1,0:T(8,128)S(1)}, f32[512,256]{1,0:T(8,128)S(1)}, u32[]{:S(2)}, u32[]{:S(2)}) collective-permute-start(f32[512,256]{1,0:T(8,128)S(1)} %get-tuple-element.39), channel_id=1, source_target_pairs={{1,0},{2,1},{3,2},{4,3},{5,4},{6,5},{7,6},{8,7},{9,8},{10,9},{11,1... | collective-permute-start | bytes 1572872 | tf_op jit(solution)/shard_map/ppermute | solution.py:34
  19.1 1.1 shard_map.77
  20.3 0.5 slice.8
  21.5 8.7 %shard_map.80 = (f32[4096,128]{1,0:T(8,128)S(1)}, f32[4096,128]{1,0:T(8,128)S(1)}, f32[128,128]{1,0:T(8,128)S(1)}, f32[128,128]{1,0:T(8,128)S(1)}, f32[8,128]{1,0:T(8,128)S(1)}) custom-call(s32[3]{0:T(128)S(1)} %shard_map.78.counts_ref, s32[1]{0:T(128)} %bitcast.2.before_ref, f32[512,1536]{1,0:T(8,128)S(1)} %copy-done.1, ...), custom_call_target="tpu_custom_call" | custom-call | flops 1000000000 | bytes 8388608 | tf_op jit(solution)/shard_map/pallas_call | solution.py:38
  30.2 3.6 %collective-permute-start.2 = (f32[128,128]{1,0:T(8,128)S(1)}, f32[128,128]{1,0:T(8,128)S(1)}, u32[]{:S(2)}, u32[]{:S(2)}) collective-permute-start(f32[128,128]{1,0:T(8,128)S(1)} %get-tuple-element.36), channel_id=1, source_target_pairs={{0,1},{1,2},{2,3},{3,4},{4,5},{5,6},{6,7},{7,8},{8,9},{9,10},{10,1... | collective-permute-start | bytes 196616 | tf_op jit(solution)/shard_map/ppermute | solution.py:34
  33.9 1.9 %collective-permute-start.3 = (f32[128,128]{1,0:T(8,128)S(1)}, f32[128,128]{1,0:T(8,128)S(1)}, u32[]{:S(2)}, u32[]{:S(2)}) collective-permute-start(f32[128,128]{1,0:T(8,128)S(1)} %get-tuple-element.37), channel_id=1, source_target_pairs={{1,0},{2,1},{3,2},{4,3},{5,4},{6,5},{7,6},{8,7},{9,8},{10,9},{11,1... | collective-permute-start | bytes 196616 | tf_op jit(solution)/shard_map/ppermute | solution.py:34
  35.8 3.8 %shard_map.82.refs_4_ = f32[4096,128]{1,0:T(8,128)S(1)} custom-call(s32[3]{0:T(128)S(1)} %shard_map.78.counts_ref, s32[1]{0:T(128)} %bitcast.2.before_ref, f32[512,1536]{1,0:T(8,128)S(1)} %copy-done.2, f32[520,256]{1,0:T(8,128)S(1)} %collective-permute-done.4.lower_ref, f32[512,256]{1,0:T(8,128)S(1)} %collective-permute-done.5.upper_ref), custom_call_target="tpu_custom_call" | custom-call | bytes 6291456 | tf_op jit(solution)/shard_map/pallas_call | solution.py:38
  39.6 4.7 %shard_map.83.refs_6_ = f32[4096,128]{1,0:T(8,128)S(1)} custom-call(s32[6,1024]{1,0:T(8,128)S(1)} %copy-done.3, f32[4096,128]{1,0:T(8,128)S(1)} %get-tuple-element.40.field_ref.refs_5_), custom_call_target="tpu_custom_call" | custom-call | flops 1000000000 | bytes 4194304 | tf_op jit(solution)/shard_map/pallas_call | solution.py:38
  44.4 8.0 %shard_map.84 = (f32[4096,128]{1,0:T(8,128)S(1)}, f32[8,128]{1,0:T(8,128)S(1)}, f32[4096,128]{1,0:T(8,128)S(1)}, f32[128,128]{1,0:T(8,128)S(1)}, f32[128,128]{1,0:T(8,128)S(1)}) custom-call(f32[1]{0:T(128)} %get-tuple-element.31.refs_0_.theta_ref, s32[6,1024]{1,0:T(8,128)S(1)} %copy-done.3, f32[128,128]{1,0:T(8,128)S(1)} %collective-permute-done.2.refs_2_, ...), custom_call_target="tpu_custom_call" | custom-call | flops 1000000000 | bytes 12582912 | tf_op jit(solution)/shard_map/pallas_call | solution.py:38
  52.3 3.6 %collective-permute-start.6 = (f32[128,128]{1,0:T(8,128)S(1)}, f32[128,128]{1,0:T(8,128)S(1)}, u32[]{:S(2)}, u32[]{:S(2)}) collective-permute-start(f32[128,128]{1,0:T(8,128)S(1)} %get-tuple-element.43), channel_id=1, source_target_pairs={{0,1},{1,2},{2,3},{3,4},{4,5},{5,6},{6,7},{7,8},{8,9},{9,10},{10,1... | collective-permute-start | bytes 196616 | tf_op jit(solution)/shard_map/ppermute | solution.py:34
  56.0 1.9 %collective-permute-start.7 = (f32[128,128]{1,0:T(8,128)S(1)}, f32[128,128]{1,0:T(8,128)S(1)}, u32[]{:S(2)}, u32[]{:S(2)}) collective-permute-start(f32[128,128]{1,0:T(8,128)S(1)} %get-tuple-element.44), channel_id=1, source_target_pairs={{1,0},{2,1},{3,2},{4,3},{5,4},{6,5},{7,6},{8,7},{9,8},{10,9},{11,1... | collective-permute-start | bytes 196616 | tf_op jit(solution)/shard_map/ppermute | solution.py:34
  57.9 4.7 %shard_map.85.refs_6_ = f32[4096,128]{1,0:T(8,128)S(1)} custom-call(s32[6,1024]{1,0:T(8,128)S(1)} %copy-done.3, f32[4096,128]{1,0:T(8,128)S(1)} %get-tuple-element.45.field_ref.refs_5_.refs_6_), custom_call_target="tpu_custom_call" | custom-call | flops 1000000000 | bytes 4194304 | tf_op jit(solution)/shard_map/pallas_call | solution.py:38
  62.7 8.1 %shard_map.86 = (f32[4096,128]{1,0:T(8,128)S(1)}, f32[8,128]{1,0:T(8,128)S(1)}, f32[4096,128]{1,0:T(8,128)S(1)}, f32[128,128]{1,0:T(8,128)S(1)}, f32[128,128]{1,0:T(8,128)S(1)}) custom-call(f32[1]{0:T(128)} %get-tuple-element.31.refs_0_.theta_ref, s32[6,1024]{1,0:T(8,128)S(1)} %copy-done.3, f32[128,128]{1,0:T(8,128)S(1)} %collective-permute-done.6.refs_2_, ...), custom_call_target="tpu_custom_call" | custom-call | flops 1000000000 | bytes 12582912 | tf_op jit(solution)/shard_map/pallas_call | solution.py:38
  70.8 3.6 %collective-permute-start.8 = (f32[128,128]{1,0:T(8,128)S(1)}, f32[128,128]{1,0:T(8,128)S(1)}, u32[]{:S(2)}, u32[]{:S(2)}) collective-permute-start(f32[128,128]{1,0:T(8,128)S(1)} %get-tuple-element.48), channel_id=1, source_target_pairs={{0,1},{1,2},{2,3},{3,4},{4,5},{5,6},{6,7},{7,8},{8,9},{9,10},{10,1... | collective-permute-start | bytes 196616 | tf_op jit(solution)/shard_map/ppermute | solution.py:34
  74.4 1.9 %collective-permute-start.9 = (f32[128,128]{1,0:T(8,128)S(1)}, f32[128,128]{1,0:T(8,128)S(1)}, u32[]{:S(2)}, u32[]{:S(2)}) collective-permute-start(f32[128,128]{1,0:T(8,128)S(1)} %get-tuple-element.49), channel_id=1, source_target_pairs={{1,0},{2,1},{3,2},{4,3},{5,4},{6,5},{7,6},{8,7},{9,8},{10,9},{11,1... | collective-permute-start | bytes 196616 | tf_op jit(solution)/shard_map/ppermute | solution.py:34
  76.4 4.8 %shard_map.87.refs_6_ = f32[4096,128]{1,0:T(8,128)S(1)} custom-call(s32[6,1024]{1,0:T(8,128)S(1)} %copy-done.3, f32[4096,128]{1,0:T(8,128)S(1)} %get-tuple-element.50.field_ref.refs_5_.refs_7_), custom_call_target="tpu_custom_call" | custom-call | flops 1000000000 | bytes 4194304 | tf_op jit(solution)/shard_map/pallas_call | solution.py:38
  81.2 8.2 %shard_map.88 = (f32[4096,128]{1,0:T(8,128)S(1)}, f32[8,128]{1,0:T(8,128)S(1)}, f32[4096,128]{1,0:T(8,128)S(1)}, f32[128,128]{1,0:T(8,128)S(1)}, f32[128,128]{1,0:T(8,128)S(1)}) custom-call(f32[1]{0:T(128)} %get-tuple-element.31.refs_0_.theta_ref, s32[6,1024]{1,0:T(8,128)S(1)} %copy-done.3, f32[128,128]{1,0:T(8,128)S(1)} %collective-permute-done.8.refs_2_, ...), custom_call_target="tpu_custom_call" | custom-call | flops 1000000000 | bytes 12582912 | tf_op jit(solution)/shard_map/pallas_call | solution.py:38
  89.4 3.6 %collective-permute-start.10 = (f32[128,128]{1,0:T(8,128)S(1)}, f32[128,128]{1,0:T(8,128)S(1)}, u32[]{:S(2)}, u32[]{:S(2)}) collective-permute-start(f32[128,128]{1,0:T(8,128)S(1)} %get-tuple-element.53), channel_id=1, source_target_pairs={{0,1},{1,2},{2,3},{3,4},{4,5},{5,6},{6,7},{7,8},{8,9},{9,10},{10,1... | collective-permute-start | bytes 196616 | tf_op jit(solution)/shard_map/ppermute | solution.py:34
  93.1 1.9 %collective-permute-start.11 = (f32[128,128]{1,0:T(8,128)S(1)}, f32[128,128]{1,0:T(8,128)S(1)}, u32[]{:S(2)}, u32[]{:S(2)}) collective-permute-start(f32[128,128]{1,0:T(8,128)S(1)} %get-tuple-element.54), channel_id=1, source_target_pairs={{1,0},{2,1},{3,2},{4,3},{5,4},{6,5},{7,6},{8,7},{9,8},{10,9},{11,1... | collective-permute-start | bytes 196616 | tf_op jit(solution)/shard_map/ppermute | solution.py:34
  95.0 4.8 %shard_map.89.refs_6_ = f32[4096,128]{1,0:T(8,128)S(1)} custom-call(s32[6,1024]{1,0:T(8,128)S(1)} %copy-done.3, f32[4096,128]{1,0:T(8,128)S(1)} %get-tuple-element.55.field_ref.refs_5_.refs_8_), custom_call_target="tpu_custom_call" | custom-call | flops 1000000000 | bytes 4194304 | tf_op jit(solution)/shard_map/pallas_call | solution.py:38
  99.9 4.2 %shard_map.90 = (f32[4096,128]{1,0:T(8,128)S(1)}, f32[8,128]{1,0:T(8,128)S(1)}) custom-call(f32[1]{0:T(128)} %get-tuple-element.31.refs_0_.theta_ref, s32[6,1024]{1,0:T(8,128)S(1)} %copy-done.3, f32[128,128]{1,0:T(8,128)S(1)} %collective-permute-done.10.refs_2_, f32[128,128]{1,0:T(8,128)S(1)} %collective-permute-done.11.refs_3_, ...), custom_call_target="tpu_custom_call" | custom-call | flops 1000000000 | bytes 12582912 | tf_op jit(solution)/shard_map/pallas_call | solution.py:38
  104.1 55.3 %all-gather = f32[128,1,128]{2,1,0:T(1,128)S(1)} all-gather(f32[1,1,128]{2,1,0:T(1,128)S(1)} %slice_bitcast_fusion), channel_id=1, replica_groups=mesh['gx'=4,'gy'=4,'gz'=8] {'gx','gy','gz'}, dimensions={0}, use_global_device_ids=true | all-gather | bytes 66048 | tf_op jit(solution)/shard_map/all_gather | solution.py:571
  159.4 5.5 %shard_map.91 = (f32[512,1024]{1,0:T(8,128)}, f32[512,1024]{1,0:T(8,128)}) custom-call(f32[1]{0:T(128)} %get-tuple-element.31.refs_0_.theta_ref, f32[128,128]{1,0:T(8,128)S(1)} %bitcast.6, f32[4096,128]{1,0:T(8,128)S(1)} %get-tuple-element.41.refs_7_.refs_0_, f32[4096,128]{1,0:T(8,128)S(1)} %get-tuple-element.46.refs_8_.refs_1_, ...), custom_call_target="tpu_custom_call" | custom-call | tf_op jit(solution)/shard_map/pallas_call | solution.py:38
  (24 shorter events, 0.1 us)
Async XLA Ops:
  0.6 0.7 copy-start.6
  2.1 1.9 %copy-start = (f32[512,1536]{1,0:T(8,128)S(1)}, f32[512,1536]{1,0:T(8,128)}, u32[]{:S(2)}) copy-start(f32[512,1536]{1,0:T(8,128)} %old_ref.5) | copy-start | bytes 9437188
  4.0 8.2 %copy-start.2 = (f32[512,1536]{1,0:T(8,128)S(1)}, f32[512,1536]{1,0:T(8,128)}, u32[]{:S(2)}) copy-start(f32[512,1536]{1,0:T(8,128)} %old_ref.7) | copy-start | bytes 9437188
  5.3 13.8 %copy-start.4 = (f32[512,512]{1,0:T(8,128)S(1)}, f32[512,512]{1,0:T(8,128)}, u32[]{:S(2)}) copy-start(f32[512,512]{1,0:T(8,128)} %inverse_ref.1) | copy-start | bytes 3145732
  5.3 15.0 %collective-permute-start = (f32[520,256]{1,0:T(8,128)S(1)}, f32[520,256]{1,0:T(8,128)S(1)}, u32[]{:S(2)}, u32[]{:S(2)}) collective-permute-start(f32[520,256]{1,0:T(8,128)S(1)} %get-tuple-element.32), channel_id=1, source_target_pairs={{0,1},{1,2},{2,3},{3,4},{4,5},{5,6},{6,7},{7,8},{8,9},{9,10},{10,1... | collective-permute-start | bytes 1597448 | tf_op jit(solution)/shard_map/ppermute | solution.py:34
  10.0 11.5 %copy-start.1 = (f32[512,1536]{1,0:T(8,128)S(1)}, f32[512,1536]{1,0:T(8,128)}, u32[]{:S(2)}) copy-start(f32[512,1536]{1,0:T(8,128)} %old_ref.5) | copy-start | bytes 9437188
  10.0 11.5 %copy-start.5 = (s32[2,256]{1,0:T(2,128)S(1)}, s32[2,256]{1,0:T(2,128)}, u32[]{:S(2)}) copy-start(s32[2,256]{1,0:T(2,128)} %refs_13_.1) | copy-start | bytes 6148
  10.0 11.5 %collective-permute-start.1 = (f32[512,256]{1,0:T(8,128)S(1)}, f32[512,256]{1,0:T(8,128)S(1)}, u32[]{:S(2)}, u32[]{:S(2)}) collective-permute-start(f32[512,256]{1,0:T(8,128)S(1)} %get-tuple-element.33), channel_id=1, source_target_pairs={{1,0},{2,1},{3,2},{4,3},{5,4},{6,5},{7,6},{8,7},{9,8},{10,9},{11,1... | collective-permute-start | bytes 1572872 | tf_op jit(solution)/shard_map/ppermute | solution.py:34
  13.5 22.3 %collective-permute-start.4 = (f32[520,256]{1,0:T(8,128)S(1)}, f32[520,256]{1,0:T(8,128)S(1)}, u32[]{:S(2)}, u32[]{:S(2)}) collective-permute-start(f32[520,256]{1,0:T(8,128)S(1)} %get-tuple-element.38), channel_id=1, source_target_pairs={{0,1},{1,2},{2,3},{3,4},{4,5},{5,6},{6,7},{7,8},{8,9},{9,10},{10,1... | collective-permute-start | bytes 1597448 | tf_op jit(solution)/shard_map/ppermute | solution.py:34
  17.2 18.6 %collective-permute-start.5 = (f32[512,256]{1,0:T(8,128)S(1)}, f32[512,256]{1,0:T(8,128)S(1)}, u32[]{:S(2)}, u32[]{:S(2)}) collective-permute-start(f32[512,256]{1,0:T(8,128)S(1)} %get-tuple-element.39), channel_id=1, source_target_pairs={{1,0},{2,1},{3,2},{4,3},{5,4},{6,5},{7,6},{8,7},{9,8},{10,9},{11,1... | collective-permute-start | bytes 1572872 | tf_op jit(solution)/shard_map/ppermute | solution.py:34
  30.2 14.2 %collective-permute-start.2 = (f32[128,128]{1,0:T(8,128)S(1)}, f32[128,128]{1,0:T(8,128)S(1)}, u32[]{:S(2)}, u32[]{:S(2)}) collective-permute-start(f32[128,128]{1,0:T(8,128)S(1)} %get-tuple-element.36), channel_id=1, source_target_pairs={{0,1},{1,2},{2,3},{3,4},{4,5},{5,6},{6,7},{7,8},{8,9},{9,10},{10,1... | collective-permute-start | bytes 196616 | tf_op jit(solution)/shard_map/ppermute | solution.py:34
  33.8 5.7 %copy-start.3 = (s32[6,1024]{1,0:T(8,128)S(1)}, s32[6,1024]{1,0:T(8,128)}, u32[]{:S(2)}) copy-start(s32[6,1024]{1,0:T(8,128)} %refs_1_.7) | copy-start | bytes 73732
  33.9 10.5 %collective-permute-start.3 = (f32[128,128]{1,0:T(8,128)S(1)}, f32[128,128]{1,0:T(8,128)S(1)}, u32[]{:S(2)}, u32[]{:S(2)}) collective-permute-start(f32[128,128]{1,0:T(8,128)S(1)} %get-tuple-element.37), channel_id=1, source_target_pairs={{1,0},{2,1},{3,2},{4,3},{5,4},{6,5},{7,6},{8,7},{9,8},{10,9},{11,1... | collective-permute-start | bytes 196616 | tf_op jit(solution)/shard_map/ppermute | solution.py:34
  52.3 10.3 %collective-permute-start.6 = (f32[128,128]{1,0:T(8,128)S(1)}, f32[128,128]{1,0:T(8,128)S(1)}, u32[]{:S(2)}, u32[]{:S(2)}) collective-permute-start(f32[128,128]{1,0:T(8,128)S(1)} %get-tuple-element.43), channel_id=1, source_target_pairs={{0,1},{1,2},{2,3},{3,4},{4,5},{5,6},{6,7},{7,8},{8,9},{9,10},{10,1... | collective-permute-start | bytes 196616 | tf_op jit(solution)/shard_map/ppermute | solution.py:34
  56.0 6.7 %collective-permute-start.7 = (f32[128,128]{1,0:T(8,128)S(1)}, f32[128,128]{1,0:T(8,128)S(1)}, u32[]{:S(2)}, u32[]{:S(2)}) collective-permute-start(f32[128,128]{1,0:T(8,128)S(1)} %get-tuple-element.44), channel_id=1, source_target_pairs={{1,0},{2,1},{3,2},{4,3},{5,4},{6,5},{7,6},{8,7},{9,8},{10,9},{11,1... | collective-permute-start | bytes 196616 | tf_op jit(solution)/shard_map/ppermute | solution.py:34
  70.8 10.4 %collective-permute-start.8 = (f32[128,128]{1,0:T(8,128)S(1)}, f32[128,128]{1,0:T(8,128)S(1)}, u32[]{:S(2)}, u32[]{:S(2)}) collective-permute-start(f32[128,128]{1,0:T(8,128)S(1)} %get-tuple-element.48), channel_id=1, source_target_pairs={{0,1},{1,2},{2,3},{3,4},{4,5},{5,6},{6,7},{7,8},{8,9},{9,10},{10,1... | collective-permute-start | bytes 196616 | tf_op jit(solution)/shard_map/ppermute | solution.py:34
  74.4 6.8 %collective-permute-start.9 = (f32[128,128]{1,0:T(8,128)S(1)}, f32[128,128]{1,0:T(8,128)S(1)}, u32[]{:S(2)}, u32[]{:S(2)}) collective-permute-start(f32[128,128]{1,0:T(8,128)S(1)} %get-tuple-element.49), channel_id=1, source_target_pairs={{1,0},{2,1},{3,2},{4,3},{5,4},{6,5},{7,6},{8,7},{9,8},{10,9},{11,1... | collective-permute-start | bytes 196616 | tf_op jit(solution)/shard_map/ppermute | solution.py:34
  89.4 10.4 %collective-permute-start.10 = (f32[128,128]{1,0:T(8,128)S(1)}, f32[128,128]{1,0:T(8,128)S(1)}, u32[]{:S(2)}, u32[]{:S(2)}) collective-permute-start(f32[128,128]{1,0:T(8,128)S(1)} %get-tuple-element.53), channel_id=1, source_target_pairs={{0,1},{1,2},{2,3},{3,4},{4,5},{5,6},{6,7},{7,8},{8,9},{9,10},{10,1... | collective-permute-start | bytes 196616 | tf_op jit(solution)/shard_map/ppermute | solution.py:34
  93.1 6.8 %collective-permute-start.11 = (f32[128,128]{1,0:T(8,128)S(1)}, f32[128,128]{1,0:T(8,128)S(1)}, u32[]{:S(2)}, u32[]{:S(2)}) collective-permute-start(f32[128,128]{1,0:T(8,128)S(1)} %get-tuple-element.54), channel_id=1, source_target_pairs={{1,0},{2,1},{3,2},{4,3},{5,4},{6,5},{7,6},{8,7},{9,8},{10,9},{11,1... | collective-permute-start | bytes 196616 | tf_op jit(solution)/shard_map/ppermute | solution.py:34

commit v2 on v1

v2 whole, which is shorter than its diff:
```python
import functools

import jax
import jax.numpy as jnp
from jax import lax
from jax.experimental import pallas as pl
from jax.experimental.pallas import tpu as pltpu
from jax.sharding import PartitionSpec as P

BE = 8
BCELLS = 512
FACE = 64
BDEV = 1024
MOVE = 256
CAP = 1536
HMAX = 256
ITERS = 2
LANES = 128
SUB = 8
CHUNKS = BDEV // LANES
AXES = ("gx", "gy", "gz")
REMOTE = 6 * BDEV
BASIS = 2 * ITERS + 1
MIB = 1024 * 1024
PARTS = 8
PAIR = 2
F32 = jnp.float32

VMEM = pl.BlockSpec(memory_space=pltpu.VMEM)
SMEM = pl.BlockSpec(memory_space=pltpu.SMEM)
HBM = pl.BlockSpec(memory_space=pltpu.HBM)


def swapped(value, cross):
    count = lax.axis_size(AXES)
    first = 1 if cross else 0
    pairs = [(low, low + 1) for low in range(first, count - 1, 2)]
    return lax.ppermute(value, AXES, pairs + [(high, low) for low, high in pairs])


def call(kernel, outs, args, in_specs, out_specs, scratch=(), limit=24, flops=0, bytes_accessed=0):
    return pl.pallas_call(
        kernel,
        out_shape=outs,
        in_specs=in_specs,
        out_specs=out_specs,
        scratch_shapes=list(scratch),
        compiler_params=pltpu.CompilerParams(vmem_limit_bytes=limit * MIB),
        cost_estimate=pl.CostEstimate(
            flops=flops, bytes_accessed=bytes_accessed, transcendentals=0
        ),
    )(*args)


def lane_iota(rows=SUB):
    return lax.broadcasted_iota(jnp.int32, (rows, LANES), 1)


def lanes(start):
    return pl.ds(pl.multiple_of(start, LANES), LANES)


def pick(values, index):
    return jnp.take_along_axis(values, index, axis=1, mode="promise_in_bounds")


def cut_rows(start, low_ref, high_ref, odd, count, cross_ref, inside_ref):
    tile = start >> 7
    shift = start & (LANES - 1)
    rows = 128

    for step in range(BCELLS // rows):
        at = slice(step * rows, (step + 1) * rows)
        first = lane_iota(rows) < LANES - shift
        turned = []
        for part in range(3):
            source = jnp.minimum(tile + part, high_ref.shape[1] // LANES - 1) * LANES
            turned.append(pltpu.roll(high_ref[at, lanes(source)], (LANES - shift) & (LANES - 1), 1))
        for half in range(2):
            lower = low_ref[at, half * LANES : (half + 1) * LANES]
            upper = jnp.where(first, turned[half], turned[half + 1])
            to = slice(half * BCELLS + step * rows, half * BCELLS + (step + 1) * rows)
            cross_ref[to, :] = jnp.where(odd, upper, lower)
            inside_ref[to, :] = jnp.where(odd, lower, upper)
    if count is not None:
        row = jnp.full((SUB, LANES), count.astype(F32))
        cross_ref[2 * BCELLS : 2 * BCELLS + SUB, :] = row
        inside_ref[2 * BCELLS : 2 * BCELLS + SUB, :] = row


def front_kernel(
    rank_ref, owner_hbm, old_ref, counts_ref, cross_ref, inside_ref,
    owner_ref, low_ref, high_ref, sems
):
    owner_copy = pltpu.make_async_copy(owner_hbm, owner_ref, sems.at[2])
    owner_copy.start()
    low_copy = pltpu.make_async_copy(old_ref.at[:, pl.ds(0, MOVE)], low_ref, sems.at[0])
    low_copy.start()
    owner_copy.wait()
    rank = rank_ref[0]
    owner = owner_ref[...]
    filled = owner >= 0
    head = jnp.sum(((owner == rank - 1) & filled).astype(jnp.int32))
    stay = jnp.sum((owner == rank).astype(jnp.int32))
    tail = jnp.sum(((owner == rank + 1) & filled).astype(jnp.int32))
    odd = rank & 1
    counts_ref[0] = head
    counts_ref[1] = stay
    counts_ref[2] = tail
    counts_ref[3] = odd
    start = head + stay
    window = jnp.clip(start >> 7, 0, CAP // LANES - 3) * LANES
    high_copy = pltpu.make_async_copy(
        old_ref.at[:, pl.ds(pl.multiple_of(window, LANES), 3 * LANES)], high_ref, sems.at[1]
    )
    high_copy.start()
    low_copy.wait()
    high_copy.wait()
    cut_rows(start - window, low_ref, high_ref, odd == 1, tail, cross_ref, inside_ref)


def cut_kernel(counts_ref, old_ref, cross_ref, inside_ref):
    start = counts_ref[0] + counts_ref[1]
    cut_rows(start, old_ref, old_ref, counts_ref[3] == 1, None, cross_ref, inside_ref)


def count_before(odd, cross_ref, inside_ref):
    row = slice(2 * BCELLS, 2 * BCELLS + SUB)
    return jnp.max(jnp.where(odd, inside_ref[row, :], cross_ref[row, :])).astype(jnp.int32)


def assemble(counts_ref, before, old_ref, cross_ref, inside_ref, out_ref, turned_ref):
    head = counts_ref[0]
    stay = counts_ref[1]
    odd = counts_ref[3] == 1
    own_start = head - before
    own_tile = own_start >> 7
    own_shift = own_start & (LANES - 1)
    up_start = -(before + stay)
    up_tile = up_start >> 7
    up_shift = up_start & (LANES - 1)
    rows = 64

    def body(step, carry):
        start = pl.multiple_of(step * rows, rows)
        at = pl.ds(start, rows)
        lane = lane_iota(rows)
        for part in range(2):
            half = pl.ds(part * BCELLS + start, rows)
            turned_ref[part] = pltpu.roll(
                jnp.where(odd, cross_ref[half, :], inside_ref[half, :]),
                (LANES - up_shift) & (LANES - 1),
                1,
            )
        last = None
        for chunk in range(CHUNKS + 1):
            source = jnp.clip(own_tile + chunk, 0, CAP // LANES - 1) * LANES
            now = pltpu.roll(
                old_ref[at, lanes(source)], (LANES - own_shift) & (LANES - 1), 1
            )
            if chunk > 0:
                place = chunk - 1
                column = lane + place * LANES
                own = jnp.where(lane < LANES - own_shift, last, now)
                low_half = turned_ref[jnp.clip(up_tile + place, 0, 1)]
                high_half = turned_ref[jnp.clip(up_tile + place + 1, 0, 1)]
                above = jnp.where(lane < LANES - up_shift, low_half, high_half)
                value = jnp.where(column < before + stay, own, above)
                if place < MOVE // LANES:
                    half = pl.ds(place * BCELLS + start, rows)
                    below = jnp.where(odd, inside_ref[half, :], cross_ref[half, :])
                    value = jnp.where(column < before, below, value)
                out_ref[pl.ds(place * BCELLS + start, rows), :] = value
            last = now
        return carry

    lax.fori_loop(0, BCELLS // rows, body, 0)


def diagonal_kernel(counts_ref, before_ref, old_ref, cross_ref, inside_ref, out_ref, turned_ref):
    assemble(counts_ref, before_ref[0], old_ref, cross_ref, inside_ref, out_ref, turned_ref)


def prepare_kernel(inverse_ref, split_ref, theta_ref):
    inverse = inverse_ref[...]
    size = jnp.abs(inverse)
    by_row = jnp.max(jnp.sum(size, axis=1, keepdims=True), axis=0, keepdims=True)
    by_column = jnp.max(jnp.sum(size, axis=0, keepdims=True), axis=1, keepdims=True)
    bound = 14.5 * jnp.sqrt(by_row) * jnp.sqrt(by_column)
    scale = jnp.full((1, 1), 0.5, F32)
    for power in (64, 32, 16, 8, 4, 2, 1):
        large = bound >= 2.0**power
        bound = jnp.where(large, bound * 2.0**-power, bound)
        scale = jnp.where(large, scale * 2.0**-power, scale)
    for power in (64, 32, 16, 8, 4, 2, 1):
        small = bound < 2.0**-power
        bound = jnp.where(small, bound * 2.0**power, bound)
        scale = jnp.where(small, scale * 2.0**power, scale)
    scaled = inverse * scale
    high = scaled.astype(jnp.bfloat16)
    split_ref[:, 0:BCELLS] = high
    split_ref[:, BCELLS : 2 * BCELLS] = high
    split_ref[:, 2 * BCELLS : 3 * BCELLS] = (scaled - high.astype(F32)).astype(jnp.bfloat16)
    row = lax.broadcasted_iota(jnp.int32, (BCELLS, BCELLS), 0)
    column = lax.broadcasted_iota(jnp.int32, (BCELLS, BCELLS), 1)
    theta_ref[0] = jnp.sum(jnp.where(row == column, scaled, 0.0)) * (6.5 / BCELLS)


def precondition(split_ref, field_ref, out_ref):
    def body(step, carry):
        base = pl.multiple_of(step * (2 * BCELLS), 2 * BCELLS)
        halves = [pl.ds(base + half * BCELLS, BCELLS) for half in range(2)]
        field = jnp.concatenate([field_ref[half, :] for half in halves], axis=1)
        top = field.astype(jnp.bfloat16)
        rest = (field - top.astype(F32)).astype(jnp.bfloat16)
        stacked = jnp.concatenate([top, rest, top], axis=0)
        found = jnp.dot(split_ref[...], stacked, preferred_element_type=F32)
        out_ref[halves[0], :] = found[:, :LANES]
        out_ref[halves[1], :] = found[:, LANES:]
        return carry

    lax.fori_loop(0, CHUNKS // 2, body, 0)


def split_ends(field_ref, first_ref, last_ref):
    first_ref[...] = field_ref[pl.ds(0, CHUNKS * FACE, stride=BE), :]
    last_ref[...] = field_ref[pl.ds(BE - 1, CHUNKS * FACE, stride=BE), :]


def layer_tile(field_ref, ends, which, part, chunk):
    if which >= 4:
        row = chunk * FACE + part * SUB
        return ends[which - 4][row : row + SUB, :]
    row = (part * BE, (BE - 1) * FACE + part * BE, part * FACE, part * FACE + (BE - 1) * BE)[which]
    row = row + chunk * BCELLS
    return field_ref[row : row + SUB, :]


def pack(field_ref, ends, send_ref, odd, cross_ref, inside_ref):
    for cross, out_ref in ((True, cross_ref), (False, inside_ref)):
        for step in range(HMAX // LANES):
            at = slice(step * LANES, (step + 1) * LANES)
            low, high = send_ref[0:1, at], send_ref[1:2, at]
            code = jnp.where(odd, high, low) if cross else jnp.where(odd, low, high)
            code = jnp.broadcast_to(code, (SUB, LANES))
            lane = code & (LANES - 1)
            tile = code >> 7
            found = [jnp.zeros((SUB, LANES), F32) for _ in range(8)]
            for which in range(6):
                for source in range(CHUNKS):
                    here = tile == which * CHUNKS + source
                    for part in range(8):
                        values = layer_tile(field_ref, ends, which, part, source)
                        found[part] = jnp.where(here, pick(values, lane), found[part])
            for part in range(8):
                row = step * FACE + part * SUB
                out_ref[row : row + SUB, :] = found[part]


def put_layers(which, found, half, faces_ref, ends_ref):
    for part in range(8):
        if which < 4:
            base = (half * 4 + which) * FACE + part * SUB
            faces_ref[base : base + SUB, :] = found[part]
        else:
            base = half * BCELLS + part * FACE + (which - 4) * (BE - 1)
            ends_ref[pl.ds(base, SUB, stride=BE), :] = found[part]


def gather_layers(step, codes_ref, first_code, flip, count, source_tile, faces_ref, ends_ref):
    pending = None
    for half in range(PAIR):
        at = lanes((step * PAIR + half) * LANES)
        for which in range(6):
            code = jnp.broadcast_to(codes_ref[which : which + 1, at], (SUB, LANES))
            code = code - first_code(which)
            lane = code & (LANES - 1)
            tile = code >> 7
            if flip is not None:
                tile = tile ^ flip
            found = [jnp.zeros((SUB, LANES), F32) for _ in range(8)]
            for source in range(count):
                here = tile == source
                for part in range(8):
                    values = source_tile(which, part, source)
                    found[part] = jnp.where(here, pick(values, lane), found[part])
            if pending is not None:
                put_layers(*pending, faces_ref, ends_ref)
            pending = (which, found, half)
    put_layers(*pending, faces_ref, ends_ref)


def layer(faces_ref, half, which, part):
    base = (half * 4 + which) * FACE + part * SUB
    return faces_ref[base : base + SUB, :]


def local_kernel(known, theta_ref, codes_ref, diagonal_ref, field_ref, *refs):
    basis = refs[:known]
    gram_in = refs[known][...] if known > 1 else jnp.zeros((SUB, LANES), F32)
    out_ref, gram_ref, first_ref, last_ref, faces_ref, ends_ref, sums_ref = refs[-7:]
    split_ends(field_ref, first_ref, last_ref)
    ends = (first_ref, last_ref)
    cell = lax.broadcasted_iota(jnp.int32, (SUB, LANES), 0)
    theta = theta_ref[0]
    sums_ref[...] = jnp.zeros_like(sums_ref)

    def source_tile(which, part, source):
        return layer_tile(field_ref, ends, which ^ 1, part, source)

    def body(step, carry):
        gather_layers(
            step, codes_ref, lambda which: (which ^ 1) * BDEV, None, CHUNKS, source_tile,
            faces_ref, ends_ref,
        )
        sums = [jnp.zeros((SUB, LANES), F32) for _ in range(known)]
        for half in range(PAIR):
            start = pl.multiple_of((step * PAIR + half) * BCELLS, BCELLS)

            def block(i, j):
                return field_ref[pl.ds(start + (i * BE + j) * BE, SUB), :]

            for i in range(BE):
                for j in range(BE):
                    row = (i * BE + j) * BE
                    rows = pl.ds(start + row, SUB)
                    here = block(i, j)
                    edge = ends_ref[half * BCELLS + row : half * BCELLS + row + SUB, :]
                    beside = block(i - 1, j) if i > 0 else layer(faces_ref, half, 0, j)
                    beside = beside + (
                        block(i + 1, j) if i < BE - 1 else layer(faces_ref, half, 1, j)
                    )
                    beside = beside + (block(i, j - 1) if j > 0 else layer(faces_ref, half, 2, i))
                    beside = beside + (
                        block(i, j + 1) if j < BE - 1 else layer(faces_ref, half, 3, i)
                    )
                    beside = beside + jnp.where(cell == 0, edge, pltpu.roll(here, 1, 0))
                    beside = beside + jnp.where(cell == BE - 1, edge, pltpu.roll(here, BE - 1, 0))
                    newest = basis[-1][rows, :]
                    value = (6.0 + diagonal_ref[rows, :]) * here - beside
                    out_ref[rows, :] = value - theta * newest
                    for k, ref in enumerate(basis):
                        old = newest if k == known - 1 else ref[rows, :]
                        sums[k] = sums[k] + newest * old
        for k, part in enumerate(sums):
            sums_ref[k] += part
        return carry

    lax.fori_loop(0, CHUNKS // PAIR, body, 0)
    place_sums(sums_ref, known, gram_in, gram_ref, (known - 1) * known // 2)


def finish(odd, codes_ref, cross_ref, inside_ref, partial_ref, basis, out_ref, faces_ref, ends_ref, sums_ref):
    cell = lax.broadcasted_iota(jnp.int32, (SUB, LANES), 0)
    is_end = (cell == 0) | (cell == BE - 1)
    if basis:
        sums_ref[...] = jnp.zeros_like(sums_ref)

    def source_tile(which, part, source):
        from_ref = cross_ref if source < HMAX // LANES else inside_ref
        base = source % (HMAX // LANES) * FACE + part * SUB
        return from_ref[base : base + SUB, :]

    def body(step, carry):
        gather_layers(
            step, codes_ref, lambda which: REMOTE, odd * 2, 2 * HMAX // LANES, source_tile,
            faces_ref, ends_ref,
        )
        sums = [jnp.zeros((SUB, LANES), F32) for _ in range(len(basis) + 1)]
        for half in range(PAIR):
            start = pl.multiple_of((step * PAIR + half) * BCELLS, BCELLS)
            for i in range(BE):
                for j in range(BE):
                    row = (i * BE + j) * BE
                    rows = pl.ds(start + row, SUB)
                    edge = ends_ref[half * BCELLS + row : half * BCELLS + row + SUB, :]
                    value = partial_ref[rows, :] - jnp.where(is_end, edge, 0.0)
                    if i == 0:
                        value = value - layer(faces_ref, half, 0, j)
                    if i == BE - 1:
                        value = value - layer(faces_ref, half, 1, j)
                    if j == 0:
                        value = value - layer(faces_ref, half, 2, i)
                    if j == BE - 1:
                        value = value - layer(faces_ref, half, 3, i)
                    out_ref[rows, :] = value
                    if basis:
                        for k, ref in enumerate(basis):
                            sums[k] = sums[k] + value * ref[rows, :]
                        sums[-1] = sums[-1] + value * value
        if basis:
            for k, part in enumerate(sums):
                sums_ref[k] += part
        return carry

    lax.fori_loop(0, CHUNKS // PAIR, body, 0)


def place_sums(sums_ref, count, gram_in, gram_out_ref, first):
    lane = lax.broadcasted_iota(jnp.int32, (SUB, LANES), 1)
    row = gram_in
    for k in range(count):
        row = row + jnp.where(lane == first + k, jnp.sum(sums_ref[k]), 0.0)
    for start in range(0, gram_out_ref.shape[0], SUB):
        gram_out_ref[start : start + SUB, :] = row


def first_kernel(
    counts_ref, old_ref, cross_ref, inside_ref, split_ref, send_ref,
    before_ref, rhs_ref, field_ref, to_cross_ref, to_inside_ref,
    turned_ref, first_ref, last_ref,
):
    odd = counts_ref[3] == 1
    before = count_before(odd, cross_ref, inside_ref)
    before_ref[0] = before
    assemble(counts_ref, before, old_ref, cross_ref, inside_ref, rhs_ref, turned_ref)
    precondition(split_ref, rhs_ref, field_ref)
    split_ends(field_ref, first_ref, last_ref)
    pack(field_ref, (first_ref, last_ref), send_ref, odd, to_cross_ref, to_inside_ref)


def next_kernel(
    counts_ref, codes_ref, cross_ref, inside_ref, partial_ref, split_ref, send_ref,
    out_ref, next_ref, to_cross_ref, to_inside_ref,
    first_ref, last_ref, faces_ref, ends_ref,
):
    odd = counts_ref[3]
    finish(
        odd, codes_ref, cross_ref, inside_ref, partial_ref, (), out_ref, faces_ref, ends_ref, None
    )
    precondition(split_ref, out_ref, next_ref)
    split_ends(next_ref, first_ref, last_ref)
    pack(next_ref, (first_ref, last_ref), send_ref, odd == 1, to_cross_ref, to_inside_ref)


def end_kernel(counts_ref, codes_ref, cross_ref, inside_ref, partial_ref, gram_in_ref, *refs):
    basis = refs[: BASIS - 1]
    out_ref, gram_ref, faces_ref, ends_ref, sums_ref = refs[BASIS - 1 :]
    finish(
        counts_ref[3], codes_ref, cross_ref, inside_ref, partial_ref, basis, out_ref, faces_ref,
        ends_ref, sums_ref,
    )
    place_sums(sums_ref, BASIS, gram_in_ref[...], gram_ref, BASIS * (BASIS - 1) // 2)


def recurrence(gram, theta):
    def dot(left, right):
        total = None
        for a, x in enumerate(left):
            if x is None:
                continue
            part = None
            for b, y in enumerate(right):
                if y is not None:
                    term = gram[max(a, b)][min(a, b)] * y
                    part = term if part is None else part + term
            total = x * part if total is None else total + x * part
        return total

    def add(left, right):
        return [
            y if x is None else x if y is None else x + y for x, y in zip(left, right)
        ]

    def times(factor, vector):
        return [None if x is None else factor * x for x in vector]

    def apply(vector):
        return add([None] + vector[:-1], times(theta, vector))

    one = jnp.ones_like(theta)
    shadow = [one] + [None] * (BASIS - 1)
    residual = shadow
    direction = residual
    rho = gram[0][0]
    rho_next = rho
    total = [None] * BASIS
    along = alpha = omega = None
    for step in range(ITERS):
        if step > 0:
            beta = (rho_next / rho) * (alpha / omega)
            rho = rho_next
            direction = add(residual, times(beta, add(direction, times(-omega, along))))
        along = apply(direction)
        alpha = rho / dot(shadow, along)
        middle = add(residual, times(-alpha, along))
        image = apply(middle)
        omega = dot(image, middle) / dot(image, image)
        total = add(total, add(times(alpha, direction), times(omega, middle)))
        residual = add(middle, times(-omega, image))
        rho_next = dot(shadow, residual)
    return total, residual


def last_kernel(theta_ref, gathered_ref, *refs):
    basis = refs[:BASIS]
    fields = refs[BASIS : 2 * BASIS - 1]
    outs = refs[2 * BASIS - 1 : 2 * BASIS + 1]
    solution_ref, residual_ref, sems = refs[2 * BASIS + 1 :]
    row = jnp.sum(gathered_ref[...], axis=0, keepdims=True)
    lane = lax.broadcasted_iota(jnp.int32, (1, LANES), 1)

    def entry(k):
        return jnp.sum(jnp.where(lane == k, row, 0.0), axis=1, keepdims=True)

    gram = [[entry(a * (a + 1) // 2 + b) for b in range(a + 1)] for a in range(BASIS)]
    theta = jnp.full((1, 1), theta_ref[0])
    total, residual = recurrence(gram, theta)
    total = [None if x is None else jnp.broadcast_to(x, (SUB, LANES)) for x in total]
    residual = [jnp.broadcast_to(x, (SUB, LANES)) for x in residual]
    part = BCELLS // PARTS
    copies = []
    for block in range(PARTS):

        def body(step, carry, block=block):
            start = pl.multiple_of(block * part + step * SUB, SUB)
            for chunk in range(CHUNKS):
                rows = pl.ds(chunk * BCELLS + start, SUB)
                at = slice(chunk * LANES, (chunk + 1) * LANES)
                value = total[0] * fields[0][rows, :]
                for k in range(1, BASIS - 1):
                    value = value + total[k] * fields[k][rows, :]
                solution_ref[pl.ds(start, SUB), at] = value
                value = residual[0] * basis[0][rows, :]
                for k in range(1, BASIS):
                    value = value + residual[k] * basis[k][rows, :]
                residual_ref[pl.ds(start, SUB), at] = value
            return carry

        lax.fori_loop(0, part // SUB, body, 0, unroll=4)
        for k, ref in enumerate((solution_ref, residual_ref)):
            at = slice(block * part, (block + 1) * part)
            copies.append(
                pltpu.make_async_copy(ref.at[at, :], outs[k].at[at, :], sems.at[k, block])
            )
            copies[-1].start()
    for copy in copies:
        copy.wait()


def per_device(rhs_old, diagonal_old, new_owner, face_source, send_layers, block_inverse):
    def of(rows):
        return jax.ShapeDtypeStruct((rows, LANES), F32)

    field_type = of(CHUNKS * BCELLS)
    out_type = jax.ShapeDtypeStruct((BCELLS, BDEV), F32)
    halo_type = of(2 * FACE)
    split_type = jax.ShapeDtypeStruct((BCELLS, 3 * BCELLS), jnp.bfloat16)
    turned = pltpu.VMEM((2, 64, LANES), F32)
    end_layers = [pltpu.VMEM((CHUNKS * FACE, LANES), F32)] * 2
    layers = [pltpu.VMEM((PAIR * 4 * FACE, LANES), F32), pltpu.VMEM((PAIR * BCELLS, LANES), F32)]
    sums = pltpu.VMEM((BASIS, SUB, LANES), F32)

    rank = lax.axis_index(AXES).astype(jnp.int32).reshape(1)
    counts, cross, inside = call(
        front_kernel,
        (jax.ShapeDtypeStruct((4,), jnp.int32), of(2 * BCELLS + SUB), of(2 * BCELLS + SUB)),
        (rank, new_owner.reshape(CAP // LANES, LANES), rhs_old),
        [SMEM, HBM, HBM],
        (SMEM, VMEM, VMEM),
        [
            pltpu.VMEM((CAP // LANES, LANES), jnp.int32),
            pltpu.VMEM((BCELLS, MOVE), F32),
            pltpu.VMEM((BCELLS, 3 * LANES), F32),
            pltpu.SemaphoreType.DMA((3,)),
        ],
        limit=58,
    )
    rhs_cross = swapped(cross, True)
    rhs_inside = swapped(inside, False)
    cross, inside = call(
        cut_kernel,
        (of(2 * BCELLS), of(2 * BCELLS)),
        (counts, diagonal_old),
        [SMEM, VMEM],
        (VMEM, VMEM),
    )
    diagonal_cross = swapped(cross, True)
    diagonal_inside = swapped(inside, False)
    split, theta = call(
        prepare_kernel,
        (split_type, jax.ShapeDtypeStruct((1,), F32)),
        (block_inverse,),
        [VMEM],
        (VMEM, SMEM),
    )
    before, rhs, field, to_cross, to_inside = call(
        first_kernel,
        (jax.ShapeDtypeStruct((1,), jnp.int32),)
        + (field_type, field_type, halo_type, halo_type),
        (counts, rhs_old, rhs_cross, rhs_inside, split, send_layers),
        [SMEM] + [VMEM] * 5,
        (SMEM,) + (VMEM,) * 4,
        [turned] + end_layers,
        flops=10**9,
        bytes_accessed=8 * MIB,
    )
    diagonal = gram = None
    basis = [rhs]
    fields = [field]
    for known in range(1, BASIS):
        from_cross = swapped(to_cross, True)
        from_inside = swapped(to_inside, False)
        if diagonal is None:
            diagonal = call(
                diagonal_kernel,
                field_type,
                (counts, before, diagonal_old, diagonal_cross, diagonal_inside),
                [SMEM, SMEM] + [VMEM] * 3,
                VMEM,
                [turned],
                bytes_accessed=6 * MIB,
            )
        args = [theta, face_source, diagonal, field] + basis + ([gram] if known > 1 else [])
        partial, gram = call(
            functools.partial(local_kernel, known),
            (field_type, of(SUB)),
            tuple(args),
            [SMEM] + [VMEM] * (len(args) - 1),
            (VMEM, VMEM),
            end_layers + layers + [sums],
            flops=10**9,
            bytes_accessed=4 * MIB,
        )
        if known < BASIS - 1:
            value, field, to_cross, to_inside = call(
                next_kernel,
                (field_type, field_type, halo_type, halo_type),
                (counts, face_source, from_cross, from_inside, partial, split, send_layers),
                [SMEM] + [VMEM] * 6,
                (VMEM,) * 4,
                end_layers + layers,
                flops=10**9,
                bytes_accessed=12 * MIB,
            )
            fields.append(field)
        else:
            value, copies = call(
                end_kernel,
                (field_type, of(lax.axis_size(AXES))),
                (counts, face_source, from_cross, from_inside, partial, gram, *basis),
                [SMEM] + [VMEM] * (5 + len(basis)),
                (VMEM, VMEM),
                layers + [sums],
                limit=32,
                flops=10**9,
                bytes_accessed=12 * MIB,
            )
        basis.append(value)
    gathered = lax.all_to_all(copies, AXES, split_axis=0, concat_axis=0, tiled=True)
    return call(
        last_kernel,
        (out_type, out_type),
        (theta, gathered, *basis, *fields),
        [SMEM] + [VMEM] * (2 * BASIS),
        (HBM, HBM),
        [pltpu.VMEM((BCELLS, BDEV), F32)] * 2 + [pltpu.SemaphoreType.DMA((2, PARTS))],
        limit=32,
    )


def solution(mesh):
    return jax.shard_map(
        per_device,
        mesh=mesh,
        in_specs=(
            P(None, AXES),
            P(None, AXES),
            P(AXES),
            P(None, AXES),
            P(None, AXES),
            P(),
        ),
        out_specs=(P(None, AXES), P(None, AXES)),
        check_vma=False,
    )
```

time: 165 us -> 119 us (0.72)
  blocking collectives: 55.3 us -> 27.1 us
  starting transfers between devices: 34.6 us -> 24.9 us
  Pallas kernels: 70.1 us -> 64.3 us
  local copies, waits for them, and re-layouts: 3.12 us -> 0.63 us
    all_gather x1 -> x0, blocking collectives: 55.3 us -> none  [per_device(): gathered = lax.all_gather(gram[0:1], AXES, axis=0, tiled=True)]
    all_to_all x0 -> x1, blocking collectives: none -> 27.1 us  [per_device(): lax.all_to_all(copies, AXES, split_axis=0, concat_axis=0, tiled=True)]
    ppermute x12, starting transfers between devices: 34.6 us -> 24.9 us  [swapped(): lax.ppermute(value, AXES, pairs + [(high, low) for low, high in pairs])]
    pallas_call x15 -> x14, Pallas kernels: 70.1 us -> 64.3 us  [call(): pl.pallas_call(kernel, out_shape=outs, in_specs=in_specs, out_specs=out_s...]
    unnamed x15 -> x18, local copies, waits for them, and re-layouts: 2.61 us -> 0.63 us
  transfers between devices with their start and end apart: 12 -> 12, of which waited for: 0 -> 1; matrix products, arithmetic and copies ran while one was open for 0% -> 0% of each run, Pallas kernels for 21% -> 28%
where the time goes in v2:
time: 119 us
  Pallas kernels  64.3 us (54%)
  blocking collectives  27.1 us (23%)
  starting transfers between devices  24.9 us (21%)
    pallas_call x14, Pallas kernels, call(): pl.pallas_call(kernel, out_shape=outs, in_specs=in_specs, out_specs=out_s...  64.3 us
    all_to_all x1, blocking collectives, per_device(): lax.all_to_all(copies, AXES, split_axis=0, concat_axis=0, tiled=True)  27.1 us
    ppermute x12, starting transfers between devices, swapped(): lax.ppermute(value, AXES, pairs + [(high, low) for low, high in pairs])  24.9 us
  transfers between devices with their start and end apart: 12, of which 1 were waited for; matrix products, arithmetic and copies ran while one was open for 0% of the time, Pallas kernels for 28%

profile of v2, /device:TPU:1, one launch (start us, length us, event | category | flops | bytes accessed | tf_op | source)
XLA Modules:
  0.0 118.8 jit_solution(6258792642168167565)
XLA Ops:
  0.6 3.6 %shard_map.78 = (s32[4]{0:T(128)}, f32[1032,128]{1,0:T(8,128)}, f32[1032,128]{1,0:T(8,128)}) custom-call(s32[1]{0:T(128)} %bitcast.rank_ref, s32[12,128]{1,0:T(8,128)} %bitcast.8, f32[512,1536]{1,0:T(8,128)} %old_ref.5), custom_call_target="tpu_custom_call" | custom-call | tf_op jit(solution)/shard_map/pallas_call | solution.py:42
  4.2 0.0 copy-start.5
  4.2 4.6 %collective-permute-start = (f32[1032,128]{1,0:T(8,128)}, f32[1032,128]{1,0:T(8,128)S(1)}, u32[]{:S(2)}, u32[]{:S(2)}) collective-permute-start(f32[1032,128]{1,0:T(8,128)} %get-tuple-element.38), channel_id=1, source_target_pairs={{1,2},{3,4},{5,6},{7,8},{9,10},{11,12},{13,14},{15,16},{17,18},{19... | collective-permute-start | bytes 1585160 | tf_op jit(solution)/shard_map/ppermute | solution.py:38
  8.9 0.1 collective-permute-start.1
  9.0 0.6 copy-done.7
  9.6 0.8 shard_map.80
  10.4 3.6 %collective-permute-start.4 = (f32[1024,128]{1,0:T(8,128)S(1)}, f32[1024,128]{1,0:T(8,128)S(1)}, u32[]{:S(2)}, u32[]{:S(2)}) collective-permute-start(f32[1024,128]{1,0:T(8,128)S(1)} %get-tuple-element.44), channel_id=1, source_target_pairs={{1,2},{3,4},{5,6},{7,8},{9,10},{11,12},{13,14},{15,16},{17,18},{19... | collective-permute-start | bytes 1572872 | tf_op jit(solution)/shard_map/ppermute | solution.py:38
  14.0 0.1 collective-permute-start.5
  14.1 1.2 shard_map.77
  15.3 0.7 collective-permute-done.cross_ref
  16.0 6.3 %shard_map.79 = (s32[1]{0:T(128)}, f32[4096,128]{1,0:T(8,128)S(1)}, f32[4096,128]{1,0:T(8,128)S(1)}, f32[128,128]{1,0:T(8,128)S(1)}, f32[128,128]{1,0:T(8,128)S(1)}) custom-call(s32[4]{0:T(128)S(1)} %copy-done.7, f32[512,1536]{1,0:T(8,128)S(1)} %copy-done, f32[1032,128]{1,0:T(8,128)S(1)} %collective-permute-done.cross_ref, ...), custom_call_target="tpu_custom_call" | custom-call | flops 1000000000 | bytes 8388608 | tf_op jit(solution)/shard_map/pallas_call | solution.py:42
  22.3 3.6 %collective-permute-start.2 = (f32[128,128]{1,0:T(8,128)S(1)}, f32[128,128]{1,0:T(8,128)S(1)}, u32[]{:S(2)}, u32[]{:S(2)}) collective-permute-start(f32[128,128]{1,0:T(8,128)S(1)} %get-tuple-element.41), channel_id=1, source_target_pairs={{1,2},{3,4},{5,6},{7,8},{9,10},{11,12},{13,14},{15,16},{17,18},{19... | collective-permute-start | bytes 196616 | tf_op jit(solution)/shard_map/ppermute | solution.py:38
  25.9 0.1 collective-permute-start.3
  26.0 0.0 copy-start.4
  26.0 2.5 %shard_map.81.diagonal_ref = f32[4096,128]{1,0:T(8,128)S(1)} custom-call(s32[4]{0:T(128)S(1)} %copy-done.7, s32[1]{0:T(128)} %get-tuple-element.43.before_ref, f32[512,1536]{1,0:T(8,128)S(1)} %copy-done.1, f32[1024,128]{1,0:T(8,128)S(1)} %collective-permute-done.4.cross_ref, f32[1024,128]{1,0:T(8,128)S(1)} %collective-permute-done.5.inside_ref), custom_call_target="tpu_custom_call" | custom-call | bytes 6291456 | tf_op jit(solution)/shard_map/pallas_call | solution.py:42
  28.5 5.4 %shard_map.82 = (f32[4096,128]{1,0:T(8,128)S(1)}, f32[8,128]{1,0:T(8,128)S(1)}) custom-call(f32[1]{0:T(128)} %get-tuple-element.36.theta_ref, s32[6,1024]{1,0:T(8,128)S(1)} %copy-done.4, f32[4096,128]{1,0:T(8,128)S(1)} %shard_map.81.diagonal_ref, f32[4096,128]{1,0:T(8,128)S(1)} %get-tuple-element.46.field_ref.refs_5_, f32[4096,128]{1,0:T(8,128)S(1)} %get-tuple-element.47.refs_0_), custom_call_target="tpu_custom_call" | custom-call | flops 1000000000 | bytes 4194304 | tf_op jit(solution)/shard_map/pallas_call | solution.py:42
  33.9 6.9 %shard_map.83 = (f32[4096,128]{1,0:T(8,128)S(1)}, f32[4096,128]{1,0:T(8,128)S(1)}, f32[128,128]{1,0:T(8,128)S(1)}, f32[128,128]{1,0:T(8,128)S(1)}) custom-call(s32[4]{0:T(128)S(1)} %copy-done.8, s32[6,1024]{1,0:T(8,128)S(1)} %copy-done.4, f32[128,128]{1,0:T(8,128)S(1)} %collective-permute-done.2.cross_ref, f32[128,128]{1,0:T(8,128)S(1)} %collective-permute-done.3.inside_ref, ...), custom_call_target="tpu_custom_call" | custom-call | flops 1000000000 | bytes 12582912 | tf_op jit(solution)/shard_map/pallas_call | solution.py:42
  40.8 0.0 copy-start.2
  40.8 3.5 %collective-permute-start.6 = (f32[128,128]{1,0:T(8,128)S(1)}, f32[128,128]{1,0:T(8,128)S(1)}, u32[]{:S(2)}, u32[]{:S(2)}) collective-permute-start(f32[128,128]{1,0:T(8,128)S(1)} %get-tuple-element.49), channel_id=1, source_target_pairs={{1,2},{3,4},{5,6},{7,8},{9,10},{11,12},{13,14},{15,16},{17,18},{19... | collective-permute-start | bytes 196616 | tf_op jit(solution)/shard_map/ppermute | solution.py:38
  44.3 0.1 collective-permute-start.7
  44.4 5.5 %shard_map.84 = (f32[4096,128]{1,0:T(8,128)S(1)}, f32[8,128]{1,0:T(8,128)S(1)}) custom-call(f32[1]{0:T(128)} %get-tuple-element.36.theta_ref, s32[6,1024]{1,0:T(8,128)S(1)} %copy-done.4, f32[4096,128]{1,0:T(8,128)S(1)} %shard_map.81.diagonal_ref, f32[4096,128]{1,0:T(8,128)S(1)} %get-tuple-element.51.field_ref.refs_6_, ...), custom_call_target="tpu_custom_call" | custom-call | flops 1000000000 | bytes 4194304 | tf_op jit(solution)/shard_map/pallas_call | solution.py:42
  50.0 6.8 %shard_map.85 = (f32[4096,128]{1,0:T(8,128)S(1)}, f32[4096,128]{1,0:T(8,128)S(1)}, f32[128,128]{1,0:T(8,128)S(1)}, f32[128,128]{1,0:T(8,128)S(1)}) custom-call(s32[4]{0:T(128)S(1)} %copy-done.8, s32[6,1024]{1,0:T(8,128)S(1)} %copy-done.4, f32[128,128]{1,0:T(8,128)S(1)} %collective-permute-done.6.cross_ref, f32[128,128]{1,0:T(8,128)S(1)} %collective-permute-done.7.inside_ref, ...), custom_call_target="tpu_custom_call" | custom-call | flops 1000000000 | bytes 12582912 | tf_op jit(solution)/shard_map/pallas_call | solution.py:42
  56.8 3.2 %collective-permute-start.8 = (f32[128,128]{1,0:T(8,128)S(1)}, f32[128,128]{1,0:T(8,128)S(1)}, u32[]{:S(2)}, u32[]{:S(2)}) collective-permute-start(f32[128,128]{1,0:T(8,128)S(1)} %get-tuple-element.55), channel_id=1, source_target_pairs={{1,2},{3,4},{5,6},{7,8},{9,10},{11,12},{13,14},{15,16},{17,18},{19... | collective-permute-start | bytes 196616 | tf_op jit(solution)/shard_map/ppermute | solution.py:38
  60.0 0.3 collective-permute-start.9
  60.3 5.6 %shard_map.86 = (f32[4096,128]{1,0:T(8,128)S(1)}, f32[8,128]{1,0:T(8,128)S(1)}) custom-call(f32[1]{0:T(128)} %get-tuple-element.36.theta_ref, s32[6,1024]{1,0:T(8,128)S(1)} %copy-done.4, f32[4096,128]{1,0:T(8,128)S(1)} %shard_map.81.diagonal_ref, f32[4096,128]{1,0:T(8,128)S(1)} %get-tuple-element.57.field_ref.refs_7_, ...), custom_call_target="tpu_custom_call" | custom-call | flops 1000000000 | bytes 4194304 | tf_op jit(solution)/shard_map/pallas_call | solution.py:42
  65.9 6.9 %shard_map.87 = (f32[4096,128]{1,0:T(8,128)S(1)}, f32[4096,128]{1,0:T(8,128)S(1)}, f32[128,128]{1,0:T(8,128)S(1)}, f32[128,128]{1,0:T(8,128)S(1)}) custom-call(s32[4]{0:T(128)S(1)} %copy-done.8, s32[6,1024]{1,0:T(8,128)S(1)} %copy-done.4, f32[128,128]{1,0:T(8,128)S(1)} %collective-permute-done.8.cross_ref, f32[128,128]{1,0:T(8,128)S(1)} %collective-permute-done.9.inside_ref, ...), custom_call_target="tpu_custom_call" | custom-call | flops 1000000000 | bytes 12582912 | tf_op jit(solution)/shard_map/pallas_call | solution.py:42
  72.8 5.6 %collective-permute-start.10 = (f32[128,128]{1,0:T(8,128)S(1)}, f32[128,128]{1,0:T(8,128)S(1)}, u32[]{:S(2)}, u32[]{:S(2)}) collective-permute-start(f32[128,128]{1,0:T(8,128)S(1)} %get-tuple-element.61), channel_id=1, source_target_pairs={{1,2},{3,4},{5,6},{7,8},{9,10},{11,12},{13,14},{15,16},{17,18},{19... | collective-permute-start | bytes 196616 | tf_op jit(solution)/shard_map/ppermute | solution.py:38
  78.4 0.1 collective-permute-start.11
  78.5 5.8 %shard_map.88 = (f32[4096,128]{1,0:T(8,128)S(1)}, f32[8,128]{1,0:T(8,128)S(1)}) custom-call(f32[1]{0:T(128)} %get-tuple-element.36.theta_ref, s32[6,1024]{1,0:T(8,128)S(1)} %copy-done.4, f32[4096,128]{1,0:T(8,128)S(1)} %shard_map.81.diagonal_ref, f32[4096,128]{1,0:T(8,128)S(1)} %get-tuple-element.63.field_ref.refs_8_, ...), custom_call_target="tpu_custom_call" | custom-call | flops 1000000000 | bytes 4194304 | tf_op jit(solution)/shard_map/pallas_call | solution.py:42
  84.3 3.5 %shard_map.89 = (f32[4096,128]{1,0:T(8,128)S(1)}, f32[128,128]{1,0:T(8,128)S(1)}) custom-call(s32[4]{0:T(128)S(1)} %copy-done.8, s32[6,1024]{1,0:T(8,128)S(1)} %copy-done.4, f32[128,128]{1,0:T(8,128)S(1)} %collective-permute-done.10.cross_ref, f32[128,128]{1,0:T(8,128)S(1)} %collective-permute-done.11.inside_ref, ...), custom_call_target="tpu_custom_call" | custom-call | flops 1000000000 | bytes 12582912 | tf_op jit(solution)/shard_map/pallas_call | solution.py:42
  87.9 27.1 %all_to_all.11 = f32[128,1,128]{2,1,0:T(1,128)S(1)} all-to-all(f32[128,1,128]{2,1,0:T(1,128)S(1)} %bitcast.7), channel_id=1, replica_groups=mesh['gx'=4,'gy'=4,'gz'=8] {'gx','gy','gz'}, dimensions={0} | all-to-all | bytes 131072 | tf_op jit(solution)/shard_map/all_to_all | solution.py:650
  115.0 3.7 %shard_map.90 = (f32[512,1024]{1,0:T(8,128)}, f32[512,1024]{1,0:T(8,128)}) custom-call(f32[1]{0:T(128)} %get-tuple-element.36.theta_ref, f32[128,128]{1,0:T(8,128)S(1)} %bitcast.6, f32[4096,128]{1,0:T(8,128)S(1)} %get-tuple-element.47.refs_0_, f32[4096,128]{1,0:T(8,128)S(1)} %get-tuple-element.52.refs_1_, f32[4096,128]{1,0:T(8,128)S(1)} %get-tuple-element.58.refs_2_, ...), custom_call_target="tpu_custom_call" | custom-call | tf_op jit(solution)/shard_map/pallas_call | solution.py:42
  (25 shorter events, 0.1 us)
Async XLA Ops:
  0.6 8.3 %copy-start.1 = (f32[512,1536]{1,0:T(8,128)S(1)}, f32[512,1536]{1,0:T(8,128)}, u32[]{:S(2)}) copy-start(f32[512,1536]{1,0:T(8,128)} %old_ref.7) | copy-start | bytes 9437188
  4.2 9.9 %copy-start.5 = (f32[512,512]{1,0:T(8,128)S(1)}, f32[512,512]{1,0:T(8,128)}, u32[]{:S(2)}) copy-start(f32[512,512]{1,0:T(8,128)} %inverse_ref.1) | copy-start | bytes 3145732
  4.2 11.8 %collective-permute-start = (f32[1032,128]{1,0:T(8,128)}, f32[1032,128]{1,0:T(8,128)S(1)}, u32[]{:S(2)}, u32[]{:S(2)}) collective-permute-start(f32[1032,128]{1,0:T(8,128)} %get-tuple-element.38), channel_id=1, source_target_pairs={{1,2},{3,4},{5,6},{7,8},{9,10},{11,12},{13,14},{15,16},{17,18},{19... | collective-permute-start | bytes 1585160 | tf_op jit(solution)/shard_map/ppermute | solution.py:38
  8.9 7.1 %collective-permute-start.1 = (f32[1032,128]{1,0:T(8,128)}, f32[1032,128]{1,0:T(8,128)S(1)}, u32[]{:S(2)}, u32[]{:S(2)}) collective-permute-start(f32[1032,128]{1,0:T(8,128)} %get-tuple-element.39), channel_id=1, source_target_pairs={{0,1},{2,3},{4,5},{6,7},{8,9},{10,11},{12,13},{14,15},{16,17},{18,... | collective-permute-start | bytes 1585160 | tf_op jit(solution)/shard_map/ppermute | solution.py:38
  9.0 0.6 copy-start.7
  9.6 6.4 %copy-start = (f32[512,1536]{1,0:T(8,128)S(1)}, f32[512,1536]{1,0:T(8,128)}, u32[]{:S(2)}) copy-start(f32[512,1536]{1,0:T(8,128)} %old_ref.5) | copy-start | bytes 9437188
  9.6 6.4 %copy-start.6 = (s32[2,256]{1,0:T(2,128)S(1)}, s32[2,256]{1,0:T(2,128)}, u32[]{:S(2)}) copy-start(s32[2,256]{1,0:T(2,128)} %send_ref.7) | copy-start | bytes 6148
  10.4 15.6 %collective-permute-start.4 = (f32[1024,128]{1,0:T(8,128)S(1)}, f32[1024,128]{1,0:T(8,128)S(1)}, u32[]{:S(2)}, u32[]{:S(2)}) collective-permute-start(f32[1024,128]{1,0:T(8,128)S(1)} %get-tuple-element.44), channel_id=1, source_target_pairs={{1,2},{3,4},{5,6},{7,8},{9,10},{11,12},{13,14},{15,16},{17,18},{19... | collective-permute-start | bytes 1572872 | tf_op jit(solution)/shard_map/ppermute | solution.py:38
  14.0 12.0 %collective-permute-start.5 = (f32[1024,128]{1,0:T(8,128)S(1)}, f32[1024,128]{1,0:T(8,128)S(1)}, u32[]{:S(2)}, u32[]{:S(2)}) collective-permute-start(f32[1024,128]{1,0:T(8,128)S(1)} %get-tuple-element.45), channel_id=1, source_target_pairs={{0,1},{2,3},{4,5},{6,7},{8,9},{10,11},{12,13},{14,15},{16,17},{18,... | collective-permute-start | bytes 1572872 | tf_op jit(solution)/shard_map/ppermute | solution.py:38
  22.3 11.7 %collective-permute-start.2 = (f32[128,128]{1,0:T(8,128)S(1)}, f32[128,128]{1,0:T(8,128)S(1)}, u32[]{:S(2)}, u32[]{:S(2)}) collective-permute-start(f32[128,128]{1,0:T(8,128)S(1)} %get-tuple-element.41), channel_id=1, source_target_pairs={{1,2},{3,4},{5,6},{7,8},{9,10},{11,12},{13,14},{15,16},{17,18},{19... | collective-permute-start | bytes 196616 | tf_op jit(solution)/shard_map/ppermute | solution.py:38
  25.9 8.0 %collective-permute-start.3 = (f32[128,128]{1,0:T(8,128)S(1)}, f32[128,128]{1,0:T(8,128)S(1)}, u32[]{:S(2)}, u32[]{:S(2)}) collective-permute-start(f32[128,128]{1,0:T(8,128)S(1)} %get-tuple-element.42), channel_id=1, source_target_pairs={{0,1},{2,3},{4,5},{6,7},{8,9},{10,11},{12,13},{14,15},{16,17},{18,... | collective-permute-start | bytes 196616 | tf_op jit(solution)/shard_map/ppermute | solution.py:38
  26.0 2.5 %copy-start.4 = (s32[6,1024]{1,0:T(8,128)S(1)}, s32[6,1024]{1,0:T(8,128)}, u32[]{:S(2)}) copy-start(s32[6,1024]{1,0:T(8,128)} %codes_ref.15) | copy-start | bytes 73732
  28.5 5.4 %copy-start.8 = (s32[4]{0:T(128)S(1)}, s32[4]{0:T(128)}, u32[]{:S(2)}) copy-start(s32[4]{0:T(128)} %get-tuple-element.37.counts_ref) | copy-start | bytes 52
  40.8 9.1 %copy-start.2 = (f32[4096,128]{1,0:T(8,128)}, f32[4096,128]{1,0:T(8,128)S(1)}, u32[]{:S(2)}) copy-start(f32[4096,128]{1,0:T(8,128)S(1)} %get-tuple-element.51.field_ref.refs_6_) | copy-start | bytes 6291460
  40.8 9.1 %collective-permute-start.6 = (f32[128,128]{1,0:T(8,128)S(1)}, f32[128,128]{1,0:T(8,128)S(1)}, u32[]{:S(2)}, u32[]{:S(2)}) collective-permute-start(f32[128,128]{1,0:T(8,128)S(1)} %get-tuple-element.49), channel_id=1, source_target_pairs={{1,2},{3,4},{5,6},{7,8},{9,10},{11,12},{13,14},{15,16},{17,18},{19... | collective-permute-start | bytes 196616 | tf_op jit(solution)/shard_map/ppermute | solution.py:38
  44.3 5.6 %collective-permute-start.7 = (f32[128,128]{1,0:T(8,128)S(1)}, f32[128,128]{1,0:T(8,128)S(1)}, u32[]{:S(2)}, u32[]{:S(2)}) collective-permute-start(f32[128,128]{1,0:T(8,128)S(1)} %get-tuple-element.50), channel_id=1, source_target_pairs={{0,1},{2,3},{4,5},{6,7},{8,9},{10,11},{12,13},{14,15},{16,17},{18,... | collective-permute-start | bytes 196616 | tf_op jit(solution)/shard_map/ppermute | solution.py:38
  56.8 9.1 %collective-permute-start.8 = (f32[128,128]{1,0:T(8,128)S(1)}, f32[128,128]{1,0:T(8,128)S(1)}, u32[]{:S(2)}, u32[]{:S(2)}) collective-permute-start(f32[128,128]{1,0:T(8,128)S(1)} %get-tuple-element.55), channel_id=1, source_target_pairs={{1,2},{3,4},{5,6},{7,8},{9,10},{11,12},{13,14},{15,16},{17,18},{19... | collective-permute-start | bytes 196616 | tf_op jit(solution)/shard_map/ppermute | solution.py:38
  60.0 5.9 %collective-permute-start.9 = (f32[128,128]{1,0:T(8,128)S(1)}, f32[128,128]{1,0:T(8,128)S(1)}, u32[]{:S(2)}, u32[]{:S(2)}) collective-permute-start(f32[128,128]{1,0:T(8,128)S(1)} %get-tuple-element.56), channel_id=1, source_target_pairs={{0,1},{2,3},{4,5},{6,7},{8,9},{10,11},{12,13},{14,15},{16,17},{18,... | collective-permute-start | bytes 196616 | tf_op jit(solution)/shard_map/ppermute | solution.py:38
  72.8 11.5 %collective-permute-start.10 = (f32[128,128]{1,0:T(8,128)S(1)}, f32[128,128]{1,0:T(8,128)S(1)}, u32[]{:S(2)}, u32[]{:S(2)}) collective-permute-start(f32[128,128]{1,0:T(8,128)S(1)} %get-tuple-element.61), channel_id=1, source_target_pairs={{1,2},{3,4},{5,6},{7,8},{9,10},{11,12},{13,14},{15,16},{17,18},{19... | collective-permute-start | bytes 196616 | tf_op jit(solution)/shard_map/ppermute | solution.py:38
  78.4 5.9 %collective-permute-start.11 = (f32[128,128]{1,0:T(8,128)S(1)}, f32[128,128]{1,0:T(8,128)S(1)}, u32[]{:S(2)}, u32[]{:S(2)}) collective-permute-start(f32[128,128]{1,0:T(8,128)S(1)} %get-tuple-element.62), channel_id=1, source_target_pairs={{0,1},{2,3},{4,5},{6,7},{8,9},{10,11},{12,13},{14,15},{16,17},{18,... | collective-permute-start | bytes 196616 | tf_op jit(solution)/shard_map/ppermute | solution.py:38
  84.3 30.6 %copy-start.3 = (f32[4096,128]{1,0:T(8,128)S(1)}, f32[4096,128]{1,0:T(8,128)}, u32[]{:S(2)}) copy-start(f32[4096,128]{1,0:T(8,128)} %copy-done.2) | copy-start | bytes 6291460

commit v3 on v2

v3 whole, which is shorter than its diff:
```python
import functools

import jax
import jax.numpy as jnp
from jax import lax
from jax.experimental import pallas as pl
from jax.experimental.pallas import tpu as pltpu
from jax.sharding import PartitionSpec as P

BE = 8
BCELLS = 512
FACE = 64
BDEV = 1024
MOVE = 256
CAP = 1536
HMAX = 256
ITERS = 2
LANES = 128
SUB = 8
CHUNKS = BDEV // LANES
AXES = ("gx", "gy", "gz")
REMOTE = 6 * BDEV
BASIS = 2 * ITERS + 1
MIB = 1024 * 1024
PARTS = 8
PAIR = 2
FRONT = 52
PRODUCT = (0, 4, 5)
F32 = jnp.float32

VMEM = pl.BlockSpec(memory_space=pltpu.VMEM)
SMEM = pl.BlockSpec(memory_space=pltpu.SMEM)
HBM = pl.BlockSpec(memory_space=pltpu.HBM)


def swapped(value, cross):
    count = lax.axis_size(AXES)
    first = 1 if cross else 0
    pairs = [(low, low + 1) for low in range(first, count - 1, 2)]
    return lax.ppermute(value, AXES, pairs + [(high, low) for low, high in pairs])


def call(kernel, outs, args, in_specs, out_specs, scratch=(), limit=16, flops=0, bytes_accessed=0, aliases=None):
    if aliases is None:
        aliases = {}
    return pl.pallas_call(
        kernel,
        out_shape=outs,
        in_specs=in_specs,
        out_specs=out_specs,
        scratch_shapes=list(scratch),
        input_output_aliases=aliases,
        compiler_params=pltpu.CompilerParams(vmem_limit_bytes=limit * MIB),
        cost_estimate=pl.CostEstimate(
            flops=flops, bytes_accessed=bytes_accessed, transcendentals=0
        ),
    )(*args)


def lane_iota(rows=SUB):
    return lax.broadcasted_iota(jnp.int32, (rows, LANES), 1)


def lanes(start):
    return pl.ds(pl.multiple_of(start, LANES), LANES)


def pick(values, index):
    return jnp.take_along_axis(values, index, axis=1, mode="promise_in_bounds")


def cut_rows(start, low_ref, high_ref, odd, count, cross_ref, inside_ref):
    tile = start >> 7
    shift = start & (LANES - 1)
    rows = 128

    for step in range(BCELLS // rows):
        at = slice(step * rows, (step + 1) * rows)
        first = lane_iota(rows) < LANES - shift
        turned = []
        for part in range(3):
            source = jnp.minimum(tile + part, high_ref.shape[1] // LANES - 1) * LANES
            turned.append(pltpu.roll(high_ref[at, lanes(source)], (LANES - shift) & (LANES - 1), 1))
        for half in range(2):
            lower = low_ref[at, half * LANES : (half + 1) * LANES]
            upper = jnp.where(first, turned[half], turned[half + 1])
            to = slice(half * BCELLS + step * rows, half * BCELLS + (step + 1) * rows)
            cross_ref[to, :] = jnp.where(odd, upper, lower)
            inside_ref[to, :] = jnp.where(odd, lower, upper)
    if count is not None:
        row = jnp.full((SUB, LANES), count.astype(F32))
        cross_ref[2 * BCELLS : 2 * BCELLS + SUB, :] = row
        inside_ref[2 * BCELLS : 2 * BCELLS + SUB, :] = row


def front_kernel(
    rank_ref, owner_ref, old_ref, counts_ref, cross_ref, inside_ref, low_ref, high_ref, sems
):
    high_copy = pltpu.make_async_copy(
        old_ref.at[:, pl.ds(2 * MOVE, CAP - 2 * MOVE)], high_ref, sems.at[1]
    )
    high_copy.start()
    low_copy = pltpu.make_async_copy(old_ref.at[:, pl.ds(0, MOVE)], low_ref, sems.at[0])
    low_copy.start()
    rank = rank_ref[0]
    owner = owner_ref[...]
    filled = owner >= 0
    head = jnp.sum(((owner == rank - 1) & filled).astype(jnp.int32))
    stay = jnp.sum((owner == rank).astype(jnp.int32))
    tail = jnp.sum(((owner == rank + 1) & filled).astype(jnp.int32))
    odd = rank & 1
    row = lax.broadcasted_iota(jnp.int32, (SUB, LANES), 0)
    counts_ref[...] = jnp.where(
        row == 0, head, jnp.where(row == 1, stay, jnp.where(row == 2, tail, odd))
    )
    high_copy.wait()
    low_copy.wait()
    start = head + stay - 2 * MOVE
    cut_rows(start, low_ref, high_ref, odd == 1, tail, cross_ref, inside_ref)


def count_of(counts_ref, row):
    return jnp.max(counts_ref[row : row + 1, :])


def cut_kernel(counts_ref, old_ref, cross_ref, inside_ref):
    start = count_of(counts_ref, 0) + count_of(counts_ref, 1)
    odd = count_of(counts_ref, 3) == 1
    cut_rows(start, old_ref, old_ref, odd, None, cross_ref, inside_ref)


def count_before(odd, cross_ref, inside_ref):
    row = slice(2 * BCELLS, 2 * BCELLS + SUB)
    return jnp.max(jnp.where(odd, inside_ref[row, :], cross_ref[row, :])).astype(jnp.int32)


def assemble(counts_ref, before, old_ref, cross_ref, inside_ref, out_ref, turned_ref):
    head = count_of(counts_ref, 0)
    stay = count_of(counts_ref, 1)
    odd = count_of(counts_ref, 3) == 1
    own_start = head - before
    own_tile = own_start >> 7
    own_shift = own_start & (LANES - 1)
    up_start = -(before + stay)
    up_tile = up_start >> 7
    up_shift = up_start & (LANES - 1)
    rows = 64

    def body(step, carry):
        start = pl.multiple_of(step * rows, rows)
        at = pl.ds(start, rows)
        lane = lane_iota(rows)
        for part in range(2):
            half = pl.ds(part * BCELLS + start, rows)
            turned_ref[part] = pltpu.roll(
                jnp.where(odd, cross_ref[half, :], inside_ref[half, :]),
                (LANES - up_shift) & (LANES - 1),
                1,
            )
        last = None
        for chunk in range(CHUNKS + 1):
            source = jnp.clip(own_tile + chunk, 0, CAP // LANES - 1) * LANES
            now = pltpu.roll(
                old_ref[at, lanes(source)], (LANES - own_shift) & (LANES - 1), 1
            )
            if chunk > 0:
                place = chunk - 1
                column = lane + place * LANES
                own = jnp.where(lane < LANES - own_shift, last, now)
                low_half = turned_ref[jnp.clip(up_tile + place, 0, 1)]
                high_half = turned_ref[jnp.clip(up_tile + place + 1, 0, 1)]
                above = jnp.where(lane < LANES - up_shift, low_half, high_half)
                value = jnp.where(column < before + stay, own, above)
                if place < MOVE // LANES:
                    half = pl.ds(place * BCELLS + start, rows)
                    below = jnp.where(odd, inside_ref[half, :], cross_ref[half, :])
                    value = jnp.where(column < before, below, value)
                out_ref[pl.ds(place * BCELLS + start, rows), :] = value
            last = now
        return carry

    lax.fori_loop(0, BCELLS // rows, body, 0)


def diagonal_kernel(counts_ref, before_ref, old_ref, cross_ref, inside_ref, out_ref, turned_ref):
    assemble(counts_ref, before_ref[0], old_ref, cross_ref, inside_ref, out_ref, turned_ref)


def prepare_kernel(
    rank_ref, inverse_ref, codes_ref, send_ref, split_ref, theta_ref, sent_ref, taken_ref, local_ref
):
    select(rank_ref[0] & 1, codes_ref, send_ref, sent_ref, taken_ref, local_ref)
    inverse = inverse_ref[...]
    size = jnp.abs(inverse)
    by_row = jnp.max(jnp.sum(size, axis=1, keepdims=True), axis=0, keepdims=True)
    by_column = jnp.max(jnp.sum(size, axis=0, keepdims=True), axis=1, keepdims=True)
    bound = 14.5 * jnp.sqrt(by_row) * jnp.sqrt(by_column)
    scale = jnp.full((1, 1), 0.5, F32)
    for power in (64, 32, 16, 8, 4, 2, 1):
        large = bound >= 2.0**power
        bound = jnp.where(large, bound * 2.0**-power, bound)
        scale = jnp.where(large, scale * 2.0**-power, scale)
    for power in (64, 32, 16, 8, 4, 2, 1):
        small = bound < 2.0**-power
        bound = jnp.where(small, bound * 2.0**power, bound)
        scale = jnp.where(small, scale * 2.0**power, scale)
    scaled = inverse * scale
    high = scaled.astype(jnp.bfloat16)
    split_ref[:, 0:BCELLS] = high
    split_ref[:, BCELLS : 2 * BCELLS] = high
    split_ref[:, 2 * BCELLS : 3 * BCELLS] = (scaled - high.astype(F32)).astype(jnp.bfloat16)
    row = lax.broadcasted_iota(jnp.int32, (BCELLS, BCELLS), 0)
    column = lax.broadcasted_iota(jnp.int32, (BCELLS, BCELLS), 1)
    theta_ref[0] = jnp.sum(jnp.where(row == column, scaled, 0.0)) * (6.5 / BCELLS)


def precondition(split_ref, field_ref, out_ref, pair):
    base = pair * 2 * BCELLS
    field = jnp.concatenate(
        [field_ref[base + half * BCELLS : base + (half + 1) * BCELLS, :] for half in range(2)],
        axis=1,
    )
    top = field.astype(jnp.bfloat16)
    rest = (field - top.astype(F32)).astype(jnp.bfloat16)
    stacked = jnp.concatenate([top, rest, top], axis=0)
    found = jnp.dot(split_ref[...], stacked, preferred_element_type=F32)
    out_ref[base : base + BCELLS, :] = found[:, :LANES]
    out_ref[base + BCELLS : base + 2 * BCELLS, :] = found[:, LANES:]


def one_hot(code, out_ref, column):
    rows = 128
    width = code.shape[1]
    base = lax.broadcasted_iota(jnp.int32, (rows, width), 0).astype(jnp.int16)
    one = jnp.ones((rows, width), jnp.bfloat16)
    zero = jnp.zeros((rows, width), jnp.bfloat16)

    def body(step, carry):
        start = pl.multiple_of(step * rows, rows)
        here = base == jnp.broadcast_to((code - start).astype(jnp.int16), (rows, width))
        out_ref[pl.ds(start, rows), column : column + width] = jnp.where(here, one, zero)
        return carry

    lax.fori_loop(0, out_ref.shape[0] // rows, body, 0)


def select(odd, codes_ref, send_ref, sent_ref, taken_ref, local_ref):
    low, high = send_ref[0:1, :], send_ref[1:2, :]
    one_hot(jnp.where(odd == 1, high, low), sent_ref, 0)
    one_hot(jnp.where(odd == 1, low, high), sent_ref, HMAX)
    for which in range(6):
        code = codes_ref[which : which + 1, :]
        for half in range(2):
            part = code[:, half * BCELLS : (half + 1) * BCELLS]
            at = which * BDEV + half * BCELLS
            one_hot((part - REMOTE) ^ (odd * HMAX), taken_ref, at)
            if which in PRODUCT:
                at = PRODUCT.index(which) * BDEV + half * BCELLS
                one_hot(part - (which ^ 1) * BDEV, local_ref, at)


def halves(value):
    top = value.astype(jnp.bfloat16)
    return jnp.concatenate([top, (value - top.astype(F32)).astype(jnp.bfloat16)], axis=0)


def whole_layer(field_ref, which, chunk):
    start = chunk * BCELLS
    if which >= 4:
        return field_ref[pl.ds(start + (which - 4) * (BE - 1), FACE, stride=BE), :]
    if which < 2:
        row = start + which * (BE - 1) * FACE
        return field_ref[row : row + FACE, :]
    rows = [start + part * FACE + (which - 2) * (BE - 1) * BE for part in range(BE)]
    return jnp.concatenate([field_ref[row : row + SUB, :] for row in rows], axis=0)


def split_layers(field_ref, chunk, layers_ref):
    for which in range(6):
        at = (which * CHUNKS + chunk) * LANES
        layers_ref[:, at : at + LANES] = halves(whole_layer(field_ref, which, chunk))


def pack(layers_ref, sent_ref, cross_ref, inside_ref):
    for out_ref, start in ((cross_ref, 0), (inside_ref, HMAX)):
        found = jnp.dot(
            layers_ref[...], sent_ref[:, start : start + HMAX], preferred_element_type=F32
        )
        found = found[:FACE, :] + found[FACE:, :]
        out_ref[0:FACE, :] = found[:, :LANES]
        out_ref[FACE : 2 * FACE, :] = found[:, LANES:]


def layer_tile(field_ref, which, part, chunk):
    row = (part * BE, (BE - 1) * FACE + part * BE, part * FACE, part * FACE + (BE - 1) * BE)[which]
    row = row + chunk * BCELLS
    return field_ref[row : row + SUB, :]


def layer(faces_ref, half, which, part):
    base = (half * 6 + which) * FACE + part * SUB
    return faces_ref[base : base + SUB, :]


def gather_layers(step, codes_ref, field_ref, layers_ref, local_ref, faces_ref):
    for index, which in enumerate(PRODUCT):
        at = index * BDEV + step * (2 * LANES)
        start = (which ^ 1) * BDEV
        found = jnp.dot(
            layers_ref[:, start : start + BDEV],
            local_ref[:, pl.ds(pl.multiple_of(at, 2 * LANES), 2 * LANES)],
            preferred_element_type=F32,
        )
        found = found[:FACE, :] + found[FACE:, :]
        for half in range(PAIR):
            base = (half * 6 + which) * FACE
            faces_ref[base : base + FACE, :] = found[:, half * LANES : (half + 1) * LANES]
    for half in range(PAIR):
        at = lanes((step * PAIR + half) * LANES)
        for which in range(6):
            if which in PRODUCT:
                continue
            partner = which ^ 1
            code = jnp.broadcast_to(codes_ref[which : which + 1, at], (SUB, LANES))
            code = code - partner * BDEV
            lane = code & (LANES - 1)
            tile = code >> 7
            found = [jnp.zeros((SUB, LANES), F32) for _ in range(8)]
            for source in range(CHUNKS):
                here = tile == source
                for part in range(8):
                    values = layer_tile(field_ref, partner, part, source)
                    found[part] = jnp.where(here, pick(values, lane), found[part])
            for part in range(8):
                base = (half * 6 + which) * FACE + part * SUB
                faces_ref[base : base + SUB, :] = found[part]


def local_kernel(
    known, theta_ref, codes_ref, diagonal_ref, field_ref, layers_ref, local_ref, *refs
):
    basis = refs[:known]
    gram_in = refs[known][...] if known > 1 else jnp.zeros((SUB, LANES), F32)
    out_ref, gram_ref, faces_ref, beside_ref, sums_ref = refs[-5:]
    theta = theta_ref[0]
    sums_ref[...] = jnp.zeros_like(sums_ref)

    def body(step, carry):
        gather_layers(step, codes_ref, field_ref, layers_ref, local_ref, faces_ref)
        sums = [jnp.zeros((SUB, LANES), F32) for _ in range(known)]
        for half in range(PAIR):
            start = pl.multiple_of((step * PAIR + half) * BCELLS, BCELLS)

            def block(i, j):
                return field_ref[pl.ds(start + (i * BE + j) * BE, SUB), :]

            for i in range(BE):
                row = [layer(faces_ref, half, 4, i)]
                row += [field_ref[pl.ds(start + i * FACE + k, SUB, stride=BE), :] for k in range(BE)]
                row += [layer(faces_ref, half, 5, i)]
                for k in range(BE):
                    at = pl.ds(half * BCELLS + i * FACE + k, SUB, stride=BE)
                    beside_ref[at, :] = row[k] + row[k + 2]
            for i in range(BE):
                for j in range(BE):
                    row = (i * BE + j) * BE
                    rows = pl.ds(start + row, SUB)
                    here = block(i, j)
                    beside = beside_ref[half * BCELLS + row : half * BCELLS + row + SUB, :]
                    beside = beside + (block(i - 1, j) if i > 0 else layer(faces_ref, half, 0, j))
                    beside = beside + (
                        block(i + 1, j) if i < BE - 1 else layer(faces_ref, half, 1, j)
                    )
                    beside = beside + (block(i, j - 1) if j > 0 else layer(faces_ref, half, 2, i))
                    beside = beside + (
                        block(i, j + 1) if j < BE - 1 else layer(faces_ref, half, 3, i)
                    )
                    newest = basis[-1][rows, :]
                    value = (6.0 + diagonal_ref[rows, :]) * here - beside
                    out_ref[rows, :] = value - theta * newest
                    for k, ref in enumerate(basis):
                        old = newest if k == known - 1 else ref[rows, :]
                        sums[k] = sums[k] + newest * old
        for k, part in enumerate(sums):
            sums_ref[k] += part
        return carry

    lax.fori_loop(0, CHUNKS // PAIR, body, 0)
    place_sums(sums_ref, known, gram_in, gram_ref, (known - 1) * known // 2)


def receive(cross_ref, inside_ref):
    parts = [
        ref[part * FACE : (part + 1) * FACE, :]
        for ref in (cross_ref, inside_ref)
        for part in range(2)
    ]
    return halves(jnp.concatenate(parts, axis=1))


def finish(taken_ref, received, out_ref, pair):
    for which in range(6):
        at = which * BDEV + pair * 2 * LANES
        found = jnp.dot(received, taken_ref[:, at : at + 2 * LANES], preferred_element_type=F32)
        found = found[:FACE, :] + found[FACE:, :]
        for half in range(2):
            start = (pair * 2 + half) * BCELLS
            beside = found[:, half * LANES : (half + 1) * LANES]
            if which >= 4:
                rows = pl.ds(start + (which - 4) * (BE - 1), FACE, stride=BE)
                out_ref[rows, :] = out_ref[rows, :] - beside
            elif which < 2:
                row = start + which * (BE - 1) * FACE
                out_ref[row : row + FACE, :] = out_ref[row : row + FACE, :] - beside
            else:
                for part in range(BE):
                    row = start + part * FACE + (which - 2) * (BE - 1) * BE
                    out_ref[row : row + SUB, :] = (
                        out_ref[row : row + SUB, :] - beside[part * SUB : (part + 1) * SUB, :]
                    )


def place_sums(sums_ref, count, gram_in, gram_out_ref, first):
    lane = lax.broadcasted_iota(jnp.int32, (SUB, LANES), 1)
    row = gram_in
    for k in range(count):
        row = row + jnp.where(lane == first + k, jnp.sum(sums_ref[k]), 0.0)
    for start in range(0, gram_out_ref.shape[0], SUB):
        gram_out_ref[start : start + SUB, :] = row


def send(split_ref, value_ref, field_ref, layers_ref, sent_ref, cross_ref, inside_ref, before):
    for pair in range(CHUNKS // 2):
        before(pair)
        precondition(split_ref, value_ref, field_ref, pair)
        split_layers(field_ref, 2 * pair, layers_ref)
        split_layers(field_ref, 2 * pair + 1, layers_ref)
    pack(layers_ref, sent_ref, cross_ref, inside_ref)


def first_kernel(
    counts_ref, old_ref, cross_ref, inside_ref, split_ref, sent_ref,
    before_ref, rhs_ref, field_ref, layers_ref, to_cross_ref, to_inside_ref,
    turned_ref,
):
    odd = count_of(counts_ref, 3) == 1
    before = count_before(odd, cross_ref, inside_ref)
    before_ref[0] = before
    assemble(counts_ref, before, old_ref, cross_ref, inside_ref, rhs_ref, turned_ref)
    send(
        split_ref, rhs_ref, field_ref, layers_ref, sent_ref, to_cross_ref, to_inside_ref,
        lambda pair: None,
    )


def next_kernel(
    cross_ref, inside_ref, partial_ref, taken_ref, split_ref, sent_ref,
    out_ref, field_ref, layers_ref, to_cross_ref, to_inside_ref,
):
    del partial_ref
    received = receive(cross_ref, inside_ref)
    send(
        split_ref, out_ref, field_ref, layers_ref, sent_ref, to_cross_ref, to_inside_ref,
        lambda pair: finish(taken_ref, received, out_ref, pair),
    )


def end_kernel(cross_ref, inside_ref, partial_ref, taken_ref, gram_in_ref, *refs):
    del partial_ref
    basis = refs[: BASIS - 1]
    out_ref, gram_ref, sums_ref = refs[BASIS - 1 :]
    received = receive(cross_ref, inside_ref)
    for pair in range(CHUNKS // 2):
        finish(taken_ref, received, out_ref, pair)
    sums_ref[...] = jnp.zeros_like(sums_ref)

    def body(step, carry):
        start = pl.multiple_of(step * BCELLS, BCELLS)
        sums = [jnp.zeros((SUB, LANES), F32) for _ in range(BASIS)]
        for row in range(0, BCELLS, SUB):
            rows = pl.ds(start + row, SUB)
            value = out_ref[rows, :]
            for k, ref in enumerate(basis):
                sums[k] = sums[k] + value * ref[rows, :]
            sums[-1] = sums[-1] + value * value
        for k, part in enumerate(sums):
            sums_ref[k] += part
        return carry

    lax.fori_loop(0, CHUNKS, body, 0)
    place_sums(sums_ref, BASIS, gram_in_ref[...], gram_ref, BASIS * (BASIS - 1) // 2)


def recurrence(gram, theta):
    def dot(left, right):
        total = None
        for a, x in enumerate(left):
            if x is None:
                continue
            part = None
            for b, y in enumerate(right):
                if y is not None:
                    term = gram[max(a, b)][min(a, b)] * y
                    part = term if part is None else part + term
            total = x * part if total is None else total + x * part
        return total

    def add(left, right):
        return [
            y if x is None else x if y is None else x + y for x, y in zip(left, right)
        ]

    def times(factor, vector):
        return [None if x is None else factor * x for x in vector]

    def apply(vector):
        return add([None] + vector[:-1], times(theta, vector))

    one = jnp.ones_like(theta)
    shadow = [one] + [None] * (BASIS - 1)
    residual = shadow
    direction = residual
    rho = gram[0][0]
    rho_next = rho
    total = [None] * BASIS
    along = alpha = omega = None
    for step in range(ITERS):
        if step > 0:
            beta = (rho_next / rho) * (alpha / omega)
            rho = rho_next
            direction = add(residual, times(beta, add(direction, times(-omega, along))))
        along = apply(direction)
        alpha = rho / dot(shadow, along)
        middle = add(residual, times(-alpha, along))
        image = apply(middle)
        omega = dot(image, middle) / dot(image, image)
        total = add(total, add(times(alpha, direction), times(omega, middle)))
        residual = add(middle, times(-omega, image))
        rho_next = dot(shadow, residual)
    return total, residual


def last_kernel(theta_ref, gathered_ref, *refs):
    basis = refs[:BASIS]
    fields = refs[BASIS : 2 * BASIS - 1]
    outs = refs[2 * BASIS - 1 : 2 * BASIS + 1]
    solution_ref, residual_ref, sems = refs[2 * BASIS + 1 :]
    row = jnp.sum(gathered_ref[...], axis=0, keepdims=True)
    lane = lax.broadcasted_iota(jnp.int32, (1, LANES), 1)

    def entry(k):
        return jnp.sum(jnp.where(lane == k, row, 0.0), axis=1, keepdims=True)

    gram = [[entry(a * (a + 1) // 2 + b) for b in range(a + 1)] for a in range(BASIS)]
    theta = jnp.full((1, 1), theta_ref[0])
    total, residual = recurrence(gram, theta)
    total = [None if x is None else jnp.broadcast_to(x, (SUB, LANES)) for x in total]
    residual = [jnp.broadcast_to(x, (SUB, LANES)) for x in residual]
    part = BCELLS // PARTS
    copies = []
    for block in range(PARTS):

        def body(step, carry, block=block):
            start = pl.multiple_of(block * part + step * SUB, SUB)
            for chunk in range(CHUNKS):
                rows = pl.ds(chunk * BCELLS + start, SUB)
                at = slice(chunk * LANES, (chunk + 1) * LANES)
                value = total[0] * fields[0][rows, :]
                for k in range(1, BASIS - 1):
                    value = value + total[k] * fields[k][rows, :]
                solution_ref[pl.ds(start, SUB), at] = value
                value = residual[0] * basis[0][rows, :]
                for k in range(1, BASIS):
                    value = value + residual[k] * basis[k][rows, :]
                residual_ref[pl.ds(start, SUB), at] = value
            return carry

        lax.fori_loop(0, part // SUB, body, 0, unroll=4)
        for k, ref in enumerate((solution_ref, residual_ref)):
            at = slice(block * part, (block + 1) * part)
            copies.append(
                pltpu.make_async_copy(ref.at[at, :], outs[k].at[at, :], sems.at[k, block])
            )
            copies[-1].start()
    for copy in copies:
        copy.wait()


def per_device(rhs_old, diagonal_old, new_owner, face_source, send_layers, block_inverse):
    def of(rows):
        return jax.ShapeDtypeStruct((rows, LANES), F32)

    field_type = of(CHUNKS * BCELLS)
    out_type = jax.ShapeDtypeStruct((BCELLS, BDEV), F32)
    halo_type = of(2 * FACE)
    split_type = jax.ShapeDtypeStruct((BCELLS, 3 * BCELLS), jnp.bfloat16)
    turned = pltpu.VMEM((2, 64, LANES), F32)
    layers = [pltpu.VMEM((PAIR * 6 * FACE, LANES), F32), pltpu.VMEM((PAIR * BCELLS, LANES), F32)]
    packed_type = jax.ShapeDtypeStruct((2 * FACE, 6 * BDEV), jnp.bfloat16)
    sums = pltpu.VMEM((BASIS, SUB, LANES), F32)

    rank = lax.axis_index(AXES).astype(jnp.int32).reshape(1)
    counts, cross, inside = call(
        front_kernel,
        (
            jax.ShapeDtypeStruct((SUB, LANES), jnp.int32),
            of(2 * BCELLS + SUB),
            of(2 * BCELLS + SUB),
        ),
        (rank, new_owner.reshape(CAP // LANES, LANES), rhs_old),
        [SMEM, VMEM, HBM],
        (VMEM, VMEM, VMEM),
        [
            pltpu.VMEM((BCELLS, MOVE), F32),
            pltpu.VMEM((BCELLS, CAP - 2 * MOVE), F32),
            pltpu.SemaphoreType.DMA((2,)),
        ],
        limit=FRONT,
    )
    rhs_cross = swapped(cross, True)
    rhs_inside = swapped(inside, False)
    cross, inside = call(
        cut_kernel,
        (of(2 * BCELLS), of(2 * BCELLS)),
        (counts, diagonal_old),
        [VMEM, VMEM],
        (VMEM, VMEM),
    )
    diagonal_cross = swapped(cross, True)
    diagonal_inside = swapped(inside, False)
    split, theta, sent, taken, local = call(
        prepare_kernel,
        (
            split_type,
            jax.ShapeDtypeStruct((1,), F32),
            jax.ShapeDtypeStruct((6 * BDEV, 2 * HMAX), jnp.bfloat16),
            jax.ShapeDtypeStruct((2 * HMAX, 6 * BDEV), jnp.bfloat16),
            jax.ShapeDtypeStruct((BDEV, len(PRODUCT) * BDEV), jnp.bfloat16),
        ),
        (rank, block_inverse, face_source, send_layers),
        [SMEM] + [VMEM] * 3,
        (VMEM, SMEM, VMEM, VMEM, VMEM),
    )
    before, rhs, field, packed, to_cross, to_inside = call(
        first_kernel,
        (jax.ShapeDtypeStruct((1,), jnp.int32),)
        + (field_type, field_type, packed_type, halo_type, halo_type),
        (counts, rhs_old, rhs_cross, rhs_inside, split, sent),
        [VMEM] * 6,
        (SMEM,) + (VMEM,) * 5,
        [turned],
        flops=10**9,
        bytes_accessed=8 * MIB,
    )
    diagonal = gram = None
    basis = [rhs]
    fields = [field]
    for known in range(1, BASIS):
        from_cross = swapped(to_cross, True)
        from_inside = swapped(to_inside, False)
        if diagonal is None:
            diagonal = call(
                diagonal_kernel,
                field_type,
                (counts, before, diagonal_old, diagonal_cross, diagonal_inside),
                [VMEM, SMEM] + [VMEM] * 3,
                VMEM,
                [turned],
                bytes_accessed=6 * MIB,
            )
        args = [theta, face_source, diagonal, field, packed, local] + basis + ([gram] if known > 1 else [])
        partial, gram = call(
            functools.partial(local_kernel, known),
            (field_type, of(SUB)),
            tuple(args),
            [SMEM] + [VMEM] * (len(args) - 1),
            (VMEM, VMEM),
            layers + [sums],
            flops=10**9,
            bytes_accessed=4 * MIB,
        )
        if known < BASIS - 1:
            value, field, packed, to_cross, to_inside = call(
                next_kernel,
                (field_type, field_type, packed_type, halo_type, halo_type),
                (from_cross, from_inside, partial, taken, split, sent),
                [VMEM] * 6,
                (VMEM,) * 5,
                flops=10**9,
                bytes_accessed=12 * MIB,
                aliases={2: 0},
            )
            fields.append(field)
        else:
            value, copies = call(
                end_kernel,
                (field_type, of(lax.axis_size(AXES))),
                (from_cross, from_inside, partial, taken, gram, *basis),
                [VMEM] * (5 + len(basis)),
                (VMEM, VMEM),
                [sums],
                flops=10**9,
                bytes_accessed=12 * MIB,
                aliases={2: 0},
            )
        basis.append(value)
    gathered = lax.all_to_all(copies, AXES, split_axis=0, concat_axis=0, tiled=True)
    return call(
        last_kernel,
        (out_type, out_type),
        (theta, gathered, *basis, *fields),
        [SMEM] + [VMEM] * (2 * BASIS),
        (HBM, HBM),
        [pltpu.VMEM((BCELLS, BDEV), F32)] * 2 + [pltpu.SemaphoreType.DMA((2, PARTS))],
        limit=16,
    )


def solution(mesh):
    return jax.shard_map(
        per_device,
        mesh=mesh,
        in_specs=(
            P(None, AXES),
            P(None, AXES),
            P(AXES),
            P(None, AXES),
            P(None, AXES),
            P(),
        ),
        out_specs=(P(None, AXES), P(None, AXES)),
        check_vma=False,
    )
```

time: 119 us -> 104 us (0.87)
  Pallas kernels: 64.3 us -> 50.4 us
  starting transfers between devices: 24.9 us -> 23.3 us
    pallas_call x14, Pallas kernels: 64.3 us -> 50.4 us  [call(): pl.pallas_call(kernel, out_shape=outs, in_specs=in_specs, out_specs=out_s...]
    ppermute x12, starting transfers between devices: 24.9 us -> 23.3 us  [swapped(): lax.ppermute(value, AXES, pairs + [(high, low) for low, high in pairs])]
  transfers between devices with their start and end apart: 12 -> 12, of which waited for: 1 -> 0; matrix products, arithmetic and copies ran while one was open for 0% -> 0% of each run, Pallas kernels for 28% -> 29%
where the time goes in v3:
time: 104 us; the launch traced here: 103 us
  Pallas kernels  50.4 us (48%)
  blocking collectives  27.3 us (26%)
  starting transfers between devices  23.3 us (22%)
  between operations  1.2 us (1%)
    pallas_call x14, Pallas kernels, call(): pl.pallas_call(kernel, out_shape=outs, in_specs=in_specs, out_specs=out_s...  50.4 us
    all_to_all x1, blocking collectives, per_device(): lax.all_to_all(copies, AXES, split_axis=0, concat_axis=0, tiled=True)  27.3 us
    ppermute x12, starting transfers between devices, swapped(): lax.ppermute(value, AXES, pairs + [(high, low) for low, high in pairs])  23.3 us
  transfers between devices with their start and end apart: 12, of which 0 were waited for; matrix products, arithmetic and copies ran while one was open for 0% of the time, Pallas kernels for 29%

profile of v3, /device:TPU:1, one launch (start us, length us, event | category | flops | bytes accessed | tf_op | source)
XLA Modules:
  0.0 103.2 jit_solution(16995821078140052371)
XLA Ops:
  0.7 0.8 copy-done.6
  1.5 2.1 %shard_map.78 = (s32[8,128]{1,0:T(8,128)S(1)}, f32[1032,128]{1,0:T(8,128)S(1)}, f32[1032,128]{1,0:T(8,128)S(1)}) custom-call(s32[1]{0:T(128)} %bitcast.rank_ref, s32[12,128]{1,0:T(8,128)S(1)} %bitcast.8, f32[512,1536]{1,0:T(8,128)} %old_ref.5), custom_call_target="tpu_custom_call" | custom-call | tf_op jit(solution)/shard_map/pallas_call | solution.py:46
  3.6 0.0 copy-start.4
  3.6 0.0 copy-start.5
  3.6 0.0 copy-start.7
  3.6 4.6 %collective-permute-start = (f32[1032,128]{1,0:T(8,128)S(1)}, f32[1032,128]{1,0:T(8,128)S(1)}, u32[]{:S(2)}, u32[]{:S(2)}) collective-permute-start(f32[1032,128]{1,0:T(8,128)S(1)} %get-tuple-element.45), channel_id=1, source_target_pairs={{1,2},{3,4},{5,6},{7,8},{9,10},{11,12},{13,14},{15,16},{17,18},{19... | collective-permute-start | bytes 1585160 | tf_op jit(solution)/shard_map/ppermute | solution.py:40
  8.2 0.1 collective-permute-start.1
  8.4 0.5 shard_map.80
  8.8 3.6 %collective-permute-start.4 = (f32[1024,128]{1,0:T(8,128)S(1)}, f32[1024,128]{1,0:T(8,128)S(1)}, u32[]{:S(2)}, u32[]{:S(2)}) collective-permute-start(f32[1024,128]{1,0:T(8,128)S(1)} %get-tuple-element.52), channel_id=1, source_target_pairs={{1,2},{3,4},{5,6},{7,8},{9,10},{11,12},{13,14},{15,16},{17,18},{19... | collective-permute-start | bytes 1572872 | tf_op jit(solution)/shard_map/ppermute | solution.py:40
  12.5 0.1 collective-permute-start.5
  12.6 4.6 %shard_map.77 = (bf16[512,1536]{1,0:T(8,128)(2,1)S(1)}, f32[1]{0:T(128)}, bf16[6144,512]{1,0:T(8,128)(2,1)S(1)}, bf16[512,6144]{1,0:T(8,128)(2,1)S(1)}, bf16[1024,3072]{1,0:T(8,128)(2,1)S(1)}) custom-call(s32[1]{0:T(128)} %bitcast.rank_ref, f32[512,512]{1,0:T(8,128)S(1)} %copy-done.4, s32[6,1024]{1,0:T(8,128)S(1)} %copy-done.5, s32[2,256]{1,0:T(2,128)S(1)} %copy-done.7), custom_call_target="tpu_custom_call" | custom-call | tf_op jit(solution)/shard_map/pallas_call | solution.py:46
  17.2 4.5 %shard_map.79 = (s32[1]{0:T(128)}, f32[4096,128]{1,0:T(8,128)S(1)}, f32[4096,128]{1,0:T(8,128)S(1)}, bf16[128,6144]{1,0:T(8,128)(2,1)S(1)}, f32[128,128]{1,0:T(8,128)S(1)}, /*index=5*/f32[128,128]{1,0:T(8,128)S(1)}) custom-call(s32[8,128]{1,0:T(8,128)S(1)} %get-tuple-element.44.counts_ref, f32[512,1536]{1,0:T(8,128)S(1)} %copy-done.1, ...), custom_call_target="tpu_custom_call" | custom-call | flops 1000000000 | bytes 8388608 | tf_op jit(solution)/shard_map/pallas_call | solution.py:46
  21.7 3.2 %collective-permute-start.2 = (f32[128,128]{1,0:T(8,128)S(1)}, f32[128,128]{1,0:T(8,128)S(1)}, u32[]{:S(2)}, u32[]{:S(2)}) collective-permute-start(f32[128,128]{1,0:T(8,128)S(1)} %get-tuple-element.49), channel_id=1, source_target_pairs={{1,2},{3,4},{5,6},{7,8},{9,10},{11,12},{13,14},{15,16},{17,18},{19... | collective-permute-start | bytes 196616 | tf_op jit(solution)/shard_map/ppermute | solution.py:40
  24.9 0.1 collective-permute-start.3
  25.0 2.1 %shard_map.81.diagonal_ref = f32[4096,128]{1,0:T(8,128)S(1)} custom-call(s32[8,128]{1,0:T(8,128)S(1)} %get-tuple-element.44.counts_ref, s32[1]{0:T(128)} %get-tuple-element.51.before_ref, f32[512,1536]{1,0:T(8,128)S(1)} %copy-done, f32[1024,128]{1,0:T(8,128)S(1)} %collective-permute-done.4.cross_ref, f32[1024,128]{1,0:T(8,128)S(1)} %collective-permute-done.5.inside_ref), custom_call_target="tpu_custom_call" | custom-call | bytes 6291456 | tf_op jit(solution)/shard_map/pallas_call | solution.py:46
  27.2 4.2 %shard_map.82 = (f32[4096,128]{1,0:T(8,128)S(1)}, f32[8,128]{1,0:T(8,128)S(1)}) custom-call(f32[1]{0:T(128)} %get-tuple-element.43.theta_ref, s32[6,1024]{1,0:T(8,128)S(1)} %copy-done.5, f32[4096,128]{1,0:T(8,128)S(1)} %shard_map.81.diagonal_ref, f32[4096,128]{1,0:T(8,128)S(1)} %get-tuple-element.54.field_ref.refs_5_, ...), custom_call_target="tpu_custom_call" | custom-call | flops 1000000000 | bytes 4194304 | tf_op jit(solution)/shard_map/pallas_call | solution.py:46
  31.4 4.0 %shard_map.83 = (f32[4096,128]{1,0:T(8,128)S(1)}, f32[4096,128]{1,0:T(8,128)S(1)}, bf16[128,6144]{1,0:T(8,128)(2,1)S(1)}, f32[128,128]{1,0:T(8,128)S(1)}, f32[128,128]{1,0:T(8,128)S(1)}) custom-call(f32[128,128]{1,0:T(8,128)S(1)} %collective-permute-done.2.cross_ref, ...), custom_call_target="tpu_custom_call", output_to_operand_aliasing={{0}: (2, {})} | custom-call | flops 1000000000 | bytes 12582912 | tf_op jit(solution)/shard_map/pallas_call | solution.py:46
  35.5 3.5 %collective-permute-start.6 = (f32[128,128]{1,0:T(8,128)S(1)}, f32[128,128]{1,0:T(8,128)S(1)}, u32[]{:S(2)}, u32[]{:S(2)}) collective-permute-start(f32[128,128]{1,0:T(8,128)S(1)} %get-tuple-element.60), channel_id=1, source_target_pairs={{1,2},{3,4},{5,6},{7,8},{9,10},{11,12},{13,14},{15,16},{17,18},{19... | collective-permute-start | bytes 196616 | tf_op jit(solution)/shard_map/ppermute | solution.py:40
  39.0 0.3 collective-permute-start.7
  39.2 4.6 %shard_map.84 = (f32[4096,128]{1,0:T(8,128)S(1)}, f32[8,128]{1,0:T(8,128)S(1)}) custom-call(f32[1]{0:T(128)} %get-tuple-element.43.theta_ref, s32[6,1024]{1,0:T(8,128)S(1)} %copy-done.5, f32[4096,128]{1,0:T(8,128)S(1)} %shard_map.81.diagonal_ref, f32[4096,128]{1,0:T(8,128)S(1)} %get-tuple-element.62.field_ref.refs_6_, ...), custom_call_target="tpu_custom_call" | custom-call | flops 1000000000 | bytes 4194304 | tf_op jit(solution)/shard_map/pallas_call | solution.py:46
  43.8 4.0 %shard_map.85 = (f32[4096,128]{1,0:T(8,128)S(1)}, f32[4096,128]{1,0:T(8,128)S(1)}, bf16[128,6144]{1,0:T(8,128)(2,1)S(1)}, f32[128,128]{1,0:T(8,128)S(1)}, f32[128,128]{1,0:T(8,128)S(1)}) custom-call(f32[128,128]{1,0:T(8,128)S(1)} %collective-permute-done.6.cross_ref, ...), custom_call_target="tpu_custom_call", output_to_operand_aliasing={{0}: (2, {})} | custom-call | flops 1000000000 | bytes 12582912 | tf_op jit(solution)/shard_map/pallas_call | solution.py:46
  47.9 4.0 %collective-permute-start.8 = (f32[128,128]{1,0:T(8,128)S(1)}, f32[128,128]{1,0:T(8,128)S(1)}, u32[]{:S(2)}, u32[]{:S(2)}) collective-permute-start(f32[128,128]{1,0:T(8,128)S(1)} %get-tuple-element.67), channel_id=1, source_target_pairs={{1,2},{3,4},{5,6},{7,8},{9,10},{11,12},{13,14},{15,16},{17,18},{19... | collective-permute-start | bytes 196616 | tf_op jit(solution)/shard_map/ppermute | solution.py:40
  51.9 0.1 collective-permute-start.9
  52.0 4.6 %shard_map.86 = (f32[4096,128]{1,0:T(8,128)S(1)}, f32[8,128]{1,0:T(8,128)S(1)}) custom-call(f32[1]{0:T(128)} %get-tuple-element.43.theta_ref, s32[6,1024]{1,0:T(8,128)S(1)} %copy-done.5, f32[4096,128]{1,0:T(8,128)S(1)} %shard_map.81.diagonal_ref, f32[4096,128]{1,0:T(8,128)S(1)} %get-tuple-element.69.field_ref.refs_7_, ...), custom_call_target="tpu_custom_call" | custom-call | flops 1000000000 | bytes 4194304 | tf_op jit(solution)/shard_map/pallas_call | solution.py:46
  56.6 4.1 %shard_map.87 = (f32[4096,128]{1,0:T(8,128)S(1)}, f32[4096,128]{1,0:T(8,128)S(1)}, bf16[128,6144]{1,0:T(8,128)(2,1)S(1)}, f32[128,128]{1,0:T(8,128)S(1)}, f32[128,128]{1,0:T(8,128)S(1)}) custom-call(f32[128,128]{1,0:T(8,128)S(1)} %collective-permute-done.8.cross_ref, ...), custom_call_target="tpu_custom_call", output_to_operand_aliasing={{0}: (2, {})} | custom-call | flops 1000000000 | bytes 12582912 | tf_op jit(solution)/shard_map/pallas_call | solution.py:46
  60.7 3.7 %collective-permute-start.10 = (f32[128,128]{1,0:T(8,128)S(1)}, f32[128,128]{1,0:T(8,128)S(1)}, u32[]{:S(2)}, u32[]{:S(2)}) collective-permute-start(f32[128,128]{1,0:T(8,128)S(1)} %get-tuple-element.74), channel_id=1, source_target_pairs={{1,2},{3,4},{5,6},{7,8},{9,10},{11,12},{13,14},{15,16},{17,18},{19... | collective-permute-start | bytes 196616 | tf_op jit(solution)/shard_map/ppermute | solution.py:40
  64.4 0.1 collective-permute-start.11
  64.5 4.8 %shard_map.88 = (f32[4096,128]{1,0:T(8,128)S(1)}, f32[8,128]{1,0:T(8,128)S(1)}) custom-call(f32[1]{0:T(128)} %get-tuple-element.43.theta_ref, s32[6,1024]{1,0:T(8,128)S(1)} %copy-done.5, f32[4096,128]{1,0:T(8,128)S(1)} %shard_map.81.diagonal_ref, f32[4096,128]{1,0:T(8,128)S(1)} %get-tuple-element.76.field_ref.refs_8_, ...), custom_call_target="tpu_custom_call" | custom-call | flops 1000000000 | bytes 4194304 | tf_op jit(solution)/shard_map/pallas_call | solution.py:46
  69.3 0.0 copy-start.3
  69.4 2.6 %shard_map.89 = (f32[4096,128]{1,0:T(8,128)S(1)}, f32[128,128]{1,0:T(8,128)S(1)}) custom-call(f32[128,128]{1,0:T(8,128)S(1)} %collective-permute-done.10.cross_ref, f32[128,128]{1,0:T(8,128)S(1)} %collective-permute-done.11.inside_ref, f32[4096,128]{1,0:T(8,128)S(1)} %get-tuple-element.80.partial_ref, ...), custom_call_target="tpu_custom_call", output_to_operand_aliasing={{0}: (2, {})} | custom-call | flops 1000000000 | bytes 12582912 | tf_op jit(solution)/shard_map/pallas_call | solution.py:46
  71.9 27.3 %all_to_all.11 = f32[128,1,128]{2,1,0:T(1,128)S(1)} all-to-all(f32[128,1,128]{2,1,0:T(1,128)S(1)} %bitcast.7), channel_id=1, replica_groups=mesh['gx'=4,'gy'=4,'gz'=8] {'gx','gy','gz'}, dimensions={0} | all-to-all | bytes 131072 | tf_op jit(solution)/shard_map/all_to_all | solution.py:707
  99.3 3.8 %shard_map.90 = (f32[512,1024]{1,0:T(8,128)}, f32[512,1024]{1,0:T(8,128)}) custom-call(f32[1]{0:T(128)} %get-tuple-element.43.theta_ref, f32[128,128]{1,0:T(8,128)S(1)} %bitcast.6, f32[4096,128]{1,0:T(8,128)S(1)} %get-tuple-element.57.refs_0_, f32[4096,128]{1,0:T(8,128)S(1)} %get-tuple-element.64.refs_1_, f32[4096,128]{1,0:T(8,128)S(1)} %get-tuple-element.71.refs_2_, ...), custom_call_target="tpu_custom_call" | custom-call | tf_op jit(solution)/shard_map/pallas_call | solution.py:46
  (23 shorter events, 0.1 us)
Async XLA Ops:
  0.6 7.7 %copy-start = (f32[512,1536]{1,0:T(8,128)S(1)}, f32[512,1536]{1,0:T(8,128)}, u32[]{:S(2)}) copy-start(f32[512,1536]{1,0:T(8,128)} %old_ref.7) | copy-start | bytes 9437188
  0.6 0.8 copy-start.6
  3.6 9.0 %copy-start.4 = (f32[512,512]{1,0:T(8,128)S(1)}, f32[512,512]{1,0:T(8,128)}, u32[]{:S(2)}) copy-start(f32[512,512]{1,0:T(8,128)} %inverse_ref.1) | copy-start | bytes 3145732
  3.6 9.0 %copy-start.5 = (s32[6,1024]{1,0:T(8,128)S(1)}, s32[6,1024]{1,0:T(8,128)}, u32[]{:S(2)}) copy-start(s32[6,1024]{1,0:T(8,128)} %codes_ref.9) | copy-start | bytes 73732
  3.6 9.0 %copy-start.7 = (s32[2,256]{1,0:T(2,128)S(1)}, s32[2,256]{1,0:T(2,128)}, u32[]{:S(2)}) copy-start(s32[2,256]{1,0:T(2,128)} %send_ref.1) | copy-start | bytes 6148
  3.6 13.6 %collective-permute-start = (f32[1032,128]{1,0:T(8,128)S(1)}, f32[1032,128]{1,0:T(8,128)S(1)}, u32[]{:S(2)}, u32[]{:S(2)}) collective-permute-start(f32[1032,128]{1,0:T(8,128)S(1)} %get-tuple-element.45), channel_id=1, source_target_pairs={{1,2},{3,4},{5,6},{7,8},{9,10},{11,12},{13,14},{15,16},{17,18},{19... | collective-permute-start | bytes 1585160 | tf_op jit(solution)/shard_map/ppermute | solution.py:40
  8.2 9.0 %collective-permute-start.1 = (f32[1032,128]{1,0:T(8,128)S(1)}, f32[1032,128]{1,0:T(8,128)S(1)}, u32[]{:S(2)}, u32[]{:S(2)}) collective-permute-start(f32[1032,128]{1,0:T(8,128)S(1)} %get-tuple-element.46), channel_id=1, source_target_pairs={{0,1},{2,3},{4,5},{6,7},{8,9},{10,11},{12,13},{14,15},{16,17},{18,... | collective-permute-start | bytes 1585160 | tf_op jit(solution)/shard_map/ppermute | solution.py:40
  8.4 8.9 %copy-start.1 = (f32[512,1536]{1,0:T(8,128)S(1)}, f32[512,1536]{1,0:T(8,128)}, u32[]{:S(2)}) copy-start(f32[512,1536]{1,0:T(8,128)} %old_ref.5) | copy-start | bytes 9437188
  8.8 16.2 %collective-permute-start.4 = (f32[1024,128]{1,0:T(8,128)S(1)}, f32[1024,128]{1,0:T(8,128)S(1)}, u32[]{:S(2)}, u32[]{:S(2)}) collective-permute-start(f32[1024,128]{1,0:T(8,128)S(1)} %get-tuple-element.52), channel_id=1, source_target_pairs={{1,2},{3,4},{5,6},{7,8},{9,10},{11,12},{13,14},{15,16},{17,18},{19... | collective-permute-start | bytes 1572872 | tf_op jit(solution)/shard_map/ppermute | solution.py:40
  12.5 12.5 %collective-permute-start.5 = (f32[1024,128]{1,0:T(8,128)S(1)}, f32[1024,128]{1,0:T(8,128)S(1)}, u32[]{:S(2)}, u32[]{:S(2)}) collective-permute-start(f32[1024,128]{1,0:T(8,128)S(1)} %get-tuple-element.53), channel_id=1, source_target_pairs={{0,1},{2,3},{4,5},{6,7},{8,9},{10,11},{12,13},{14,15},{16,17},{18,... | collective-permute-start | bytes 1572872 | tf_op jit(solution)/shard_map/ppermute | solution.py:40
  21.7 5.5 %copy-start.2 = (f32[4096,128]{1,0:T(8,128)}, f32[4096,128]{1,0:T(8,128)S(1)}, u32[]{:S(2)}) copy-start(f32[4096,128]{1,0:T(8,128)S(1)} %get-tuple-element.54.field_ref.refs_5_) | copy-start | bytes 6291460
  21.7 9.7 %collective-permute-start.2 = (f32[128,128]{1,0:T(8,128)S(1)}, f32[128,128]{1,0:T(8,128)S(1)}, u32[]{:S(2)}, u32[]{:S(2)}) collective-permute-start(f32[128,128]{1,0:T(8,128)S(1)} %get-tuple-element.49), channel_id=1, source_target_pairs={{1,2},{3,4},{5,6},{7,8},{9,10},{11,12},{13,14},{15,16},{17,18},{19... | collective-permute-start | bytes 196616 | tf_op jit(solution)/shard_map/ppermute | solution.py:40
  24.9 6.5 %collective-permute-start.3 = (f32[128,128]{1,0:T(8,128)S(1)}, f32[128,128]{1,0:T(8,128)S(1)}, u32[]{:S(2)}, u32[]{:S(2)}) collective-permute-start(f32[128,128]{1,0:T(8,128)S(1)} %get-tuple-element.50), channel_id=1, source_target_pairs={{0,1},{2,3},{4,5},{6,7},{8,9},{10,11},{12,13},{14,15},{16,17},{18,... | collective-permute-start | bytes 196616 | tf_op jit(solution)/shard_map/ppermute | solution.py:40
  35.5 8.4 %collective-permute-start.6 = (f32[128,128]{1,0:T(8,128)S(1)}, f32[128,128]{1,0:T(8,128)S(1)}, u32[]{:S(2)}, u32[]{:S(2)}) collective-permute-start(f32[128,128]{1,0:T(8,128)S(1)} %get-tuple-element.60), channel_id=1, source_target_pairs={{1,2},{3,4},{5,6},{7,8},{9,10},{11,12},{13,14},{15,16},{17,18},{19... | collective-permute-start | bytes 196616 | tf_op jit(solution)/shard_map/ppermute | solution.py:40
  39.0 4.9 %collective-permute-start.7 = (f32[128,128]{1,0:T(8,128)S(1)}, f32[128,128]{1,0:T(8,128)S(1)}, u32[]{:S(2)}, u32[]{:S(2)}) collective-permute-start(f32[128,128]{1,0:T(8,128)S(1)} %get-tuple-element.61), channel_id=1, source_target_pairs={{0,1},{2,3},{4,5},{6,7},{8,9},{10,11},{12,13},{14,15},{16,17},{18,... | collective-permute-start | bytes 196616 | tf_op jit(solution)/shard_map/ppermute | solution.py:40
  47.9 8.7 %collective-permute-start.8 = (f32[128,128]{1,0:T(8,128)S(1)}, f32[128,128]{1,0:T(8,128)S(1)}, u32[]{:S(2)}, u32[]{:S(2)}) collective-permute-start(f32[128,128]{1,0:T(8,128)S(1)} %get-tuple-element.67), channel_id=1, source_target_pairs={{1,2},{3,4},{5,6},{7,8},{9,10},{11,12},{13,14},{15,16},{17,18},{19... | collective-permute-start | bytes 196616 | tf_op jit(solution)/shard_map/ppermute | solution.py:40
  51.9 4.7 %collective-permute-start.9 = (f32[128,128]{1,0:T(8,128)S(1)}, f32[128,128]{1,0:T(8,128)S(1)}, u32[]{:S(2)}, u32[]{:S(2)}) collective-permute-start(f32[128,128]{1,0:T(8,128)S(1)} %get-tuple-element.68), channel_id=1, source_target_pairs={{0,1},{2,3},{4,5},{6,7},{8,9},{10,11},{12,13},{14,15},{16,17},{18,... | collective-permute-start | bytes 196616 | tf_op jit(solution)/shard_map/ppermute | solution.py:40
  60.7 8.6 %collective-permute-start.10 = (f32[128,128]{1,0:T(8,128)S(1)}, f32[128,128]{1,0:T(8,128)S(1)}, u32[]{:S(2)}, u32[]{:S(2)}) collective-permute-start(f32[128,128]{1,0:T(8,128)S(1)} %get-tuple-element.74), channel_id=1, source_target_pairs={{1,2},{3,4},{5,6},{7,8},{9,10},{11,12},{13,14},{15,16},{17,18},{19... | collective-permute-start | bytes 196616 | tf_op jit(solution)/shard_map/ppermute | solution.py:40
  64.4 4.9 %collective-permute-start.11 = (f32[128,128]{1,0:T(8,128)S(1)}, f32[128,128]{1,0:T(8,128)S(1)}, u32[]{:S(2)}, u32[]{:S(2)}) collective-permute-start(f32[128,128]{1,0:T(8,128)S(1)} %get-tuple-element.75), channel_id=1, source_target_pairs={{0,1},{2,3},{4,5},{6,7},{8,9},{10,11},{12,13},{14,15},{16,17},{18,... | collective-permute-start | bytes 196616 | tf_op jit(solution)/shard_map/ppermute | solution.py:40
  69.3 29.9 %copy-start.3 = (f32[4096,128]{1,0:T(8,128)S(1)}, f32[4096,128]{1,0:T(8,128)}, u32[]{:S(2)}) copy-start(f32[4096,128]{1,0:T(8,128)} %copy-done.2) | copy-start | bytes 6291460

commit v4 on v3

--- a/solution.py
+++ b/solution.py
@@ -26,6 +26,8 @@
 PAIR = 2
 FRONT = 52
 PRODUCT = (0, 4, 5)
+SENT = (4, 5, 0, 3)
+SPLIT = (1,) + SENT
 F32 = jnp.float32
 
 VMEM = pl.BlockSpec(memory_space=pltpu.VMEM)
@@ -167,10 +169,12 @@
                 place = chunk - 1
                 column = lane + place * LANES
                 own = jnp.where(lane < LANES - own_shift, last, now)
-                low_half = turned_ref[jnp.clip(up_tile + place, 0, 1)]
-                high_half = turned_ref[jnp.clip(up_tile + place + 1, 0, 1)]
-                above = jnp.where(lane < LANES - up_shift, low_half, high_half)
-                value = jnp.where(column < before + stay, own, above)
+                value = own
+                if place >= 2 * MOVE // LANES:
+                    low_half = turned_ref[jnp.clip(up_tile + place, 0, 1)]
+                    high_half = turned_ref[jnp.clip(up_tile + place + 1, 0, 1)]
+                    above = jnp.where(lane < LANES - up_shift, low_half, high_half)
+                    value = jnp.where(column < before + stay, own, above)
                 if place < MOVE // LANES:
                     half = pl.ds(place * BCELLS + start, rows)
                     below = jnp.where(odd, inside_ref[half, :], cross_ref[half, :])
@@ -180,10 +184,6 @@
         return carry
 
     lax.fori_loop(0, BCELLS // rows, body, 0)
-
-
-def diagonal_kernel(counts_ref, before_ref, old_ref, cross_ref, inside_ref, out_ref, turned_ref):
-    assemble(counts_ref, before_ref[0], old_ref, cross_ref, inside_ref, out_ref, turned_ref)
 
 
 def prepare_kernel(
@@ -228,35 +228,32 @@
     out_ref[base + BCELLS : base + 2 * BCELLS, :] = found[:, LANES:]
 
 
-def one_hot(code, out_ref, column):
-    rows = 128
+def one_hot(code, out_ref, row, count, column):
+    rows = 512
     width = code.shape[1]
     base = lax.broadcasted_iota(jnp.int32, (rows, width), 0).astype(jnp.int16)
     one = jnp.ones((rows, width), jnp.bfloat16)
     zero = jnp.zeros((rows, width), jnp.bfloat16)
-
-    def body(step, carry):
-        start = pl.multiple_of(step * rows, rows)
+    for start in range(0, count, rows):
         here = base == jnp.broadcast_to((code - start).astype(jnp.int16), (rows, width))
-        out_ref[pl.ds(start, rows), column : column + width] = jnp.where(here, one, zero)
-        return carry
-
-    lax.fori_loop(0, out_ref.shape[0] // rows, body, 0)
+        out_ref[row + start : row + start + rows, column : column + width] = jnp.where(
+            here, one, zero
+        )
 
 
 def select(odd, codes_ref, send_ref, sent_ref, taken_ref, local_ref):
     low, high = send_ref[0:1, :], send_ref[1:2, :]
-    one_hot(jnp.where(odd == 1, high, low), sent_ref, 0)
-    one_hot(jnp.where(odd == 1, low, high), sent_ref, HMAX)
-    for which in range(6):
-        code = codes_ref[which : which + 1, :]
+    for index, which in enumerate(SENT):
+        for column, code in (
+            (0, jnp.where(odd == 1, high, low)), (HMAX, jnp.where(odd == 1, low, high))
+        ):
+            one_hot(code - which * BDEV, sent_ref, index * BDEV, BDEV, column)
+    for index, which in enumerate(PRODUCT):
         for half in range(2):
-            part = code[:, half * BCELLS : (half + 1) * BCELLS]
-            at = which * BDEV + half * BCELLS
-            one_hot((part - REMOTE) ^ (odd * HMAX), taken_ref, at)
-            if which in PRODUCT:
-                at = PRODUCT.index(which) * BDEV + half * BCELLS
-                one_hot(part - (which ^ 1) * BDEV, local_ref, at)
+            code = codes_ref[which : which + 1, half * BCELLS : (half + 1) * BCELLS]
+            at = index * BDEV + half * BCELLS
+            one_hot((code - REMOTE) ^ (odd * HMAX), taken_ref, 0, 2 * HMAX, at)
+            one_hot(code - (which ^ 1) * BDEV, local_ref, 0, BDEV, at)
 
 
 def halves(value):
@@ -276,19 +273,39 @@
 
 
 def split_layers(field_ref, chunk, layers_ref):
-    for which in range(6):
-        at = (which * CHUNKS + chunk) * LANES
+    for index, which in enumerate(SPLIT):
+        at = (index * CHUNKS + chunk) * LANES
         layers_ref[:, at : at + LANES] = halves(whole_layer(field_ref, which, chunk))
 
 
-def pack(layers_ref, sent_ref, cross_ref, inside_ref):
-    for out_ref, start in ((cross_ref, 0), (inside_ref, HMAX)):
-        found = jnp.dot(
-            layers_ref[...], sent_ref[:, start : start + HMAX], preferred_element_type=F32
+def pack(field_ref, layers_ref, sent_ref, send_ref, odd, cross_ref, inside_ref):
+    low, high = send_ref[0:1, :], send_ref[1:2, :]
+    for out_ref, start, codes in (
+        (cross_ref, 0, jnp.where(odd, high, low)), (inside_ref, HMAX, jnp.where(odd, low, high))
+    ):
+        product = jnp.dot(
+            layers_ref[:, BDEV:], sent_ref[:, start : start + HMAX], preferred_element_type=F32
         )
-        found = found[:FACE, :] + found[FACE:, :]
-        out_ref[0:FACE, :] = found[:, :LANES]
-        out_ref[FACE : 2 * FACE, :] = found[:, LANES:]
+        product = product[:FACE, :] + product[FACE:, :]
+        for step in range(2):
+            code = jnp.broadcast_to(codes[:, step * LANES : (step + 1) * LANES], (SUB, LANES))
+            lane = code & (LANES - 1)
+            tile = code >> 7
+            found = [
+                product[part * SUB : (part + 1) * SUB, step * LANES : (step + 1) * LANES]
+                for part in range(8)
+            ]
+            for which in range(6):
+                if which in SENT:
+                    continue
+                for source in range(CHUNKS):
+                    here = tile == which * CHUNKS + source
+                    for part in range(8):
+                        values = layer_tile(field_ref, which, part, source)
+                        found[part] = jnp.where(here, pick(values, lane), found[part])
+            for part in range(8):
+                row = step * FACE + part * SUB
+                out_ref[row : row + SUB, :] = found[part]
 
 
 def layer_tile(field_ref, which, part, chunk):
@@ -305,7 +322,7 @@
 def gather_layers(step, codes_ref, field_ref, layers_ref, local_ref, faces_ref):
     for index, which in enumerate(PRODUCT):
         at = index * BDEV + step * (2 * LANES)
-        start = (which ^ 1) * BDEV
+        start = SPLIT.index(which ^ 1) * BDEV
         found = jnp.dot(
             layers_ref[:, start : start + BDEV],
             local_ref[:, pl.ds(pl.multiple_of(at, 2 * LANES), 2 * LANES)],
@@ -336,12 +353,21 @@
                 faces_ref[base : base + SUB, :] = found[part]
 
 
-def local_kernel(
-    known, theta_ref, codes_ref, diagonal_ref, field_ref, layers_ref, local_ref, *refs
-):
+def local_kernel(known, theta_ref, codes_ref, field_ref, layers_ref, local_ref, *refs):
     basis = refs[:known]
-    gram_in = refs[known][...] if known > 1 else jnp.zeros((SUB, LANES), F32)
-    out_ref, gram_ref, faces_ref, beside_ref, sums_ref = refs[-5:]
+    faces_ref, beside_ref, sums_ref = refs[-3:]
+    if known > 1:
+        diagonal_ref, gram_in_ref, out_ref, gram_ref = refs[known:-3]
+        gram_in = gram_in_ref[...]
+    else:
+        counts_ref, before_ref, old_ref, cross_ref, inside_ref, out_ref, gram_ref, diagonal_ref = (
+            refs[1:9]
+        )
+        turned_ref = refs[9]
+        gram_in = jnp.zeros((SUB, LANES), F32)
+        assemble(
+            counts_ref, before_ref[0], old_ref, cross_ref, inside_ref, diagonal_ref, turned_ref
+        )
     theta = theta_ref[0]
     sums_ref[...] = jnp.zeros_like(sums_ref)
 
@@ -398,14 +424,33 @@
     return halves(jnp.concatenate(parts, axis=1))
 
 
-def finish(taken_ref, received, out_ref, pair):
+def finish(odd, codes_ref, taken_ref, received, cross_ref, inside_ref, out_ref, pair):
     for which in range(6):
-        at = which * BDEV + pair * 2 * LANES
-        found = jnp.dot(received, taken_ref[:, at : at + 2 * LANES], preferred_element_type=F32)
-        found = found[:FACE, :] + found[FACE:, :]
+        if which in PRODUCT:
+            at = PRODUCT.index(which) * BDEV + pair * 2 * LANES
+            product = jnp.dot(
+                received, taken_ref[:, at : at + 2 * LANES], preferred_element_type=F32
+            )
+            product = product[:FACE, :] + product[FACE:, :]
         for half in range(2):
-            start = (pair * 2 + half) * BCELLS
-            beside = found[:, half * LANES : (half + 1) * LANES]
+            chunk = pair * 2 + half
+            start = chunk * BCELLS
+            if which in PRODUCT:
+                beside = product[:, half * LANES : (half + 1) * LANES]
+            else:
+                code = codes_ref[which : which + 1, chunk * LANES : (chunk + 1) * LANES] - REMOTE
+                code = jnp.broadcast_to(code, (SUB, LANES))
+                lane = code & (LANES - 1)
+                tile = (code >> 7) ^ (odd * 2)
+                found = [jnp.zeros((SUB, LANES), F32) for _ in range(8)]
+                for source in range(2 * HMAX // LANES):
+                    here = tile == source
+                    from_ref = cross_ref if source < HMAX // LANES else inside_ref
+                    base = source % (HMAX // LANES) * FACE
+                    for part in range(8):
+                        values = from_ref[base + part * SUB : base + (part + 1) * SUB, :]
+                        found[part] = jnp.where(here, pick(values, lane), found[part])
+                beside = jnp.concatenate(found, axis=0)
             if which >= 4:
                 rows = pl.ds(start + (which - 4) * (BE - 1), FACE, stride=BE)
                 out_ref[rows, :] = out_ref[rows, :] - beside
@@ -429,17 +474,20 @@
         gram_out_ref[start : start + SUB, :] = row
 
 
-def send(split_ref, value_ref, field_ref, layers_ref, sent_ref, cross_ref, inside_ref, before):
+def send(
+    split_ref, value_ref, field_ref, layers_ref, sent_ref, send_ref, odd, cross_ref, inside_ref,
+    before,
+):
     for pair in range(CHUNKS // 2):
         before(pair)
         precondition(split_ref, value_ref, field_ref, pair)
         split_layers(field_ref, 2 * pair, layers_ref)
         split_layers(field_ref, 2 * pair + 1, layers_ref)
-    pack(layers_ref, sent_ref, cross_ref, inside_ref)
+    pack(field_ref, layers_ref, sent_ref, send_ref, odd, cross_ref, inside_ref)
 
 
 def first_kernel(
-    counts_ref, old_ref, cross_ref, inside_ref, split_ref, sent_ref,
+    counts_ref, old_ref, cross_ref, inside_ref, split_ref, sent_ref, send_ref,
     before_ref, rhs_ref, field_ref, layers_ref, to_cross_ref, to_inside_ref,
     turned_ref,
 ):
@@ -448,46 +496,48 @@
     before_ref[0] = before
     assemble(counts_ref, before, old_ref, cross_ref, inside_ref, rhs_ref, turned_ref)
     send(
-        split_ref, rhs_ref, field_ref, layers_ref, sent_ref, to_cross_ref, to_inside_ref,
-        lambda pair: None,
+        split_ref, rhs_ref, field_ref, layers_ref, sent_ref, send_ref, odd, to_cross_ref,
+        to_inside_ref, lambda pair: None,
     )
 
 
 def next_kernel(
-    cross_ref, inside_ref, partial_ref, taken_ref, split_ref, sent_ref,
+    rank_ref, codes_ref, send_ref, cross_ref, inside_ref, partial_ref, taken_ref, split_ref,
+    sent_ref,
     out_ref, field_ref, layers_ref, to_cross_ref, to_inside_ref,
 ):
     del partial_ref
+    odd = rank_ref[0] & 1
     received = receive(cross_ref, inside_ref)
+
+    def before(pair):
+        finish(odd, codes_ref, taken_ref, received, cross_ref, inside_ref, out_ref, pair)
+
     send(
-        split_ref, out_ref, field_ref, layers_ref, sent_ref, to_cross_ref, to_inside_ref,
-        lambda pair: finish(taken_ref, received, out_ref, pair),
-    )
-
-
-def end_kernel(cross_ref, inside_ref, partial_ref, taken_ref, gram_in_ref, *refs):
+        split_ref, out_ref, field_ref, layers_ref, sent_ref, send_ref, odd == 1, to_cross_ref,
+        to_inside_ref, before,
+    )
+
+
+def end_kernel(
+    rank_ref, codes_ref, cross_ref, inside_ref, partial_ref, taken_ref, gram_in_ref, *refs
+):
     del partial_ref
     basis = refs[: BASIS - 1]
     out_ref, gram_ref, sums_ref = refs[BASIS - 1 :]
+    odd = rank_ref[0] & 1
     received = receive(cross_ref, inside_ref)
+    sums = [jnp.zeros((SUB, LANES), F32) for _ in range(BASIS)]
     for pair in range(CHUNKS // 2):
-        finish(taken_ref, received, out_ref, pair)
-    sums_ref[...] = jnp.zeros_like(sums_ref)
-
-    def body(step, carry):
-        start = pl.multiple_of(step * BCELLS, BCELLS)
-        sums = [jnp.zeros((SUB, LANES), F32) for _ in range(BASIS)]
-        for row in range(0, BCELLS, SUB):
-            rows = pl.ds(start + row, SUB)
+        finish(odd, codes_ref, taken_ref, received, cross_ref, inside_ref, out_ref, pair)
+        for row in range(pair * 2 * BCELLS, (pair + 1) * 2 * BCELLS, SUB):
+            rows = slice(row, row + SUB)
             value = out_ref[rows, :]
             for k, ref in enumerate(basis):
                 sums[k] = sums[k] + value * ref[rows, :]
             sums[-1] = sums[-1] + value * value
-        for k, part in enumerate(sums):
-            sums_ref[k] += part
-        return carry
-
-    lax.fori_loop(0, CHUNKS, body, 0)
+    for k, part in enumerate(sums):
+        sums_ref[k] = part
     place_sums(sums_ref, BASIS, gram_in_ref[...], gram_ref, BASIS * (BASIS - 1) // 2)
 
 
@@ -596,7 +646,7 @@
     split_type = jax.ShapeDtypeStruct((BCELLS, 3 * BCELLS), jnp.bfloat16)
     turned = pltpu.VMEM((2, 64, LANES), F32)
     layers = [pltpu.VMEM((PAIR * 6 * FACE, LANES), F32), pltpu.VMEM((PAIR * BCELLS, LANES), F32)]
-    packed_type = jax.ShapeDtypeStruct((2 * FACE, 6 * BDEV), jnp.bfloat16)
+    packed_type = jax.ShapeDtypeStruct((2 * FACE, len(SPLIT) * BDEV), jnp.bfloat16)
     sums = pltpu.VMEM((BASIS, SUB, LANES), F32)
 
     rank = lax.axis_index(AXES).astype(jnp.int32).reshape(1)
@@ -633,8 +683,8 @@
         (
             split_type,
             jax.ShapeDtypeStruct((1,), F32),
-            jax.ShapeDtypeStruct((6 * BDEV, 2 * HMAX), jnp.bfloat16),
-            jax.ShapeDtypeStruct((2 * HMAX, 6 * BDEV), jnp.bfloat16),
+            jax.ShapeDtypeStruct((len(SENT) * BDEV, 2 * HMAX), jnp.bfloat16),
+            jax.ShapeDtypeStruct((2 * HMAX, len(PRODUCT) * BDEV), jnp.bfloat16),
             jax.ShapeDtypeStruct((BDEV, len(PRODUCT) * BDEV), jnp.bfloat16),
         ),
         (rank, block_inverse, face_source, send_layers),
@@ -645,8 +695,8 @@
         first_kernel,
         (jax.ShapeDtypeStruct((1,), jnp.int32),)
         + (field_type, field_type, packed_type, halo_type, halo_type),
-        (counts, rhs_old, rhs_cross, rhs_inside, split, sent),
-        [VMEM] * 6,
+        (counts, rhs_old, rhs_cross, rhs_inside, split, sent, send_layers),
+        [VMEM] * 7,
         (SMEM,) + (VMEM,) * 5,
         [turned],
         flops=10**9,
@@ -658,50 +708,57 @@
     for known in range(1, BASIS):
         from_cross = swapped(to_cross, True)
         from_inside = swapped(to_inside, False)
-        if diagonal is None:
-            diagonal = call(
-                diagonal_kernel,
-                field_type,
-                (counts, before, diagonal_old, diagonal_cross, diagonal_inside),
-                [VMEM, SMEM] + [VMEM] * 3,
-                VMEM,
-                [turned],
-                bytes_accessed=6 * MIB,
-            )
-        args = [theta, face_source, diagonal, field, packed, local] + basis + ([gram] if known > 1 else [])
-        partial, gram = call(
+        args = [theta, face_source, field, packed, local] + basis
+        outs = [field_type, of(SUB)]
+        specs = [SMEM] + [VMEM] * (len(args) - 1)
+        if known > 1:
+            args += [diagonal, gram]
+            specs += [VMEM, VMEM]
+            scratch = layers + [sums]
+        else:
+            args += [counts, before, diagonal_old, diagonal_cross, diagonal_inside]
+            specs += [VMEM, SMEM] + [VMEM] * 3
+            outs.append(field_type)
+            scratch = [turned] + layers + [sums]
+        found = call(
             functools.partial(local_kernel, known),
-            (field_type, of(SUB)),
+            tuple(outs),
             tuple(args),
-            [SMEM] + [VMEM] * (len(args) - 1),
-            (VMEM, VMEM),
-            layers + [sums],
+            specs,
+            (VMEM,) * len(outs),
+            scratch,
             flops=10**9,
             bytes_accessed=4 * MIB,
         )
+        partial, gram = found[:2]
+        if known == 1:
+            diagonal = found[2]
         if known < BASIS - 1:
             value, field, packed, to_cross, to_inside = call(
                 next_kernel,
                 (field_type, field_type, packed_type, halo_type, halo_type),
-                (from_cross, from_inside, partial, taken, split, sent),
-                [VMEM] * 6,
+                (
+                    rank, face_source, send_layers, from_cross, from_inside, partial, taken,
+                    split, sent,
+                ),
+                [SMEM] + [VMEM] * 8,
                 (VMEM,) * 5,
                 flops=10**9,
                 bytes_accessed=12 * MIB,
-                aliases={2: 0},
+                aliases={5: 0},
             )
             fields.append(field)
         else:
             value, copies = call(
                 end_kernel,
                 (field_type, of(lax.axis_size(AXES))),
-                (from_cross, from_inside, partial, taken, gram, *basis),
-                [VMEM] * (5 + len(basis)),
+                (rank, face_source, from_cross, from_inside, partial, taken, gram, *basis),
+                [SMEM] + [VMEM] * (6 + len(basis)),
                 (VMEM, VMEM),
                 [sums],
                 flops=10**9,
                 bytes_accessed=12 * MIB,
-                aliases={2: 0},
+                aliases={4: 0},
             )
         basis.append(value)
     gathered = lax.all_to_all(copies, AXES, split_axis=0, concat_axis=0, tiled=True)

time: 104 us -> 103 us (level)
  Pallas kernels: 50.4 us -> 48.3 us
  starting transfers between devices: 23.3 us -> 24.6 us
    pallas_call x14 -> x13, Pallas kernels: 50.4 us -> 48.3 us  [call(): pl.pallas_call(kernel, out_shape=outs, in_specs=in_specs, out_specs=out_s...]
    ppermute x12, starting transfers between devices: 23.3 us -> 24.6 us  [swapped(): lax.ppermute(value, AXES, pairs + [(high, low) for low, high in pairs])]
  transfers between devices with their start and end apart: 12 -> 12, of which waited for: 0 -> 0; matrix products, arithmetic and copies ran while one was open for 0% -> 0% of each run, Pallas kernels for 29% -> 27%
where the time goes in v4:
time: 103 us; the launch traced here: 102 us
  Pallas kernels  48.3 us (47%)
  blocking collectives  27.4 us (27%)
  starting transfers between devices  24.6 us (24%)
  between operations  1.19 us (1%)
    pallas_call x13, Pallas kernels, call(): pl.pallas_call(kernel, out_shape=outs, in_specs=in_specs, out_specs=out_s...  48.3 us
    all_to_all x1, blocking collectives, per_device(): lax.all_to_all(copies, AXES, split_axis=0, concat_axis=0, tiled=True)  27.4 us
    ppermute x12, starting transfers between devices, swapped(): lax.ppermute(value, AXES, pairs + [(high, low) for low, high in pairs])  24.6 us
  transfers between devices with their start and end apart: 12, of which 0 were waited for; matrix products, arithmetic and copies ran while one was open for 0% of the time, Pallas kernels for 27%

profile of v4, /device:TPU:1, one launch (start us, length us, event | category | flops | bytes accessed | tf_op | source)
XLA Modules:
  0.0 102.4 jit_solution(4680958703361882080)
XLA Ops:
  0.7 0.8 copy-done.7
  1.5 2.1 %shard_map.78 = (s32[8,128]{1,0:T(8,128)S(1)}, f32[1032,128]{1,0:T(8,128)S(1)}, f32[1032,128]{1,0:T(8,128)S(1)}) custom-call(s32[1]{0:T(128)} %bitcast.rank_ref, s32[12,128]{1,0:T(8,128)S(1)} %bitcast.8, f32[512,1536]{1,0:T(8,128)} %old_ref.4), custom_call_target="tpu_custom_call" | custom-call | tf_op jit(solution)/shard_map/pallas_call | solution.py:48
  3.6 0.0 copy-start.4
  3.6 0.0 copy-start.5
  3.6 0.0 copy-start.6
  3.6 4.6 %collective-permute-start = (f32[1032,128]{1,0:T(8,128)S(1)}, f32[1032,128]{1,0:T(8,128)S(1)}, u32[]{:S(2)}, u32[]{:S(2)}) collective-permute-start(f32[1032,128]{1,0:T(8,128)S(1)} %get-tuple-element.46), channel_id=1, source_target_pairs={{1,2},{3,4},{5,6},{7,8},{9,10},{11,12},{13,14},{15,16},{17,18},{19... | collective-permute-start | bytes 1585160 | tf_op jit(solution)/shard_map/ppermute | solution.py:42
  8.2 0.1 collective-permute-start.1
  8.4 0.0 copy-start.1
  8.4 0.5 shard_map.80
  8.8 3.6 %collective-permute-start.4 = (f32[1024,128]{1,0:T(8,128)S(1)}, f32[1024,128]{1,0:T(8,128)S(1)}, u32[]{:S(2)}, u32[]{:S(2)}) collective-permute-start(f32[1024,128]{1,0:T(8,128)S(1)} %get-tuple-element.57), channel_id=1, source_target_pairs={{1,2},{3,4},{5,6},{7,8},{9,10},{11,12},{13,14},{15,16},{17,18},{19... | collective-permute-start | bytes 1572872 | tf_op jit(solution)/shard_map/ppermute | solution.py:42
  12.5 0.1 collective-permute-start.5
  12.6 2.8 %shard_map.77 = (bf16[512,1536]{1,0:T(8,128)(2,1)S(1)}, f32[1]{0:T(128)}, bf16[4096,512]{1,0:T(8,128)(2,1)S(1)}, bf16[512,3072]{1,0:T(8,128)(2,1)S(1)}, bf16[1024,3072]{1,0:T(8,128)(2,1)S(1)}) custom-call(s32[1]{0:T(128)} %bitcast.rank_ref, f32[512,512]{1,0:T(8,128)S(1)} %copy-done.5, s32[6,1024]{1,0:T(8,128)S(1)} %copy-done.4, s32[2,256]{1,0:T(2,128)S(1)} %copy-done.6), custom_call_target="tpu_custom_call" | custom-call | tf_op jit(solution)/shard_map/pallas_call | solution.py:48
  15.4 4.6 %shard_map.79 = (s32[1]{0:T(128)}, f32[4096,128]{1,0:T(8,128)S(1)}, f32[4096,128]{1,0:T(8,128)S(1)}, bf16[128,5120]{1,0:T(8,128)(2,1)S(1)}, f32[128,128]{1,0:T(8,128)S(1)}, /*index=5*/f32[128,128]{1,0:T(8,128)S(1)}) custom-call(s32[8,128]{1,0:T(8,128)S(1)} %get-tuple-element.45.counts_ref.refs_1_, f32[512,1536]{1,0:T(8,128)S(1)} %copy-done.1, ...), custom_call_target="tpu_custom_call" | custom-call | flops 1000000000 | bytes 8388608 | tf_op jit(solution)/shard_map/pallas_call | solution.py:48
  20.1 0.0 copy-start.2
  20.1 3.4 %collective-permute-start.2 = (f32[128,128]{1,0:T(8,128)S(1)}, f32[128,128]{1,0:T(8,128)S(1)}, u32[]{:S(2)}, u32[]{:S(2)}) collective-permute-start(f32[128,128]{1,0:T(8,128)S(1)} %get-tuple-element.50), channel_id=1, source_target_pairs={{1,2},{3,4},{5,6},{7,8},{9,10},{11,12},{13,14},{15,16},{17,18},{19... | collective-permute-start | bytes 196616 | tf_op jit(solution)/shard_map/ppermute | solution.py:42
  23.4 0.1 collective-permute-start.3
  23.6 6.3 %shard_map.81 = (f32[4096,128]{1,0:T(8,128)S(1)}, f32[8,128]{1,0:T(8,128)S(1)}, f32[4096,128]{1,0:T(8,128)S(1)}) custom-call(f32[1]{0:T(128)} %get-tuple-element.44.theta_ref, s32[6,1024]{1,0:T(8,128)S(1)} %copy-done.4, f32[4096,128]{1,0:T(8,128)S(1)} %get-tuple-element.52.field_ref.refs_5_, bf16[128,5120]{1,0:T(8,128)(2,1)S(1)} %get-tuple-element.53.layers_ref, ...), custom_call_target="tpu_custom_call" | custom-call | flops 1000000000 | bytes 4194304 | tf_op jit(solution)/shard_map/pallas_call | solution.py:48
  29.9 4.1 %shard_map.82 = (f32[4096,128]{1,0:T(8,128)S(1)}, f32[4096,128]{1,0:T(8,128)S(1)}, bf16[128,5120]{1,0:T(8,128)(2,1)S(1)}, f32[128,128]{1,0:T(8,128)S(1)}, f32[128,128]{1,0:T(8,128)S(1)}) custom-call(s32[1]{0:T(128)} %bitcast.rank_ref, s32[6,1024]{1,0:T(8,128)S(1)} %copy-done.4, s32[2,256]{1,0:T(2,128)S(1)} %copy-done.6, ...), custom_call_target="tpu_custom_call", output_to_operand_aliasing={{0}: (5, {})} | custom-call | flops 1000000000 | bytes 12582912 | tf_op jit(solution)/shard_map/pallas_call | solution.py:48
  34.0 3.5 %collective-permute-start.6 = (f32[128,128]{1,0:T(8,128)S(1)}, f32[128,128]{1,0:T(8,128)S(1)}, u32[]{:S(2)}, u32[]{:S(2)}) collective-permute-start(f32[128,128]{1,0:T(8,128)S(1)} %get-tuple-element.61), channel_id=1, source_target_pairs={{1,2},{3,4},{5,6},{7,8},{9,10},{11,12},{13,14},{15,16},{17,18},{19... | collective-permute-start | bytes 196616 | tf_op jit(solution)/shard_map/ppermute | solution.py:42
  37.5 0.3 collective-permute-start.7
  37.8 4.5 %shard_map.83 = (f32[4096,128]{1,0:T(8,128)S(1)}, f32[8,128]{1,0:T(8,128)S(1)}) custom-call(f32[1]{0:T(128)} %get-tuple-element.44.theta_ref, s32[6,1024]{1,0:T(8,128)S(1)} %copy-done.4, f32[4096,128]{1,0:T(8,128)S(1)} %get-tuple-element.63.field_ref.refs_6_, bf16[128,5120]{1,0:T(8,128)(2,1)S(1)} %get-tuple-element.64.layers_ref, ...), custom_call_target="tpu_custom_call" | custom-call | flops 1000000000 | bytes 4194304 | tf_op jit(solution)/shard_map/pallas_call | solution.py:48
  42.3 4.1 %shard_map.84 = (f32[4096,128]{1,0:T(8,128)S(1)}, f32[4096,128]{1,0:T(8,128)S(1)}, bf16[128,5120]{1,0:T(8,128)(2,1)S(1)}, f32[128,128]{1,0:T(8,128)S(1)}, f32[128,128]{1,0:T(8,128)S(1)}) custom-call(s32[1]{0:T(128)} %bitcast.rank_ref, s32[6,1024]{1,0:T(8,128)S(1)} %copy-done.4, s32[2,256]{1,0:T(2,128)S(1)} %copy-done.6, ...), custom_call_target="tpu_custom_call", output_to_operand_aliasing={{0}: (5, {})} | custom-call | flops 1000000000 | bytes 12582912 | tf_op jit(solution)/shard_map/pallas_call | solution.py:48
  46.5 3.8 %collective-permute-start.8 = (f32[128,128]{1,0:T(8,128)S(1)}, f32[128,128]{1,0:T(8,128)S(1)}, u32[]{:S(2)}, u32[]{:S(2)}) collective-permute-start(f32[128,128]{1,0:T(8,128)S(1)} %get-tuple-element.69), channel_id=1, source_target_pairs={{1,2},{3,4},{5,6},{7,8},{9,10},{11,12},{13,14},{15,16},{17,18},{19... | collective-permute-start | bytes 196616 | tf_op jit(solution)/shard_map/ppermute | solution.py:42
  50.3 0.1 collective-permute-start.9
  50.4 4.6 %shard_map.85 = (f32[4096,128]{1,0:T(8,128)S(1)}, f32[8,128]{1,0:T(8,128)S(1)}) custom-call(f32[1]{0:T(128)} %get-tuple-element.44.theta_ref, s32[6,1024]{1,0:T(8,128)S(1)} %copy-done.4, f32[4096,128]{1,0:T(8,128)S(1)} %get-tuple-element.71.field_ref.refs_7_, bf16[128,5120]{1,0:T(8,128)(2,1)S(1)} %get-tuple-element.72.layers_ref, ...), custom_call_target="tpu_custom_call" | custom-call | flops 1000000000 | bytes 4194304 | tf_op jit(solution)/shard_map/pallas_call | solution.py:48
  55.0 4.1 %shard_map.86 = (f32[4096,128]{1,0:T(8,128)S(1)}, f32[4096,128]{1,0:T(8,128)S(1)}, bf16[128,5120]{1,0:T(8,128)(2,1)S(1)}, f32[128,128]{1,0:T(8,128)S(1)}, f32[128,128]{1,0:T(8,128)S(1)}) custom-call(s32[1]{0:T(128)} %bitcast.rank_ref, s32[6,1024]{1,0:T(8,128)S(1)} %copy-done.4, s32[2,256]{1,0:T(2,128)S(1)} %copy-done.6, ...), custom_call_target="tpu_custom_call", output_to_operand_aliasing={{0}: (5, {})} | custom-call | flops 1000000000 | bytes 12582912 | tf_op jit(solution)/shard_map/pallas_call | solution.py:48
  59.2 5.0 %collective-permute-start.10 = (f32[128,128]{1,0:T(8,128)S(1)}, f32[128,128]{1,0:T(8,128)S(1)}, u32[]{:S(2)}, u32[]{:S(2)}) collective-permute-start(f32[128,128]{1,0:T(8,128)S(1)} %get-tuple-element.76), channel_id=1, source_target_pairs={{1,2},{3,4},{5,6},{7,8},{9,10},{11,12},{13,14},{15,16},{17,18},{19... | collective-permute-start | bytes 196616 | tf_op jit(solution)/shard_map/ppermute | solution.py:42
  64.2 0.1 collective-permute-start.11
  64.3 4.7 %shard_map.87 = (f32[4096,128]{1,0:T(8,128)S(1)}, f32[8,128]{1,0:T(8,128)S(1)}) custom-call(f32[1]{0:T(128)} %get-tuple-element.44.theta_ref, s32[6,1024]{1,0:T(8,128)S(1)} %copy-done.4, f32[4096,128]{1,0:T(8,128)S(1)} %get-tuple-element.78.field_ref.refs_8_, bf16[128,5120]{1,0:T(8,128)(2,1)S(1)} %get-tuple-element.79.layers_ref, ...), custom_call_target="tpu_custom_call" | custom-call | flops 1000000000 | bytes 4194304 | tf_op jit(solution)/shard_map/pallas_call | solution.py:48
  69.0 2.0 %shard_map.88 = (f32[4096,128]{1,0:T(8,128)S(1)}, f32[128,128]{1,0:T(8,128)S(1)}) custom-call(s32[1]{0:T(128)} %bitcast.rank_ref, s32[6,1024]{1,0:T(8,128)S(1)} %copy-done.4, f32[128,128]{1,0:T(8,128)S(1)} %collective-permute-done.10.cross_ref, f32[128,128]{1,0:T(8,128)S(1)} %collective-permute-done.11.inside_ref, ...), custom_call_target="tpu_custom_call", output_to_operand_aliasing={{0}: (4, {})} | custom-call | flops 1000000000 | bytes 12582912 | tf_op jit(solution)/shard_map/pallas_call | solution.py:48
  71.0 27.4 %all_to_all.11 = f32[128,1,128]{2,1,0:T(1,128)S(1)} all-to-all(f32[128,1,128]{2,1,0:T(1,128)S(1)} %bitcast.7), channel_id=1, replica_groups=mesh['gx'=4,'gy'=4,'gz'=8] {'gx','gy','gz'}, dimensions={0} | all-to-all | bytes 131072 | tf_op jit(solution)/shard_map/all_to_all | solution.py:764
  98.4 3.8 %shard_map.89 = (f32[512,1024]{1,0:T(8,128)}, f32[512,1024]{1,0:T(8,128)}) custom-call(f32[1]{0:T(128)} %get-tuple-element.44.theta_ref, f32[128,128]{1,0:T(8,128)S(1)} %bitcast.6, f32[4096,128]{1,0:T(8,128)S(1)} %get-tuple-element.55.refs_0_, f32[4096,128]{1,0:T(8,128)S(1)} %get-tuple-element.65.refs_1_, f32[4096,128]{1,0:T(8,128)S(1)} %get-tuple-element.73.refs_2_, ...), custom_call_target="tpu_custom_call" | custom-call | tf_op jit(solution)/shard_map/pallas_call | solution.py:48
  (22 shorter events, 0.1 us)
Async XLA Ops:
  0.6 7.7 %copy-start = (f32[512,1536]{1,0:T(8,128)S(1)}, f32[512,1536]{1,0:T(8,128)}, u32[]{:S(2)}) copy-start(f32[512,1536]{1,0:T(8,128)} %refs_3_.1) | copy-start | bytes 9437188
  0.6 0.8 copy-start.7
  3.6 9.0 %copy-start.4 = (s32[6,1024]{1,0:T(8,128)S(1)}, s32[6,1024]{1,0:T(8,128)}, u32[]{:S(2)}) copy-start(s32[6,1024]{1,0:T(8,128)} %codes_ref.17) | copy-start | bytes 73732
  3.6 9.0 %copy-start.5 = (f32[512,512]{1,0:T(8,128)S(1)}, f32[512,512]{1,0:T(8,128)}, u32[]{:S(2)}) copy-start(f32[512,512]{1,0:T(8,128)} %inverse_ref.1) | copy-start | bytes 3145732
  3.6 9.0 %copy-start.6 = (s32[2,256]{1,0:T(2,128)S(1)}, s32[2,256]{1,0:T(2,128)}, u32[]{:S(2)}) copy-start(s32[2,256]{1,0:T(2,128)} %send_ref.9) | copy-start | bytes 6148
  3.6 11.8 %collective-permute-start = (f32[1032,128]{1,0:T(8,128)S(1)}, f32[1032,128]{1,0:T(8,128)S(1)}, u32[]{:S(2)}, u32[]{:S(2)}) collective-permute-start(f32[1032,128]{1,0:T(8,128)S(1)} %get-tuple-element.46), channel_id=1, source_target_pairs={{1,2},{3,4},{5,6},{7,8},{9,10},{11,12},{13,14},{15,16},{17,18},{19... | collective-permute-start | bytes 1585160 | tf_op jit(solution)/shard_map/ppermute | solution.py:42
  8.2 7.2 %collective-permute-start.1 = (f32[1032,128]{1,0:T(8,128)S(1)}, f32[1032,128]{1,0:T(8,128)S(1)}, u32[]{:S(2)}, u32[]{:S(2)}) collective-permute-start(f32[1032,128]{1,0:T(8,128)S(1)} %get-tuple-element.47), channel_id=1, source_target_pairs={{0,1},{2,3},{4,5},{6,7},{8,9},{10,11},{12,13},{14,15},{16,17},{18,... | collective-permute-start | bytes 1585160 | tf_op jit(solution)/shard_map/ppermute | solution.py:42
  8.4 7.1 %copy-start.1 = (f32[512,1536]{1,0:T(8,128)S(1)}, f32[512,1536]{1,0:T(8,128)}, u32[]{:S(2)}) copy-start(f32[512,1536]{1,0:T(8,128)} %old_ref.4) | copy-start | bytes 9437188
  8.8 14.7 %collective-permute-start.4 = (f32[1024,128]{1,0:T(8,128)S(1)}, f32[1024,128]{1,0:T(8,128)S(1)}, u32[]{:S(2)}, u32[]{:S(2)}) collective-permute-start(f32[1024,128]{1,0:T(8,128)S(1)} %get-tuple-element.57), channel_id=1, source_target_pairs={{1,2},{3,4},{5,6},{7,8},{9,10},{11,12},{13,14},{15,16},{17,18},{19... | collective-permute-start | bytes 1572872 | tf_op jit(solution)/shard_map/ppermute | solution.py:42
  12.5 11.1 %collective-permute-start.5 = (f32[1024,128]{1,0:T(8,128)S(1)}, f32[1024,128]{1,0:T(8,128)S(1)}, u32[]{:S(2)}, u32[]{:S(2)}) collective-permute-start(f32[1024,128]{1,0:T(8,128)S(1)} %get-tuple-element.58), channel_id=1, source_target_pairs={{0,1},{2,3},{4,5},{6,7},{8,9},{10,11},{12,13},{14,15},{16,17},{18,... | collective-permute-start | bytes 1572872 | tf_op jit(solution)/shard_map/ppermute | solution.py:42
  20.1 9.8 %copy-start.2 = (f32[4096,128]{1,0:T(8,128)}, f32[4096,128]{1,0:T(8,128)S(1)}, u32[]{:S(2)}) copy-start(f32[4096,128]{1,0:T(8,128)S(1)} %get-tuple-element.52.field_ref.refs_5_) | copy-start | bytes 6291460
  20.1 9.8 %collective-permute-start.2 = (f32[128,128]{1,0:T(8,128)S(1)}, f32[128,128]{1,0:T(8,128)S(1)}, u32[]{:S(2)}, u32[]{:S(2)}) collective-permute-start(f32[128,128]{1,0:T(8,128)S(1)} %get-tuple-element.50), channel_id=1, source_target_pairs={{1,2},{3,4},{5,6},{7,8},{9,10},{11,12},{13,14},{15,16},{17,18},{19... | collective-permute-start | bytes 196616 | tf_op jit(solution)/shard_map/ppermute | solution.py:42
  23.4 6.5 %collective-permute-start.3 = (f32[128,128]{1,0:T(8,128)S(1)}, f32[128,128]{1,0:T(8,128)S(1)}, u32[]{:S(2)}, u32[]{:S(2)}) collective-permute-start(f32[128,128]{1,0:T(8,128)S(1)} %get-tuple-element.51), channel_id=1, source_target_pairs={{0,1},{2,3},{4,5},{6,7},{8,9},{10,11},{12,13},{14,15},{16,17},{18,... | collective-permute-start | bytes 196616 | tf_op jit(solution)/shard_map/ppermute | solution.py:42
  34.0 8.3 %collective-permute-start.6 = (f32[128,128]{1,0:T(8,128)S(1)}, f32[128,128]{1,0:T(8,128)S(1)}, u32[]{:S(2)}, u32[]{:S(2)}) collective-permute-start(f32[128,128]{1,0:T(8,128)S(1)} %get-tuple-element.61), channel_id=1, source_target_pairs={{1,2},{3,4},{5,6},{7,8},{9,10},{11,12},{13,14},{15,16},{17,18},{19... | collective-permute-start | bytes 196616 | tf_op jit(solution)/shard_map/ppermute | solution.py:42
  37.5 4.8 %collective-permute-start.7 = (f32[128,128]{1,0:T(8,128)S(1)}, f32[128,128]{1,0:T(8,128)S(1)}, u32[]{:S(2)}, u32[]{:S(2)}) collective-permute-start(f32[128,128]{1,0:T(8,128)S(1)} %get-tuple-element.62), channel_id=1, source_target_pairs={{0,1},{2,3},{4,5},{6,7},{8,9},{10,11},{12,13},{14,15},{16,17},{18,... | collective-permute-start | bytes 196616 | tf_op jit(solution)/shard_map/ppermute | solution.py:42
  46.5 8.6 %collective-permute-start.8 = (f32[128,128]{1,0:T(8,128)S(1)}, f32[128,128]{1,0:T(8,128)S(1)}, u32[]{:S(2)}, u32[]{:S(2)}) collective-permute-start(f32[128,128]{1,0:T(8,128)S(1)} %get-tuple-element.69), channel_id=1, source_target_pairs={{1,2},{3,4},{5,6},{7,8},{9,10},{11,12},{13,14},{15,16},{17,18},{19... | collective-permute-start | bytes 196616 | tf_op jit(solution)/shard_map/ppermute | solution.py:42
  50.3 4.7 %collective-permute-start.9 = (f32[128,128]{1,0:T(8,128)S(1)}, f32[128,128]{1,0:T(8,128)S(1)}, u32[]{:S(2)}, u32[]{:S(2)}) collective-permute-start(f32[128,128]{1,0:T(8,128)S(1)} %get-tuple-element.70), channel_id=1, source_target_pairs={{0,1},{2,3},{4,5},{6,7},{8,9},{10,11},{12,13},{14,15},{16,17},{18,... | collective-permute-start | bytes 196616 | tf_op jit(solution)/shard_map/ppermute | solution.py:42
  59.2 9.8 %collective-permute-start.10 = (f32[128,128]{1,0:T(8,128)S(1)}, f32[128,128]{1,0:T(8,128)S(1)}, u32[]{:S(2)}, u32[]{:S(2)}) collective-permute-start(f32[128,128]{1,0:T(8,128)S(1)} %get-tuple-element.76), channel_id=1, source_target_pairs={{1,2},{3,4},{5,6},{7,8},{9,10},{11,12},{13,14},{15,16},{17,18},{19... | collective-permute-start | bytes 196616 | tf_op jit(solution)/shard_map/ppermute | solution.py:42
  64.2 4.8 %collective-permute-start.11 = (f32[128,128]{1,0:T(8,128)S(1)}, f32[128,128]{1,0:T(8,128)S(1)}, u32[]{:S(2)}, u32[]{:S(2)}) collective-permute-start(f32[128,128]{1,0:T(8,128)S(1)} %get-tuple-element.77), channel_id=1, source_target_pairs={{0,1},{2,3},{4,5},{6,7},{8,9},{10,11},{12,13},{14,15},{16,17},{18,... | collective-permute-start | bytes 196616 | tf_op jit(solution)/shard_map/ppermute | solution.py:42
  69.0 29.3 %copy-start.3 = (f32[4096,128]{1,0:T(8,128)S(1)}, f32[4096,128]{1,0:T(8,128)}, u32[]{:S(2)}) copy-start(f32[4096,128]{1,0:T(8,128)} %copy-done.2) | copy-start | bytes 6291460

commit v5 on v4

--- a/solution.py
+++ b/solution.py
@@ -147,18 +147,17 @@
     up_tile = up_start >> 7
     up_shift = up_start & (LANES - 1)
     rows = 64
-
-    def body(step, carry):
-        start = pl.multiple_of(step * rows, rows)
-        at = pl.ds(start, rows)
-        lane = lane_iota(rows)
+    lane = lane_iota(rows)
+    for start in range(0, BCELLS, rows):
         for part in range(2):
-            half = pl.ds(part * BCELLS + start, rows)
-            turned_ref[part] = pltpu.roll(
+            half = slice(part * BCELLS + start, part * BCELLS + start + rows)
+            turned_ref[part, start : start + rows, :] = pltpu.roll(
                 jnp.where(odd, cross_ref[half, :], inside_ref[half, :]),
                 (LANES - up_shift) & (LANES - 1),
                 1,
             )
+    for start in range(0, BCELLS, rows):
+        at = slice(start, start + rows)
         last = None
         for chunk in range(CHUNKS + 1):
             source = jnp.clip(own_tile + chunk, 0, CAP // LANES - 1) * LANES
@@ -168,22 +167,18 @@
             if chunk > 0:
                 place = chunk - 1
                 column = lane + place * LANES
-                own = jnp.where(lane < LANES - own_shift, last, now)
-                value = own
+                value = jnp.where(lane < LANES - own_shift, last, now)
                 if place >= 2 * MOVE // LANES:
-                    low_half = turned_ref[jnp.clip(up_tile + place, 0, 1)]
-                    high_half = turned_ref[jnp.clip(up_tile + place + 1, 0, 1)]
+                    low_half = turned_ref[jnp.clip(up_tile + place, 0, 1), at, :]
+                    high_half = turned_ref[jnp.clip(up_tile + place + 1, 0, 1), at, :]
                     above = jnp.where(lane < LANES - up_shift, low_half, high_half)
-                    value = jnp.where(column < before + stay, own, above)
+                    value = jnp.where(column < before + stay, value, above)
                 if place < MOVE // LANES:
-                    half = pl.ds(place * BCELLS + start, rows)
+                    half = slice(place * BCELLS + start, place * BCELLS + start + rows)
                     below = jnp.where(odd, inside_ref[half, :], cross_ref[half, :])
                     value = jnp.where(column < before, below, value)
-                out_ref[pl.ds(place * BCELLS + start, rows), :] = value
+                out_ref[place * BCELLS + start : place * BCELLS + start + rows, :] = value
             last = now
-        return carry
-
-    lax.fori_loop(0, BCELLS // rows, body, 0)
 
 
 def prepare_kernel(
@@ -644,7 +639,7 @@
     out_type = jax.ShapeDtypeStruct((BCELLS, BDEV), F32)
     halo_type = of(2 * FACE)
     split_type = jax.ShapeDtypeStruct((BCELLS, 3 * BCELLS), jnp.bfloat16)
-    turned = pltpu.VMEM((2, 64, LANES), F32)
+    turned = pltpu.VMEM((2, BCELLS, LANES), F32)
     layers = [pltpu.VMEM((PAIR * 6 * FACE, LANES), F32), pltpu.VMEM((PAIR * BCELLS, LANES), F32)]
     packed_type = jax.ShapeDtypeStruct((2 * FACE, len(SPLIT) * BDEV), jnp.bfloat16)
     sums = pltpu.VMEM((BASIS, SUB, LANES), F32)

time: 103 us -> 101 us (0.981)
  Pallas kernels: 48.3 us -> 46.8 us
    pallas_call x13, Pallas kernels: 48.3 us -> 46.8 us  [call(): pl.pallas_call(kernel, out_shape=outs, in_specs=in_specs, out_specs=out_s...]
  transfers between devices with their start and end apart: 12 -> 12, of which waited for: 0 -> 0; matrix products, arithmetic and copies ran while one was open for 0% -> 0% of each run, Pallas kernels for 27% -> 26%
where the time goes in v5:
time: 101 us
  Pallas kernels  46.8 us (46%)
  blocking collectives  27.3 us (27%)
  starting transfers between devices  24.8 us (25%)
  between operations  1.21 us (1%)
    pallas_call x13, Pallas kernels, call(): pl.pallas_call(kernel, out_shape=outs, in_specs=in_specs, out_specs=out_s...  46.8 us
    all_to_all x1, blocking collectives, per_device(): lax.all_to_all(copies, AXES, split_axis=0, concat_axis=0, tiled=True)  27.3 us
    ppermute x12, starting transfers between devices, swapped(): lax.ppermute(value, AXES, pairs + [(high, low) for low, high in pairs])  24.8 us
  transfers between devices with their start and end apart: 12, of which 0 were waited for; matrix products, arithmetic and copies ran while one was open for 0% of the time, Pallas kernels for 26%

profile of v5, /device:TPU:1, one launch (start us, length us, event | category | flops | bytes accessed | tf_op | source)
XLA Modules:
  0.0 101.1 jit_solution(2888615657301521687)
XLA Ops:
  0.7 0.8 copy-done.7
  1.5 2.1 %shard_map.78 = (s32[8,128]{1,0:T(8,128)S(1)}, f32[1032,128]{1,0:T(8,128)S(1)}, f32[1032,128]{1,0:T(8,128)S(1)}) custom-call(s32[1]{0:T(128)} %bitcast.rank_ref, s32[12,128]{1,0:T(8,128)S(1)} %bitcast.8, f32[512,1536]{1,0:T(8,128)} %old_ref.4), custom_call_target="tpu_custom_call" | custom-call | tf_op jit(solution)/shard_map/pallas_call | solution.py:48
  3.6 0.0 copy-start.4
  3.6 0.0 copy-start.5
  3.6 0.0 copy-start.6
  3.6 4.6 %collective-permute-start = (f32[1032,128]{1,0:T(8,128)S(1)}, f32[1032,128]{1,0:T(8,128)S(1)}, u32[]{:S(2)}, u32[]{:S(2)}) collective-permute-start(f32[1032,128]{1,0:T(8,128)S(1)} %get-tuple-element.46), channel_id=1, source_target_pairs={{1,2},{3,4},{5,6},{7,8},{9,10},{11,12},{13,14},{15,16},{17,18},{19... | collective-permute-start | bytes 1585160 | tf_op jit(solution)/shard_map/ppermute | solution.py:42
  8.2 0.1 collective-permute-start.1
  8.4 0.0 copy-start.1
  8.4 0.5 shard_map.80
  8.8 3.6 %collective-permute-start.4 = (f32[1024,128]{1,0:T(8,128)S(1)}, f32[1024,128]{1,0:T(8,128)S(1)}, u32[]{:S(2)}, u32[]{:S(2)}) collective-permute-start(f32[1024,128]{1,0:T(8,128)S(1)} %get-tuple-element.57), channel_id=1, source_target_pairs={{1,2},{3,4},{5,6},{7,8},{9,10},{11,12},{13,14},{15,16},{17,18},{19... | collective-permute-start | bytes 1572872 | tf_op jit(solution)/shard_map/ppermute | solution.py:42
  12.5 0.1 collective-permute-start.5
  12.6 2.8 %shard_map.77 = (bf16[512,1536]{1,0:T(8,128)(2,1)S(1)}, f32[1]{0:T(128)}, bf16[4096,512]{1,0:T(8,128)(2,1)S(1)}, bf16[512,3072]{1,0:T(8,128)(2,1)S(1)}, bf16[1024,3072]{1,0:T(8,128)(2,1)S(1)}) custom-call(s32[1]{0:T(128)} %bitcast.rank_ref, f32[512,512]{1,0:T(8,128)S(1)} %copy-done.5, s32[6,1024]{1,0:T(8,128)S(1)} %copy-done.4, s32[2,256]{1,0:T(2,128)S(1)} %copy-done.6), custom_call_target="tpu_custom_call" | custom-call | tf_op jit(solution)/shard_map/pallas_call | solution.py:48
  15.4 3.6 %shard_map.79 = (s32[1]{0:T(128)}, f32[4096,128]{1,0:T(8,128)S(1)}, f32[4096,128]{1,0:T(8,128)S(1)}, bf16[128,5120]{1,0:T(8,128)(2,1)S(1)}, f32[128,128]{1,0:T(8,128)S(1)}, /*index=5*/f32[128,128]{1,0:T(8,128)S(1)}) custom-call(s32[8,128]{1,0:T(8,128)S(1)} %get-tuple-element.45.counts_ref.refs_1_, f32[512,1536]{1,0:T(8,128)S(1)} %copy-done.1, ...), custom_call_target="tpu_custom_call" | custom-call | flops 1000000000 | bytes 8388608 | tf_op jit(solution)/shard_map/pallas_call | solution.py:48
  19.0 0.0 copy-start.2
  19.1 3.4 %collective-permute-start.2 = (f32[128,128]{1,0:T(8,128)S(1)}, f32[128,128]{1,0:T(8,128)S(1)}, u32[]{:S(2)}, u32[]{:S(2)}) collective-permute-start(f32[128,128]{1,0:T(8,128)S(1)} %get-tuple-element.50), channel_id=1, source_target_pairs={{1,2},{3,4},{5,6},{7,8},{9,10},{11,12},{13,14},{15,16},{17,18},{19... | collective-permute-start | bytes 196616 | tf_op jit(solution)/shard_map/ppermute | solution.py:42
  22.4 0.3 collective-permute-start.3
  22.7 5.9 %shard_map.81 = (f32[4096,128]{1,0:T(8,128)S(1)}, f32[8,128]{1,0:T(8,128)S(1)}, f32[4096,128]{1,0:T(8,128)S(1)}) custom-call(f32[1]{0:T(128)} %get-tuple-element.44.theta_ref, s32[6,1024]{1,0:T(8,128)S(1)} %copy-done.4, f32[4096,128]{1,0:T(8,128)S(1)} %get-tuple-element.52.field_ref.refs_5_, bf16[128,5120]{1,0:T(8,128)(2,1)S(1)} %get-tuple-element.53.layers_ref, ...), custom_call_target="tpu_custom_call" | custom-call | flops 1000000000 | bytes 4194304 | tf_op jit(solution)/shard_map/pallas_call | solution.py:48
  28.6 4.1 %shard_map.82 = (f32[4096,128]{1,0:T(8,128)S(1)}, f32[4096,128]{1,0:T(8,128)S(1)}, bf16[128,5120]{1,0:T(8,128)(2,1)S(1)}, f32[128,128]{1,0:T(8,128)S(1)}, f32[128,128]{1,0:T(8,128)S(1)}) custom-call(s32[1]{0:T(128)} %bitcast.rank_ref, s32[6,1024]{1,0:T(8,128)S(1)} %copy-done.4, s32[2,256]{1,0:T(2,128)S(1)} %copy-done.6, ...), custom_call_target="tpu_custom_call", output_to_operand_aliasing={{0}: (5, {})} | custom-call | flops 1000000000 | bytes 12582912 | tf_op jit(solution)/shard_map/pallas_call | solution.py:48
  32.7 3.5 %collective-permute-start.6 = (f32[128,128]{1,0:T(8,128)S(1)}, f32[128,128]{1,0:T(8,128)S(1)}, u32[]{:S(2)}, u32[]{:S(2)}) collective-permute-start(f32[128,128]{1,0:T(8,128)S(1)} %get-tuple-element.61), channel_id=1, source_target_pairs={{1,2},{3,4},{5,6},{7,8},{9,10},{11,12},{13,14},{15,16},{17,18},{19... | collective-permute-start | bytes 196616 | tf_op jit(solution)/shard_map/ppermute | solution.py:42
  36.2 0.1 collective-permute-start.7
  36.3 4.5 %shard_map.83 = (f32[4096,128]{1,0:T(8,128)S(1)}, f32[8,128]{1,0:T(8,128)S(1)}) custom-call(f32[1]{0:T(128)} %get-tuple-element.44.theta_ref, s32[6,1024]{1,0:T(8,128)S(1)} %copy-done.4, f32[4096,128]{1,0:T(8,128)S(1)} %get-tuple-element.63.field_ref.refs_6_, bf16[128,5120]{1,0:T(8,128)(2,1)S(1)} %get-tuple-element.64.layers_ref, ...), custom_call_target="tpu_custom_call" | custom-call | flops 1000000000 | bytes 4194304 | tf_op jit(solution)/shard_map/pallas_call | solution.py:48
  40.8 4.1 %shard_map.84 = (f32[4096,128]{1,0:T(8,128)S(1)}, f32[4096,128]{1,0:T(8,128)S(1)}, bf16[128,5120]{1,0:T(8,128)(2,1)S(1)}, f32[128,128]{1,0:T(8,128)S(1)}, f32[128,128]{1,0:T(8,128)S(1)}) custom-call(s32[1]{0:T(128)} %bitcast.rank_ref, s32[6,1024]{1,0:T(8,128)S(1)} %copy-done.4, s32[2,256]{1,0:T(2,128)S(1)} %copy-done.6, ...), custom_call_target="tpu_custom_call", output_to_operand_aliasing={{0}: (5, {})} | custom-call | flops 1000000000 | bytes 12582912 | tf_op jit(solution)/shard_map/pallas_call | solution.py:48
  45.0 3.8 %collective-permute-start.8 = (f32[128,128]{1,0:T(8,128)S(1)}, f32[128,128]{1,0:T(8,128)S(1)}, u32[]{:S(2)}, u32[]{:S(2)}) collective-permute-start(f32[128,128]{1,0:T(8,128)S(1)} %get-tuple-element.69), channel_id=1, source_target_pairs={{1,2},{3,4},{5,6},{7,8},{9,10},{11,12},{13,14},{15,16},{17,18},{19... | collective-permute-start | bytes 196616 | tf_op jit(solution)/shard_map/ppermute | solution.py:42
  48.8 0.3 collective-permute-start.9
  49.1 4.6 %shard_map.85 = (f32[4096,128]{1,0:T(8,128)S(1)}, f32[8,128]{1,0:T(8,128)S(1)}) custom-call(f32[1]{0:T(128)} %get-tuple-element.44.theta_ref, s32[6,1024]{1,0:T(8,128)S(1)} %copy-done.4, f32[4096,128]{1,0:T(8,128)S(1)} %get-tuple-element.71.field_ref.refs_7_, bf16[128,5120]{1,0:T(8,128)(2,1)S(1)} %get-tuple-element.72.layers_ref, ...), custom_call_target="tpu_custom_call" | custom-call | flops 1000000000 | bytes 4194304 | tf_op jit(solution)/shard_map/pallas_call | solution.py:48
  53.8 4.1 %shard_map.86 = (f32[4096,128]{1,0:T(8,128)S(1)}, f32[4096,128]{1,0:T(8,128)S(1)}, bf16[128,5120]{1,0:T(8,128)(2,1)S(1)}, f32[128,128]{1,0:T(8,128)S(1)}, f32[128,128]{1,0:T(8,128)S(1)}) custom-call(s32[1]{0:T(128)} %bitcast.rank_ref, s32[6,1024]{1,0:T(8,128)S(1)} %copy-done.4, s32[2,256]{1,0:T(2,128)S(1)} %copy-done.6, ...), custom_call_target="tpu_custom_call", output_to_operand_aliasing={{0}: (5, {})} | custom-call | flops 1000000000 | bytes 12582912 | tf_op jit(solution)/shard_map/pallas_call | solution.py:48
  57.9 5.0 %collective-permute-start.10 = (f32[128,128]{1,0:T(8,128)S(1)}, f32[128,128]{1,0:T(8,128)S(1)}, u32[]{:S(2)}, u32[]{:S(2)}) collective-permute-start(f32[128,128]{1,0:T(8,128)S(1)} %get-tuple-element.76), channel_id=1, source_target_pairs={{1,2},{3,4},{5,6},{7,8},{9,10},{11,12},{13,14},{15,16},{17,18},{19... | collective-permute-start | bytes 196616 | tf_op jit(solution)/shard_map/ppermute | solution.py:42
  62.9 0.1 collective-permute-start.11
  63.0 4.7 %shard_map.87 = (f32[4096,128]{1,0:T(8,128)S(1)}, f32[8,128]{1,0:T(8,128)S(1)}) custom-call(f32[1]{0:T(128)} %get-tuple-element.44.theta_ref, s32[6,1024]{1,0:T(8,128)S(1)} %copy-done.4, f32[4096,128]{1,0:T(8,128)S(1)} %get-tuple-element.78.field_ref.refs_8_, bf16[128,5120]{1,0:T(8,128)(2,1)S(1)} %get-tuple-element.79.layers_ref, ...), custom_call_target="tpu_custom_call" | custom-call | flops 1000000000 | bytes 4194304 | tf_op jit(solution)/shard_map/pallas_call | solution.py:48
  67.8 2.0 %shard_map.88 = (f32[4096,128]{1,0:T(8,128)S(1)}, f32[128,128]{1,0:T(8,128)S(1)}) custom-call(s32[1]{0:T(128)} %bitcast.rank_ref, s32[6,1024]{1,0:T(8,128)S(1)} %copy-done.4, f32[128,128]{1,0:T(8,128)S(1)} %collective-permute-done.10.cross_ref, f32[128,128]{1,0:T(8,128)S(1)} %collective-permute-done.11.inside_ref, ...), custom_call_target="tpu_custom_call", output_to_operand_aliasing={{0}: (4, {})} | custom-call | flops 1000000000 | bytes 12582912 | tf_op jit(solution)/shard_map/pallas_call | solution.py:48
  69.8 27.3 %all_to_all.11 = f32[128,1,128]{2,1,0:T(1,128)S(1)} all-to-all(f32[128,1,128]{2,1,0:T(1,128)S(1)} %bitcast.7), channel_id=1, replica_groups=mesh['gx'=4,'gy'=4,'gz'=8] {'gx','gy','gz'}, dimensions={0} | all-to-all | bytes 131072 | tf_op jit(solution)/shard_map/all_to_all | solution.py:759
  97.1 3.8 %shard_map.89 = (f32[512,1024]{1,0:T(8,128)}, f32[512,1024]{1,0:T(8,128)}) custom-call(f32[1]{0:T(128)} %get-tuple-element.44.theta_ref, f32[128,128]{1,0:T(8,128)S(1)} %bitcast.6, f32[4096,128]{1,0:T(8,128)S(1)} %get-tuple-element.55.refs_0_, f32[4096,128]{1,0:T(8,128)S(1)} %get-tuple-element.65.refs_1_, f32[4096,128]{1,0:T(8,128)S(1)} %get-tuple-element.73.refs_2_, ...), custom_call_target="tpu_custom_call" | custom-call | tf_op jit(solution)/shard_map/pallas_call | solution.py:48
  (22 shorter events, 0.1 us)
Async XLA Ops:
  0.6 7.7 %copy-start = (f32[512,1536]{1,0:T(8,128)S(1)}, f32[512,1536]{1,0:T(8,128)}, u32[]{:S(2)}) copy-start(f32[512,1536]{1,0:T(8,128)} %refs_3_.1) | copy-start | bytes 9437188
  0.6 0.8 copy-start.7
  3.6 9.0 %copy-start.4 = (s32[6,1024]{1,0:T(8,128)S(1)}, s32[6,1024]{1,0:T(8,128)}, u32[]{:S(2)}) copy-start(s32[6,1024]{1,0:T(8,128)} %codes_ref.17) | copy-start | bytes 73732
  3.6 9.0 %copy-start.5 = (f32[512,512]{1,0:T(8,128)S(1)}, f32[512,512]{1,0:T(8,128)}, u32[]{:S(2)}) copy-start(f32[512,512]{1,0:T(8,128)} %inverse_ref.1) | copy-start | bytes 3145732
  3.6 9.0 %copy-start.6 = (s32[2,256]{1,0:T(2,128)S(1)}, s32[2,256]{1,0:T(2,128)}, u32[]{:S(2)}) copy-start(s32[2,256]{1,0:T(2,128)} %send_ref.9) | copy-start | bytes 6148
  3.6 11.8 %collective-permute-start = (f32[1032,128]{1,0:T(8,128)S(1)}, f32[1032,128]{1,0:T(8,128)S(1)}, u32[]{:S(2)}, u32[]{:S(2)}) collective-permute-start(f32[1032,128]{1,0:T(8,128)S(1)} %get-tuple-element.46), channel_id=1, source_target_pairs={{1,2},{3,4},{5,6},{7,8},{9,10},{11,12},{13,14},{15,16},{17,18},{19... | collective-permute-start | bytes 1585160 | tf_op jit(solution)/shard_map/ppermute | solution.py:42
  8.2 7.2 %collective-permute-start.1 = (f32[1032,128]{1,0:T(8,128)S(1)}, f32[1032,128]{1,0:T(8,128)S(1)}, u32[]{:S(2)}, u32[]{:S(2)}) collective-permute-start(f32[1032,128]{1,0:T(8,128)S(1)} %get-tuple-element.47), channel_id=1, source_target_pairs={{0,1},{2,3},{4,5},{6,7},{8,9},{10,11},{12,13},{14,15},{16,17},{18,... | collective-permute-start | bytes 1585160 | tf_op jit(solution)/shard_map/ppermute | solution.py:42
  8.4 7.1 %copy-start.1 = (f32[512,1536]{1,0:T(8,128)S(1)}, f32[512,1536]{1,0:T(8,128)}, u32[]{:S(2)}) copy-start(f32[512,1536]{1,0:T(8,128)} %old_ref.4) | copy-start | bytes 9437188
  8.8 13.8 %collective-permute-start.4 = (f32[1024,128]{1,0:T(8,128)S(1)}, f32[1024,128]{1,0:T(8,128)S(1)}, u32[]{:S(2)}, u32[]{:S(2)}) collective-permute-start(f32[1024,128]{1,0:T(8,128)S(1)} %get-tuple-element.57), channel_id=1, source_target_pairs={{1,2},{3,4},{5,6},{7,8},{9,10},{11,12},{13,14},{15,16},{17,18},{19... | collective-permute-start | bytes 1572872 | tf_op jit(solution)/shard_map/ppermute | solution.py:42
  12.5 10.2 %collective-permute-start.5 = (f32[1024,128]{1,0:T(8,128)S(1)}, f32[1024,128]{1,0:T(8,128)S(1)}, u32[]{:S(2)}, u32[]{:S(2)}) collective-permute-start(f32[1024,128]{1,0:T(8,128)S(1)} %get-tuple-element.58), channel_id=1, source_target_pairs={{0,1},{2,3},{4,5},{6,7},{8,9},{10,11},{12,13},{14,15},{16,17},{18,... | collective-permute-start | bytes 1572872 | tf_op jit(solution)/shard_map/ppermute | solution.py:42
  19.0 9.5 %copy-start.2 = (f32[4096,128]{1,0:T(8,128)}, f32[4096,128]{1,0:T(8,128)S(1)}, u32[]{:S(2)}) copy-start(f32[4096,128]{1,0:T(8,128)S(1)} %get-tuple-element.52.field_ref.refs_5_) | copy-start | bytes 6291460
  19.1 9.5 %collective-permute-start.2 = (f32[128,128]{1,0:T(8,128)S(1)}, f32[128,128]{1,0:T(8,128)S(1)}, u32[]{:S(2)}, u32[]{:S(2)}) collective-permute-start(f32[128,128]{1,0:T(8,128)S(1)} %get-tuple-element.50), channel_id=1, source_target_pairs={{1,2},{3,4},{5,6},{7,8},{9,10},{11,12},{13,14},{15,16},{17,18},{19... | collective-permute-start | bytes 196616 | tf_op jit(solution)/shard_map/ppermute | solution.py:42
  22.4 6.2 %collective-permute-start.3 = (f32[128,128]{1,0:T(8,128)S(1)}, f32[128,128]{1,0:T(8,128)S(1)}, u32[]{:S(2)}, u32[]{:S(2)}) collective-permute-start(f32[128,128]{1,0:T(8,128)S(1)} %get-tuple-element.51), channel_id=1, source_target_pairs={{0,1},{2,3},{4,5},{6,7},{8,9},{10,11},{12,13},{14,15},{16,17},{18,... | collective-permute-start | bytes 196616 | tf_op jit(solution)/shard_map/ppermute | solution.py:42
  32.7 8.1 %collective-permute-start.6 = (f32[128,128]{1,0:T(8,128)S(1)}, f32[128,128]{1,0:T(8,128)S(1)}, u32[]{:S(2)}, u32[]{:S(2)}) collective-permute-start(f32[128,128]{1,0:T(8,128)S(1)} %get-tuple-element.61), channel_id=1, source_target_pairs={{1,2},{3,4},{5,6},{7,8},{9,10},{11,12},{13,14},{15,16},{17,18},{19... | collective-permute-start | bytes 196616 | tf_op jit(solution)/shard_map/ppermute | solution.py:42
  36.2 4.6 %collective-permute-start.7 = (f32[128,128]{1,0:T(8,128)S(1)}, f32[128,128]{1,0:T(8,128)S(1)}, u32[]{:S(2)}, u32[]{:S(2)}) collective-permute-start(f32[128,128]{1,0:T(8,128)S(1)} %get-tuple-element.62), channel_id=1, source_target_pairs={{0,1},{2,3},{4,5},{6,7},{8,9},{10,11},{12,13},{14,15},{16,17},{18,... | collective-permute-start | bytes 196616 | tf_op jit(solution)/shard_map/ppermute | solution.py:42
  45.0 8.8 %collective-permute-start.8 = (f32[128,128]{1,0:T(8,128)S(1)}, f32[128,128]{1,0:T(8,128)S(1)}, u32[]{:S(2)}, u32[]{:S(2)}) collective-permute-start(f32[128,128]{1,0:T(8,128)S(1)} %get-tuple-element.69), channel_id=1, source_target_pairs={{1,2},{3,4},{5,6},{7,8},{9,10},{11,12},{13,14},{15,16},{17,18},{19... | collective-permute-start | bytes 196616 | tf_op jit(solution)/shard_map/ppermute | solution.py:42
  48.8 5.0 %collective-permute-start.9 = (f32[128,128]{1,0:T(8,128)S(1)}, f32[128,128]{1,0:T(8,128)S(1)}, u32[]{:S(2)}, u32[]{:S(2)}) collective-permute-start(f32[128,128]{1,0:T(8,128)S(1)} %get-tuple-element.70), channel_id=1, source_target_pairs={{0,1},{2,3},{4,5},{6,7},{8,9},{10,11},{12,13},{14,15},{16,17},{18,... | collective-permute-start | bytes 196616 | tf_op jit(solution)/shard_map/ppermute | solution.py:42
  57.9 9.8 %collective-permute-start.10 = (f32[128,128]{1,0:T(8,128)S(1)}, f32[128,128]{1,0:T(8,128)S(1)}, u32[]{:S(2)}, u32[]{:S(2)}) collective-permute-start(f32[128,128]{1,0:T(8,128)S(1)} %get-tuple-element.76), channel_id=1, source_target_pairs={{1,2},{3,4},{5,6},{7,8},{9,10},{11,12},{13,14},{15,16},{17,18},{19... | collective-permute-start | bytes 196616 | tf_op jit(solution)/shard_map/ppermute | solution.py:42
  62.9 4.8 %collective-permute-start.11 = (f32[128,128]{1,0:T(8,128)S(1)}, f32[128,128]{1,0:T(8,128)S(1)}, u32[]{:S(2)}, u32[]{:S(2)}) collective-permute-start(f32[128,128]{1,0:T(8,128)S(1)} %get-tuple-element.77), channel_id=1, source_target_pairs={{0,1},{2,3},{4,5},{6,7},{8,9},{10,11},{12,13},{14,15},{16,17},{18,... | collective-permute-start | bytes 196616 | tf_op jit(solution)/shard_map/ppermute | solution.py:42
  67.8 29.3 %copy-start.3 = (f32[4096,128]{1,0:T(8,128)S(1)}, f32[4096,128]{1,0:T(8,128)}, u32[]{:S(2)}) copy-start(f32[4096,128]{1,0:T(8,128)} %copy-done.2) | copy-start | bytes 6291460

commit v6 on v5

--- a/solution.py
+++ b/solution.py
@@ -23,7 +23,6 @@
 BASIS = 2 * ITERS + 1
 MIB = 1024 * 1024
 PARTS = 8
-PAIR = 2
 FRONT = 52
 PRODUCT = (0, 4, 5)
 SENT = (4, 5, 0, 3)
@@ -309,26 +308,26 @@
     return field_ref[row : row + SUB, :]
 
 
-def layer(faces_ref, half, which, part):
-    base = (half * 6 + which) * FACE + part * SUB
+def layer(faces_ref, chunk, which, part):
+    base = (chunk * 6 + which) * FACE + part * SUB
     return faces_ref[base : base + SUB, :]
 
 
-def gather_layers(step, codes_ref, field_ref, layers_ref, local_ref, faces_ref):
+def gather_layers(pair, codes_ref, field_ref, layers_ref, local_ref, faces_ref):
     for index, which in enumerate(PRODUCT):
-        at = index * BDEV + step * (2 * LANES)
+        at = index * BDEV + pair * (2 * LANES)
         start = SPLIT.index(which ^ 1) * BDEV
         found = jnp.dot(
             layers_ref[:, start : start + BDEV],
-            local_ref[:, pl.ds(pl.multiple_of(at, 2 * LANES), 2 * LANES)],
+            local_ref[:, at : at + 2 * LANES],
             preferred_element_type=F32,
         )
         found = found[:FACE, :] + found[FACE:, :]
-        for half in range(PAIR):
-            base = (half * 6 + which) * FACE
+        for half in range(2):
+            base = ((2 * pair + half) * 6 + which) * FACE
             faces_ref[base : base + FACE, :] = found[:, half * LANES : (half + 1) * LANES]
-    for half in range(PAIR):
-        at = lanes((step * PAIR + half) * LANES)
+    for chunk in (2 * pair, 2 * pair + 1):
+        at = slice(chunk * LANES, (chunk + 1) * LANES)
         for which in range(6):
             if which in PRODUCT:
                 continue
@@ -344,7 +343,7 @@
                     values = layer_tile(field_ref, partner, part, source)
                     found[part] = jnp.where(here, pick(values, lane), found[part])
             for part in range(8):
-                base = (half * 6 + which) * FACE + part * SUB
+                base = (chunk * 6 + which) * FACE + part * SUB
                 faces_ref[base : base + SUB, :] = found[part]
 
 
@@ -364,49 +363,48 @@
             counts_ref, before_ref[0], old_ref, cross_ref, inside_ref, diagonal_ref, turned_ref
         )
     theta = theta_ref[0]
-    sums_ref[...] = jnp.zeros_like(sums_ref)
-
-    def body(step, carry):
-        gather_layers(step, codes_ref, field_ref, layers_ref, local_ref, faces_ref)
-        sums = [jnp.zeros((SUB, LANES), F32) for _ in range(known)]
-        for half in range(PAIR):
-            start = pl.multiple_of((step * PAIR + half) * BCELLS, BCELLS)
-
-            def block(i, j):
-                return field_ref[pl.ds(start + (i * BE + j) * BE, SUB), :]
-
-            for i in range(BE):
-                row = [layer(faces_ref, half, 4, i)]
-                row += [field_ref[pl.ds(start + i * FACE + k, SUB, stride=BE), :] for k in range(BE)]
-                row += [layer(faces_ref, half, 5, i)]
-                for k in range(BE):
-                    at = pl.ds(half * BCELLS + i * FACE + k, SUB, stride=BE)
-                    beside_ref[at, :] = row[k] + row[k + 2]
-            for i in range(BE):
-                for j in range(BE):
-                    row = (i * BE + j) * BE
-                    rows = pl.ds(start + row, SUB)
-                    here = block(i, j)
-                    beside = beside_ref[half * BCELLS + row : half * BCELLS + row + SUB, :]
-                    beside = beside + (block(i - 1, j) if i > 0 else layer(faces_ref, half, 0, j))
-                    beside = beside + (
-                        block(i + 1, j) if i < BE - 1 else layer(faces_ref, half, 1, j)
-                    )
-                    beside = beside + (block(i, j - 1) if j > 0 else layer(faces_ref, half, 2, i))
-                    beside = beside + (
-                        block(i, j + 1) if j < BE - 1 else layer(faces_ref, half, 3, i)
-                    )
-                    newest = basis[-1][rows, :]
-                    value = (6.0 + diagonal_ref[rows, :]) * here - beside
-                    out_ref[rows, :] = value - theta * newest
-                    for k, ref in enumerate(basis):
-                        old = newest if k == known - 1 else ref[rows, :]
-                        sums[k] = sums[k] + newest * old
-        for k, part in enumerate(sums):
-            sums_ref[k] += part
-        return carry
-
-    lax.fori_loop(0, CHUNKS // PAIR, body, 0)
+    sums = [jnp.zeros((SUB, LANES), F32) for _ in range(known)]
+
+    def stencil(chunk):
+        start = chunk * BCELLS
+
+        def block(i, j):
+            row = start + (i * BE + j) * BE
+            return field_ref[row : row + SUB, :]
+
+        for i in range(BE):
+            row = [layer(faces_ref, chunk, 4, i)]
+            row += [field_ref[pl.ds(start + i * FACE + k, SUB, stride=BE), :] for k in range(BE)]
+            row += [layer(faces_ref, chunk, 5, i)]
+            for k in range(BE):
+                beside_ref[pl.ds(start + i * FACE + k, SUB, stride=BE), :] = row[k] + row[k + 2]
+        for i in range(BE):
+            for j in range(BE):
+                rows = slice(start + (i * BE + j) * BE, start + (i * BE + j + 1) * BE)
+                beside = beside_ref[rows, :]
+                beside = beside + (block(i - 1, j) if i > 0 else layer(faces_ref, chunk, 0, j))
+                beside = beside + (
+                    block(i + 1, j) if i < BE - 1 else layer(faces_ref, chunk, 1, j)
+                )
+                beside = beside + (block(i, j - 1) if j > 0 else layer(faces_ref, chunk, 2, i))
+                beside = beside + (
+                    block(i, j + 1) if j < BE - 1 else layer(faces_ref, chunk, 3, i)
+                )
+                newest = basis[-1][rows, :]
+                value = (6.0 + diagonal_ref[rows, :]) * block(i, j) - beside
+                out_ref[rows, :] = value - theta * newest
+                for k, ref in enumerate(basis):
+                    old = newest if k == known - 1 else ref[rows, :]
+                    sums[k] = sums[k] + newest * old
+
+    gather_layers(0, codes_ref, field_ref, layers_ref, local_ref, faces_ref)
+    for pair in range(CHUNKS // 2):
+        if pair + 1 < CHUNKS // 2:
+            gather_layers(pair + 1, codes_ref, field_ref, layers_ref, local_ref, faces_ref)
+        stencil(2 * pair)
+        stencil(2 * pair + 1)
+    for k, part in enumerate(sums):
+        sums_ref[k] = part
     place_sums(sums_ref, known, gram_in, gram_ref, (known - 1) * known // 2)
 
 
@@ -640,7 +638,10 @@
     halo_type = of(2 * FACE)
     split_type = jax.ShapeDtypeStruct((BCELLS, 3 * BCELLS), jnp.bfloat16)
     turned = pltpu.VMEM((2, BCELLS, LANES), F32)
-    layers = [pltpu.VMEM((PAIR * 6 * FACE, LANES), F32), pltpu.VMEM((PAIR * BCELLS, LANES), F32)]
+    layers = [
+        pltpu.VMEM((CHUNKS * 6 * FACE, LANES), F32),
+        pltpu.VMEM((CHUNKS * BCELLS, LANES), F32),
+    ]
     packed_type = jax.ShapeDtypeStruct((2 * FACE, len(SPLIT) * BDEV), jnp.bfloat16)
     sums = pltpu.VMEM((BASIS, SUB, LANES), F32)
 

time: 101 us -> 101 us (level)
  Pallas kernels: 46.8 us -> 45.5 us
    pallas_call x13, Pallas kernels: 46.8 us -> 45.5 us  [call(): pl.pallas_call(kernel, out_shape=outs, in_specs=in_specs, out_specs=out_s...]
  transfers between devices with their start and end apart: 12 -> 12, of which waited for: 0 -> 0; matrix products, arithmetic and copies ran while one was open for 0% -> 0% of each run, Pallas kernels for 26% -> 25%
where the time goes in v6:
time: 101 us; the launch traced here: 100 us
  Pallas kernels  45.5 us (45%)
  blocking collectives  27.5 us (27%)
  starting transfers between devices  25.1 us (25%)
  between operations  1.2 us (1%)
    pallas_call x13, Pallas kernels, call(): pl.pallas_call(kernel, out_shape=outs, in_specs=in_specs, out_specs=out_s...  45.5 us
    all_to_all x1, blocking collectives, per_device(): lax.all_to_all(copies, AXES, split_axis=0, concat_axis=0, tiled=True)  27.5 us
    ppermute x12, starting transfers between devices, swapped(): lax.ppermute(value, AXES, pairs + [(high, low) for low, high in pairs])  25.1 us
  transfers between devices with their start and end apart: 12, of which 0 were waited for; matrix products, arithmetic and copies ran while one was open for 0% of the time, Pallas kernels for 25%

profile of v6, /device:TPU:1, one launch (start us, length us, event | category | flops | bytes accessed | tf_op | source)
XLA Modules:
  0.0 100.3 jit_solution(11144024359919631978)
XLA Ops:
  0.7 0.8 copy-done.7
  1.5 2.1 %shard_map.78 = (s32[8,128]{1,0:T(8,128)S(1)}, f32[1032,128]{1,0:T(8,128)S(1)}, f32[1032,128]{1,0:T(8,128)S(1)}) custom-call(s32[1]{0:T(128)} %bitcast.rank_ref, s32[12,128]{1,0:T(8,128)S(1)} %bitcast.8, f32[512,1536]{1,0:T(8,128)} %old_ref.4), custom_call_target="tpu_custom_call" | custom-call | tf_op jit(solution)/shard_map/pallas_call | solution.py:47
  3.6 0.0 copy-start.4
  3.6 0.0 copy-start.5
  3.6 0.0 copy-start.6
  3.6 4.6 %collective-permute-start = (f32[1032,128]{1,0:T(8,128)S(1)}, f32[1032,128]{1,0:T(8,128)S(1)}, u32[]{:S(2)}, u32[]{:S(2)}) collective-permute-start(f32[1032,128]{1,0:T(8,128)S(1)} %get-tuple-element.46), channel_id=1, source_target_pairs={{1,2},{3,4},{5,6},{7,8},{9,10},{11,12},{13,14},{15,16},{17,18},{19... | collective-permute-start | bytes 1585160 | tf_op jit(solution)/shard_map/ppermute | solution.py:41
  8.2 0.1 collective-permute-start.1
  8.4 0.0 copy-start.1
  8.4 0.5 shard_map.80
  8.8 3.6 %collective-permute-start.4 = (f32[1024,128]{1,0:T(8,128)S(1)}, f32[1024,128]{1,0:T(8,128)S(1)}, u32[]{:S(2)}, u32[]{:S(2)}) collective-permute-start(f32[1024,128]{1,0:T(8,128)S(1)} %get-tuple-element.57), channel_id=1, source_target_pairs={{1,2},{3,4},{5,6},{7,8},{9,10},{11,12},{13,14},{15,16},{17,18},{19... | collective-permute-start | bytes 1572872 | tf_op jit(solution)/shard_map/ppermute | solution.py:41
  12.5 0.1 collective-permute-start.5
  12.6 2.8 %shard_map.77 = (bf16[512,1536]{1,0:T(8,128)(2,1)S(1)}, f32[1]{0:T(128)}, bf16[4096,512]{1,0:T(8,128)(2,1)S(1)}, bf16[512,3072]{1,0:T(8,128)(2,1)S(1)}, bf16[1024,3072]{1,0:T(8,128)(2,1)S(1)}) custom-call(s32[1]{0:T(128)} %bitcast.rank_ref, f32[512,512]{1,0:T(8,128)S(1)} %copy-done.5, s32[6,1024]{1,0:T(8,128)S(1)} %copy-done.4, s32[2,256]{1,0:T(2,128)S(1)} %copy-done.6), custom_call_target="tpu_custom_call" | custom-call | tf_op jit(solution)/shard_map/pallas_call | solution.py:47
  15.4 3.6 %shard_map.79 = (s32[1]{0:T(128)}, f32[4096,128]{1,0:T(8,128)S(1)}, f32[4096,128]{1,0:T(8,128)S(1)}, bf16[128,5120]{1,0:T(8,128)(2,1)S(1)}, f32[128,128]{1,0:T(8,128)S(1)}, /*index=5*/f32[128,128]{1,0:T(8,128)S(1)}) custom-call(s32[8,128]{1,0:T(8,128)S(1)} %get-tuple-element.45.counts_ref.refs_1_, f32[512,1536]{1,0:T(8,128)S(1)} %copy-done.1, ...), custom_call_target="tpu_custom_call" | custom-call | flops 1000000000 | bytes 8388608 | tf_op jit(solution)/shard_map/pallas_call | solution.py:47
  19.1 3.4 %collective-permute-start.2 = (f32[128,128]{1,0:T(8,128)S(1)}, f32[128,128]{1,0:T(8,128)S(1)}, u32[]{:S(2)}, u32[]{:S(2)}) collective-permute-start(f32[128,128]{1,0:T(8,128)S(1)} %get-tuple-element.50), channel_id=1, source_target_pairs={{1,2},{3,4},{5,6},{7,8},{9,10},{11,12},{13,14},{15,16},{17,18},{19... | collective-permute-start | bytes 196616 | tf_op jit(solution)/shard_map/ppermute | solution.py:41
  22.4 0.3 collective-permute-start.3
  22.7 5.2 %shard_map.81 = (f32[4096,128]{1,0:T(8,128)S(1)}, f32[8,128]{1,0:T(8,128)S(1)}, f32[4096,128]{1,0:T(8,128)S(1)}) custom-call(f32[1]{0:T(128)} %get-tuple-element.44.theta_ref, s32[6,1024]{1,0:T(8,128)S(1)} %copy-done.4, f32[4096,128]{1,0:T(8,128)S(1)} %get-tuple-element.52.field_ref.refs_5_, bf16[128,5120]{1,0:T(8,128)(2,1)S(1)} %get-tuple-element.53.layers_ref, ...), custom_call_target="tpu_custom_call" | custom-call | flops 1000000000 | bytes 4194304 | tf_op jit(solution)/shard_map/pallas_call | solution.py:47
  27.9 4.1 %shard_map.82 = (f32[4096,128]{1,0:T(8,128)S(1)}, f32[4096,128]{1,0:T(8,128)S(1)}, bf16[128,5120]{1,0:T(8,128)(2,1)S(1)}, f32[128,128]{1,0:T(8,128)S(1)}, f32[128,128]{1,0:T(8,128)S(1)}) custom-call(s32[1]{0:T(128)} %bitcast.rank_ref, s32[6,1024]{1,0:T(8,128)S(1)} %copy-done.4, s32[2,256]{1,0:T(2,128)S(1)} %copy-done.6, ...), custom_call_target="tpu_custom_call", output_to_operand_aliasing={{0}: (5, {})} | custom-call | flops 1000000000 | bytes 12582912 | tf_op jit(solution)/shard_map/pallas_call | solution.py:47
  32.0 3.5 %collective-permute-start.6 = (f32[128,128]{1,0:T(8,128)S(1)}, f32[128,128]{1,0:T(8,128)S(1)}, u32[]{:S(2)}, u32[]{:S(2)}) collective-permute-start(f32[128,128]{1,0:T(8,128)S(1)} %get-tuple-element.61), channel_id=1, source_target_pairs={{1,2},{3,4},{5,6},{7,8},{9,10},{11,12},{13,14},{15,16},{17,18},{19... | collective-permute-start | bytes 196616 | tf_op jit(solution)/shard_map/ppermute | solution.py:41
  35.5 0.3 collective-permute-start.7
  35.8 4.3 %shard_map.83 = (f32[4096,128]{1,0:T(8,128)S(1)}, f32[8,128]{1,0:T(8,128)S(1)}) custom-call(f32[1]{0:T(128)} %get-tuple-element.44.theta_ref, s32[6,1024]{1,0:T(8,128)S(1)} %copy-done.4, f32[4096,128]{1,0:T(8,128)S(1)} %get-tuple-element.63.field_ref.refs_6_, bf16[128,5120]{1,0:T(8,128)(2,1)S(1)} %get-tuple-element.64.layers_ref, ...), custom_call_target="tpu_custom_call" | custom-call | flops 1000000000 | bytes 4194304 | tf_op jit(solution)/shard_map/pallas_call | solution.py:47
  40.1 4.1 %shard_map.84 = (f32[4096,128]{1,0:T(8,128)S(1)}, f32[4096,128]{1,0:T(8,128)S(1)}, bf16[128,5120]{1,0:T(8,128)(2,1)S(1)}, f32[128,128]{1,0:T(8,128)S(1)}, f32[128,128]{1,0:T(8,128)S(1)}) custom-call(s32[1]{0:T(128)} %bitcast.rank_ref, s32[6,1024]{1,0:T(8,128)S(1)} %copy-done.4, s32[2,256]{1,0:T(2,128)S(1)} %copy-done.6, ...), custom_call_target="tpu_custom_call", output_to_operand_aliasing={{0}: (5, {})} | custom-call | flops 1000000000 | bytes 12582912 | tf_op jit(solution)/shard_map/pallas_call | solution.py:47
  44.3 3.8 %collective-permute-start.8 = (f32[128,128]{1,0:T(8,128)S(1)}, f32[128,128]{1,0:T(8,128)S(1)}, u32[]{:S(2)}, u32[]{:S(2)}) collective-permute-start(f32[128,128]{1,0:T(8,128)S(1)} %get-tuple-element.69), channel_id=1, source_target_pairs={{1,2},{3,4},{5,6},{7,8},{9,10},{11,12},{13,14},{15,16},{17,18},{19... | collective-permute-start | bytes 196616 | tf_op jit(solution)/shard_map/ppermute | solution.py:41
  48.1 0.3 collective-permute-start.9
  48.5 4.4 %shard_map.85 = (f32[4096,128]{1,0:T(8,128)S(1)}, f32[8,128]{1,0:T(8,128)S(1)}) custom-call(f32[1]{0:T(128)} %get-tuple-element.44.theta_ref, s32[6,1024]{1,0:T(8,128)S(1)} %copy-done.4, f32[4096,128]{1,0:T(8,128)S(1)} %get-tuple-element.71.field_ref.refs_7_, bf16[128,5120]{1,0:T(8,128)(2,1)S(1)} %get-tuple-element.72.layers_ref, ...), custom_call_target="tpu_custom_call" | custom-call | flops 1000000000 | bytes 4194304 | tf_op jit(solution)/shard_map/pallas_call | solution.py:47
  52.9 4.1 %shard_map.86 = (f32[4096,128]{1,0:T(8,128)S(1)}, f32[4096,128]{1,0:T(8,128)S(1)}, bf16[128,5120]{1,0:T(8,128)(2,1)S(1)}, f32[128,128]{1,0:T(8,128)S(1)}, f32[128,128]{1,0:T(8,128)S(1)}) custom-call(s32[1]{0:T(128)} %bitcast.rank_ref, s32[6,1024]{1,0:T(8,128)S(1)} %copy-done.4, s32[2,256]{1,0:T(2,128)S(1)} %copy-done.6, ...), custom_call_target="tpu_custom_call", output_to_operand_aliasing={{0}: (5, {})} | custom-call | flops 1000000000 | bytes 12582912 | tf_op jit(solution)/shard_map/pallas_call | solution.py:47
  57.0 5.0 %collective-permute-start.10 = (f32[128,128]{1,0:T(8,128)S(1)}, f32[128,128]{1,0:T(8,128)S(1)}, u32[]{:S(2)}, u32[]{:S(2)}) collective-permute-start(f32[128,128]{1,0:T(8,128)S(1)} %get-tuple-element.76), channel_id=1, source_target_pairs={{1,2},{3,4},{5,6},{7,8},{9,10},{11,12},{13,14},{15,16},{17,18},{19... | collective-permute-start | bytes 196616 | tf_op jit(solution)/shard_map/ppermute | solution.py:41
  62.0 0.1 collective-permute-start.11
  62.1 4.6 %shard_map.87 = (f32[4096,128]{1,0:T(8,128)S(1)}, f32[8,128]{1,0:T(8,128)S(1)}) custom-call(f32[1]{0:T(128)} %get-tuple-element.44.theta_ref, s32[6,1024]{1,0:T(8,128)S(1)} %copy-done.4, f32[4096,128]{1,0:T(8,128)S(1)} %get-tuple-element.78.field_ref.refs_8_, bf16[128,5120]{1,0:T(8,128)(2,1)S(1)} %get-tuple-element.79.layers_ref, ...), custom_call_target="tpu_custom_call" | custom-call | flops 1000000000 | bytes 4194304 | tf_op jit(solution)/shard_map/pallas_call | solution.py:47
  66.7 0.0 copy-start.3
  66.7 2.0 %shard_map.88 = (f32[4096,128]{1,0:T(8,128)S(1)}, f32[128,128]{1,0:T(8,128)S(1)}) custom-call(s32[1]{0:T(128)} %bitcast.rank_ref, s32[6,1024]{1,0:T(8,128)S(1)} %copy-done.4, f32[128,128]{1,0:T(8,128)S(1)} %collective-permute-done.10.cross_ref, f32[128,128]{1,0:T(8,128)S(1)} %collective-permute-done.11.inside_ref, ...), custom_call_target="tpu_custom_call", output_to_operand_aliasing={{0}: (4, {})} | custom-call | flops 1000000000 | bytes 12582912 | tf_op jit(solution)/shard_map/pallas_call | solution.py:47
  68.7 27.5 %all_to_all.11 = f32[128,1,128]{2,1,0:T(1,128)S(1)} all-to-all(f32[128,1,128]{2,1,0:T(1,128)S(1)} %bitcast.7), channel_id=1, replica_groups=mesh['gx'=4,'gy'=4,'gz'=8] {'gx','gy','gz'}, dimensions={0} | all-to-all | bytes 131072 | tf_op jit(solution)/shard_map/all_to_all | solution.py:760
  96.2 3.8 %shard_map.89 = (f32[512,1024]{1,0:T(8,128)}, f32[512,1024]{1,0:T(8,128)}) custom-call(f32[1]{0:T(128)} %get-tuple-element.44.theta_ref, f32[128,128]{1,0:T(8,128)S(1)} %bitcast.6, f32[4096,128]{1,0:T(8,128)S(1)} %get-tuple-element.55.refs_0_, f32[4096,128]{1,0:T(8,128)S(1)} %get-tuple-element.65.refs_1_, f32[4096,128]{1,0:T(8,128)S(1)} %get-tuple-element.73.refs_2_, ...), custom_call_target="tpu_custom_call" | custom-call | tf_op jit(solution)/shard_map/pallas_call | solution.py:47
  (22 shorter events, 0.1 us)
Async XLA Ops:
  0.6 7.7 %copy-start = (f32[512,1536]{1,0:T(8,128)S(1)}, f32[512,1536]{1,0:T(8,128)}, u32[]{:S(2)}) copy-start(f32[512,1536]{1,0:T(8,128)} %refs_3_.1) | copy-start | bytes 9437188
  0.6 0.8 copy-start.7
  3.6 9.0 %copy-start.4 = (s32[6,1024]{1,0:T(8,128)S(1)}, s32[6,1024]{1,0:T(8,128)}, u32[]{:S(2)}) copy-start(s32[6,1024]{1,0:T(8,128)} %codes_ref.17) | copy-start | bytes 73732
  3.6 9.0 %copy-start.5 = (f32[512,512]{1,0:T(8,128)S(1)}, f32[512,512]{1,0:T(8,128)}, u32[]{:S(2)}) copy-start(f32[512,512]{1,0:T(8,128)} %inverse_ref.1) | copy-start | bytes 3145732
  3.6 9.0 %copy-start.6 = (s32[2,256]{1,0:T(2,128)S(1)}, s32[2,256]{1,0:T(2,128)}, u32[]{:S(2)}) copy-start(s32[2,256]{1,0:T(2,128)} %send_ref.9) | copy-start | bytes 6148
  3.6 11.8 %collective-permute-start = (f32[1032,128]{1,0:T(8,128)S(1)}, f32[1032,128]{1,0:T(8,128)S(1)}, u32[]{:S(2)}, u32[]{:S(2)}) collective-permute-start(f32[1032,128]{1,0:T(8,128)S(1)} %get-tuple-element.46), channel_id=1, source_target_pairs={{1,2},{3,4},{5,6},{7,8},{9,10},{11,12},{13,14},{15,16},{17,18},{19... | collective-permute-start | bytes 1585160 | tf_op jit(solution)/shard_map/ppermute | solution.py:41
  8.2 7.2 %collective-permute-start.1 = (f32[1032,128]{1,0:T(8,128)S(1)}, f32[1032,128]{1,0:T(8,128)S(1)}, u32[]{:S(2)}, u32[]{:S(2)}) collective-permute-start(f32[1032,128]{1,0:T(8,128)S(1)} %get-tuple-element.47), channel_id=1, source_target_pairs={{0,1},{2,3},{4,5},{6,7},{8,9},{10,11},{12,13},{14,15},{16,17},{18,... | collective-permute-start | bytes 1585160 | tf_op jit(solution)/shard_map/ppermute | solution.py:41
  8.4 7.1 %copy-start.1 = (f32[512,1536]{1,0:T(8,128)S(1)}, f32[512,1536]{1,0:T(8,128)}, u32[]{:S(2)}) copy-start(f32[512,1536]{1,0:T(8,128)} %old_ref.4) | copy-start | bytes 9437188
  8.8 13.9 %collective-permute-start.4 = (f32[1024,128]{1,0:T(8,128)S(1)}, f32[1024,128]{1,0:T(8,128)S(1)}, u32[]{:S(2)}, u32[]{:S(2)}) collective-permute-start(f32[1024,128]{1,0:T(8,128)S(1)} %get-tuple-element.57), channel_id=1, source_target_pairs={{1,2},{3,4},{5,6},{7,8},{9,10},{11,12},{13,14},{15,16},{17,18},{19... | collective-permute-start | bytes 1572872 | tf_op jit(solution)/shard_map/ppermute | solution.py:41
  12.5 10.2 %collective-permute-start.5 = (f32[1024,128]{1,0:T(8,128)S(1)}, f32[1024,128]{1,0:T(8,128)S(1)}, u32[]{:S(2)}, u32[]{:S(2)}) collective-permute-start(f32[1024,128]{1,0:T(8,128)S(1)} %get-tuple-element.58), channel_id=1, source_target_pairs={{0,1},{2,3},{4,5},{6,7},{8,9},{10,11},{12,13},{14,15},{16,17},{18,... | collective-permute-start | bytes 1572872 | tf_op jit(solution)/shard_map/ppermute | solution.py:41
  19.0 8.8 %copy-start.2 = (f32[4096,128]{1,0:T(8,128)}, f32[4096,128]{1,0:T(8,128)S(1)}, u32[]{:S(2)}) copy-start(f32[4096,128]{1,0:T(8,128)S(1)} %get-tuple-element.52.field_ref.refs_5_) | copy-start | bytes 6291460
  19.1 8.8 %collective-permute-start.2 = (f32[128,128]{1,0:T(8,128)S(1)}, f32[128,128]{1,0:T(8,128)S(1)}, u32[]{:S(2)}, u32[]{:S(2)}) collective-permute-start(f32[128,128]{1,0:T(8,128)S(1)} %get-tuple-element.50), channel_id=1, source_target_pairs={{1,2},{3,4},{5,6},{7,8},{9,10},{11,12},{13,14},{15,16},{17,18},{19... | collective-permute-start | bytes 196616 | tf_op jit(solution)/shard_map/ppermute | solution.py:41
  22.4 5.5 %collective-permute-start.3 = (f32[128,128]{1,0:T(8,128)S(1)}, f32[128,128]{1,0:T(8,128)S(1)}, u32[]{:S(2)}, u32[]{:S(2)}) collective-permute-start(f32[128,128]{1,0:T(8,128)S(1)} %get-tuple-element.51), channel_id=1, source_target_pairs={{0,1},{2,3},{4,5},{6,7},{8,9},{10,11},{12,13},{14,15},{16,17},{18,... | collective-permute-start | bytes 196616 | tf_op jit(solution)/shard_map/ppermute | solution.py:41
  32.0 8.1 %collective-permute-start.6 = (f32[128,128]{1,0:T(8,128)S(1)}, f32[128,128]{1,0:T(8,128)S(1)}, u32[]{:S(2)}, u32[]{:S(2)}) collective-permute-start(f32[128,128]{1,0:T(8,128)S(1)} %get-tuple-element.61), channel_id=1, source_target_pairs={{1,2},{3,4},{5,6},{7,8},{9,10},{11,12},{13,14},{15,16},{17,18},{19... | collective-permute-start | bytes 196616 | tf_op jit(solution)/shard_map/ppermute | solution.py:41
  35.5 4.6 %collective-permute-start.7 = (f32[128,128]{1,0:T(8,128)S(1)}, f32[128,128]{1,0:T(8,128)S(1)}, u32[]{:S(2)}, u32[]{:S(2)}) collective-permute-start(f32[128,128]{1,0:T(8,128)S(1)} %get-tuple-element.62), channel_id=1, source_target_pairs={{0,1},{2,3},{4,5},{6,7},{8,9},{10,11},{12,13},{14,15},{16,17},{18,... | collective-permute-start | bytes 196616 | tf_op jit(solution)/shard_map/ppermute | solution.py:41
  44.3 8.6 %collective-permute-start.8 = (f32[128,128]{1,0:T(8,128)S(1)}, f32[128,128]{1,0:T(8,128)S(1)}, u32[]{:S(2)}, u32[]{:S(2)}) collective-permute-start(f32[128,128]{1,0:T(8,128)S(1)} %get-tuple-element.69), channel_id=1, source_target_pairs={{1,2},{3,4},{5,6},{7,8},{9,10},{11,12},{13,14},{15,16},{17,18},{19... | collective-permute-start | bytes 196616 | tf_op jit(solution)/shard_map/ppermute | solution.py:41
  48.1 4.8 %collective-permute-start.9 = (f32[128,128]{1,0:T(8,128)S(1)}, f32[128,128]{1,0:T(8,128)S(1)}, u32[]{:S(2)}, u32[]{:S(2)}) collective-permute-start(f32[128,128]{1,0:T(8,128)S(1)} %get-tuple-element.70), channel_id=1, source_target_pairs={{0,1},{2,3},{4,5},{6,7},{8,9},{10,11},{12,13},{14,15},{16,17},{18,... | collective-permute-start | bytes 196616 | tf_op jit(solution)/shard_map/ppermute | solution.py:41
  57.0 9.7 %collective-permute-start.10 = (f32[128,128]{1,0:T(8,128)S(1)}, f32[128,128]{1,0:T(8,128)S(1)}, u32[]{:S(2)}, u32[]{:S(2)}) collective-permute-start(f32[128,128]{1,0:T(8,128)S(1)} %get-tuple-element.76), channel_id=1, source_target_pairs={{1,2},{3,4},{5,6},{7,8},{9,10},{11,12},{13,14},{15,16},{17,18},{19... | collective-permute-start | bytes 196616 | tf_op jit(solution)/shard_map/ppermute | solution.py:41
  62.0 4.7 %collective-permute-start.11 = (f32[128,128]{1,0:T(8,128)S(1)}, f32[128,128]{1,0:T(8,128)S(1)}, u32[]{:S(2)}, u32[]{:S(2)}) collective-permute-start(f32[128,128]{1,0:T(8,128)S(1)} %get-tuple-element.77), channel_id=1, source_target_pairs={{0,1},{2,3},{4,5},{6,7},{8,9},{10,11},{12,13},{14,15},{16,17},{18,... | collective-permute-start | bytes 196616 | tf_op jit(solution)/shard_map/ppermute | solution.py:41
  66.7 29.5 %copy-start.3 = (f32[4096,128]{1,0:T(8,128)S(1)}, f32[4096,128]{1,0:T(8,128)}, u32[]{:S(2)}) copy-start(f32[4096,128]{1,0:T(8,128)} %copy-done.2) | copy-start | bytes 6291460

commit v7 on v6

--- a/solution.py
+++ b/solution.py
@@ -205,7 +205,8 @@
     split_ref[:, 2 * BCELLS : 3 * BCELLS] = (scaled - high.astype(F32)).astype(jnp.bfloat16)
     row = lax.broadcasted_iota(jnp.int32, (BCELLS, BCELLS), 0)
     column = lax.broadcasted_iota(jnp.int32, (BCELLS, BCELLS), 1)
-    theta_ref[0] = jnp.sum(jnp.where(row == column, scaled, 0.0)) * (6.5 / BCELLS)
+    theta = jnp.sum(jnp.where(row == column, scaled, 0.0)) * (6.5 / BCELLS)
+    theta_ref[...] = jnp.full((SUB, LANES), theta)
 
 
 def precondition(split_ref, field_ref, out_ref, pair):
@@ -274,6 +275,7 @@
 
 def pack(field_ref, layers_ref, sent_ref, send_ref, odd, cross_ref, inside_ref):
     low, high = send_ref[0:1, :], send_ref[1:2, :]
+    odd = jnp.concatenate([odd, odd], axis=1) == 1
     for out_ref, start, codes in (
         (cross_ref, 0, jnp.where(odd, high, low)), (inside_ref, HMAX, jnp.where(odd, low, high))
     ):
@@ -360,9 +362,9 @@
         turned_ref = refs[9]
         gram_in = jnp.zeros((SUB, LANES), F32)
         assemble(
-            counts_ref, before_ref[0], old_ref, cross_ref, inside_ref, diagonal_ref, turned_ref
+            counts_ref, count_of(before_ref, 0), old_ref, cross_ref, inside_ref, diagonal_ref, turned_ref
         )
-    theta = theta_ref[0]
+    theta = theta_ref[...]
     sums = [jnp.zeros((SUB, LANES), F32) for _ in range(known)]
 
     def stencil(chunk):
@@ -432,9 +434,8 @@
                 beside = product[:, half * LANES : (half + 1) * LANES]
             else:
                 code = codes_ref[which : which + 1, chunk * LANES : (chunk + 1) * LANES] - REMOTE
-                code = jnp.broadcast_to(code, (SUB, LANES))
-                lane = code & (LANES - 1)
-                tile = (code >> 7) ^ (odd * 2)
+                lane = jnp.broadcast_to(code & (LANES - 1), (SUB, LANES))
+                tile = jnp.broadcast_to((code >> 7) ^ (odd * 2), (SUB, LANES))
                 found = [jnp.zeros((SUB, LANES), F32) for _ in range(8)]
                 for source in range(2 * HMAX // LANES):
                     here = tile == source
@@ -486,39 +487,39 @@
 ):
     odd = count_of(counts_ref, 3) == 1
     before = count_before(odd, cross_ref, inside_ref)
-    before_ref[0] = before
+    before_ref[...] = jnp.full((SUB, LANES), before)
     assemble(counts_ref, before, old_ref, cross_ref, inside_ref, rhs_ref, turned_ref)
     send(
-        split_ref, rhs_ref, field_ref, layers_ref, sent_ref, send_ref, odd, to_cross_ref,
-        to_inside_ref, lambda pair: None,
+        split_ref, rhs_ref, field_ref, layers_ref, sent_ref, send_ref, counts_ref[3:4, :],
+        to_cross_ref, to_inside_ref, lambda pair: None,
     )
 
 
 def next_kernel(
-    rank_ref, codes_ref, send_ref, cross_ref, inside_ref, partial_ref, taken_ref, split_ref,
+    counts_ref, codes_ref, send_ref, cross_ref, inside_ref, partial_ref, taken_ref, split_ref,
     sent_ref,
     out_ref, field_ref, layers_ref, to_cross_ref, to_inside_ref,
 ):
     del partial_ref
-    odd = rank_ref[0] & 1
+    odd = counts_ref[3:4, :]
     received = receive(cross_ref, inside_ref)
 
     def before(pair):
         finish(odd, codes_ref, taken_ref, received, cross_ref, inside_ref, out_ref, pair)
 
     send(
-        split_ref, out_ref, field_ref, layers_ref, sent_ref, send_ref, odd == 1, to_cross_ref,
+        split_ref, out_ref, field_ref, layers_ref, sent_ref, send_ref, odd, to_cross_ref,
         to_inside_ref, before,
     )
 
 
 def end_kernel(
-    rank_ref, codes_ref, cross_ref, inside_ref, partial_ref, taken_ref, gram_in_ref, *refs
+    counts_ref, codes_ref, cross_ref, inside_ref, partial_ref, taken_ref, gram_in_ref, *refs
 ):
     del partial_ref
     basis = refs[: BASIS - 1]
     out_ref, gram_ref, sums_ref = refs[BASIS - 1 :]
-    odd = rank_ref[0] & 1
+    odd = counts_ref[3:4, :]
     received = receive(cross_ref, inside_ref)
     sums = [jnp.zeros((SUB, LANES), F32) for _ in range(BASIS)]
     for pair in range(CHUNKS // 2):
@@ -595,7 +596,7 @@
         return jnp.sum(jnp.where(lane == k, row, 0.0), axis=1, keepdims=True)
 
     gram = [[entry(a * (a + 1) // 2 + b) for b in range(a + 1)] for a in range(BASIS)]
-    theta = jnp.full((1, 1), theta_ref[0])
+    theta = theta_ref[0:1, 0:1]
     total, residual = recurrence(gram, theta)
     total = [None if x is None else jnp.broadcast_to(x, (SUB, LANES)) for x in total]
     residual = [jnp.broadcast_to(x, (SUB, LANES)) for x in residual]
@@ -678,22 +679,22 @@
         prepare_kernel,
         (
             split_type,
-            jax.ShapeDtypeStruct((1,), F32),
+            of(SUB),
             jax.ShapeDtypeStruct((len(SENT) * BDEV, 2 * HMAX), jnp.bfloat16),
             jax.ShapeDtypeStruct((2 * HMAX, len(PRODUCT) * BDEV), jnp.bfloat16),
             jax.ShapeDtypeStruct((BDEV, len(PRODUCT) * BDEV), jnp.bfloat16),
         ),
         (rank, block_inverse, face_source, send_layers),
         [SMEM] + [VMEM] * 3,
-        (VMEM, SMEM, VMEM, VMEM, VMEM),
+        (VMEM,) * 5,
     )
     before, rhs, field, packed, to_cross, to_inside = call(
         first_kernel,
-        (jax.ShapeDtypeStruct((1,), jnp.int32),)
+        (jax.ShapeDtypeStruct((SUB, LANES), jnp.int32),)
         + (field_type, field_type, packed_type, halo_type, halo_type),
         (counts, rhs_old, rhs_cross, rhs_inside, split, sent, send_layers),
         [VMEM] * 7,
-        (SMEM,) + (VMEM,) * 5,
+        (VMEM,) * 6,
         [turned],
         flops=10**9,
         bytes_accessed=8 * MIB,
@@ -706,21 +707,18 @@
         from_inside = swapped(to_inside, False)
         args = [theta, face_source, field, packed, local] + basis
         outs = [field_type, of(SUB)]
-        specs = [SMEM] + [VMEM] * (len(args) - 1)
         if known > 1:
             args += [diagonal, gram]
-            specs += [VMEM, VMEM]
             scratch = layers + [sums]
         else:
             args += [counts, before, diagonal_old, diagonal_cross, diagonal_inside]
-            specs += [VMEM, SMEM] + [VMEM] * 3
             outs.append(field_type)
             scratch = [turned] + layers + [sums]
         found = call(
             functools.partial(local_kernel, known),
             tuple(outs),
             tuple(args),
-            specs,
+            [VMEM] * len(args),
             (VMEM,) * len(outs),
             scratch,
             flops=10**9,
@@ -734,10 +732,10 @@
                 next_kernel,
                 (field_type, field_type, packed_type, halo_type, halo_type),
                 (
-                    rank, face_source, send_layers, from_cross, from_inside, partial, taken,
+                    counts, face_source, send_layers, from_cross, from_inside, partial, taken,
                     split, sent,
                 ),
-                [SMEM] + [VMEM] * 8,
+                [VMEM] * 9,
                 (VMEM,) * 5,
                 flops=10**9,
                 bytes_accessed=12 * MIB,
@@ -748,8 +746,8 @@
             value, copies = call(
                 end_kernel,
                 (field_type, of(lax.axis_size(AXES))),
-                (rank, face_source, from_cross, from_inside, partial, taken, gram, *basis),
-                [SMEM] + [VMEM] * (6 + len(basis)),
+                (counts, face_source, from_cross, from_inside, partial, taken, gram, *basis),
+                [VMEM] * (7 + len(basis)),
                 (VMEM, VMEM),
                 [sums],
                 flops=10**9,
@@ -762,7 +760,7 @@
         last_kernel,
         (out_type, out_type),
         (theta, gathered, *basis, *fields),
-        [SMEM] + [VMEM] * (2 * BASIS),
+        [VMEM] * (2 * BASIS + 1),
         (HBM, HBM),
         [pltpu.VMEM((BCELLS, BDEV), F32)] * 2 + [pltpu.SemaphoreType.DMA((2, PARTS))],
         limit=16,

time: 101 us -> 98.8 us (0.978)
  Pallas kernels: 45.5 us -> 40.6 us
  blocking collectives: 27.5 us -> 30.2 us
    pallas_call x13, Pallas kernels: 45.5 us -> 40.6 us  [call(): pl.pallas_call(kernel, out_shape=outs, in_specs=in_specs, out_specs=out_s...]
    all_to_all x1, blocking collectives: 27.5 us -> 30.2 us  [per_device(): lax.all_to_all(copies, AXES, split_axis=0, concat_axis=0, tiled=True)]
  transfers between devices with their start and end apart: 12 -> 12, of which waited for: 0 -> 1; matrix products, arithmetic and copies ran while one was open for 0% -> 0% of each run, Pallas kernels for 25% -> 21%
where the time goes in v7:
time: 98.8 us; the launch traced here: 98.5 us
  Pallas kernels  40.6 us (41%)
  blocking collectives  30.2 us (31%)
  starting transfers between devices  25.4 us (26%)
  between operations  1.18 us (1%)
    pallas_call x13, Pallas kernels, call(): pl.pallas_call(kernel, out_shape=outs, in_specs=in_specs, out_specs=out_s...  40.6 us
    all_to_all x1, blocking collectives, per_device(): lax.all_to_all(copies, AXES, split_axis=0, concat_axis=0, tiled=True)  30.2 us
    ppermute x12, starting transfers between devices, swapped(): lax.ppermute(value, AXES, pairs + [(high, low) for low, high in pairs])  25.4 us
  transfers between devices with their start and end apart: 12, of which 1 were waited for; matrix products, arithmetic and copies ran while one was open for 0% of the time, Pallas kernels for 21%

profile of v7, /device:TPU:1, one launch (start us, length us, event | category | flops | bytes accessed | tf_op | source)
XLA Modules:
  0.0 98.5 jit_solution(1398951340123347860)
XLA Ops:
  0.7 0.8 copy-done.7
  1.5 2.1 %shard_map.78 = (s32[8,128]{1,0:T(8,128)S(1)}, f32[1032,128]{1,0:T(8,128)S(1)}, f32[1032,128]{1,0:T(8,128)S(1)}) custom-call(s32[1]{0:T(128)} %bitcast.rank_ref, s32[12,128]{1,0:T(8,128)S(1)} %bitcast.8, f32[512,1536]{1,0:T(8,128)} %old_ref.4), custom_call_target="tpu_custom_call" | custom-call | tf_op jit(solution)/shard_map/pallas_call | solution.py:47
  3.6 0.0 copy-start.4
  3.6 0.0 copy-start.5
  3.6 0.0 copy-start.6
  3.6 4.6 %collective-permute-start = (f32[1032,128]{1,0:T(8,128)S(1)}, f32[1032,128]{1,0:T(8,128)S(1)}, u32[]{:S(2)}, u32[]{:S(2)}) collective-permute-start(f32[1032,128]{1,0:T(8,128)S(1)} %get-tuple-element.46), channel_id=1, source_target_pairs={{1,2},{3,4},{5,6},{7,8},{9,10},{11,12},{13,14},{15,16},{17,18},{19... | collective-permute-start | bytes 1585160 | tf_op jit(solution)/shard_map/ppermute | solution.py:41
  8.2 0.1 collective-permute-start.1
  8.4 0.5 shard_map.80
  8.8 3.6 %collective-permute-start.4 = (f32[1024,128]{1,0:T(8,128)S(1)}, f32[1024,128]{1,0:T(8,128)S(1)}, u32[]{:S(2)}, u32[]{:S(2)}) collective-permute-start(f32[1024,128]{1,0:T(8,128)S(1)} %get-tuple-element.57), channel_id=1, source_target_pairs={{1,2},{3,4},{5,6},{7,8},{9,10},{11,12},{13,14},{15,16},{17,18},{19... | collective-permute-start | bytes 1572872 | tf_op jit(solution)/shard_map/ppermute | solution.py:41
  12.5 0.1 collective-permute-start.5
  12.6 2.3 %shard_map.77 = (bf16[512,1536]{1,0:T(8,128)(2,1)S(1)}, f32[8,128]{1,0:T(8,128)S(1)}, bf16[4096,512]{1,0:T(8,128)(2,1)S(1)}, bf16[512,3072]{1,0:T(8,128)(2,1)S(1)}, bf16[1024,3072]{1,0:T(8,128)(2,1)S(1)}) custom-call(s32[1]{0:T(128)} %bitcast.rank_ref, f32[512,512]{1,0:T(8,128)S(1)} %copy-done.5, s32[6,1024]{1,0:T(8,128)S(1)} %copy-done.4, ...), custom_call_target="tpu_custom_call" | custom-call | tf_op jit(solution)/shard_map/pallas_call | solution.py:47
  14.9 0.2 collective-permute-done.cross_ref
  15.1 3.3 %shard_map.79 = (s32[8,128]{1,0:T(8,128)S(1)}, f32[4096,128]{1,0:T(8,128)S(1)}, f32[4096,128]{1,0:T(8,128)S(1)}, bf16[128,5120]{1,0:T(8,128)(2,1)S(1)}, f32[128,128]{1,0:T(8,128)S(1)}, /*index=5*/f32[128,128]{1,0:T(8,128)S(1)}) custom-call(s32[8,128]{1,0:T(8,128)S(1)} %get-tuple-element.45.counts_ref.refs_1_, f32[512,1536]{1,0:T(8,128)S(1)} %copy-done.1, ...), custom_call_target="tpu_custom_call" | custom-call | flops 1000000000 | bytes 8388608 | tf_op jit(solution)/shard_map/pallas_call | solution.py:47
  18.5 3.6 %collective-permute-start.2 = (f32[128,128]{1,0:T(8,128)S(1)}, f32[128,128]{1,0:T(8,128)S(1)}, u32[]{:S(2)}, u32[]{:S(2)}) collective-permute-start(f32[128,128]{1,0:T(8,128)S(1)} %get-tuple-element.50), channel_id=1, source_target_pairs={{1,2},{3,4},{5,6},{7,8},{9,10},{11,12},{13,14},{15,16},{17,18},{19... | collective-permute-start | bytes 196616 | tf_op jit(solution)/shard_map/ppermute | solution.py:41
  22.2 0.3 collective-permute-start.3
  22.4 3.9 %shard_map.81 = (f32[4096,128]{1,0:T(8,128)S(1)}, f32[8,128]{1,0:T(8,128)S(1)}, f32[4096,128]{1,0:T(8,128)S(1)}) custom-call(f32[8,128]{1,0:T(8,128)S(1)} %get-tuple-element.44.theta_ref, s32[6,1024]{1,0:T(8,128)S(1)} %copy-done.4, f32[4096,128]{1,0:T(8,128)S(1)} %get-tuple-element.52.field_ref.refs_5_, bf16[128,5120]{1,0:T(8,128)(2,1)S(1)} %get-tuple-element.53.layers_ref, ...), custom_call_target="tpu_custom_call" | custom-call | flops 1000000000 | bytes 4194304 | tf_op jit(solution)/shard_map/pallas_call | solution.py:47
  26.4 4.1 %shard_map.82 = (f32[4096,128]{1,0:T(8,128)S(1)}, f32[4096,128]{1,0:T(8,128)S(1)}, bf16[128,5120]{1,0:T(8,128)(2,1)S(1)}, f32[128,128]{1,0:T(8,128)S(1)}, f32[128,128]{1,0:T(8,128)S(1)}) custom-call(s32[8,128]{1,0:T(8,128)S(1)} %get-tuple-element.45.counts_ref.refs_1_, s32[6,1024]{1,0:T(8,128)S(1)} %copy-done.4, ...), custom_call_target="tpu_custom_call", output_to_operand_aliasing={{0}: (5, {})} | custom-call | flops 1000000000 | bytes 12582912 | tf_op jit(solution)/shard_map/pallas_call | solution.py:47
  30.5 3.5 %collective-permute-start.6 = (f32[128,128]{1,0:T(8,128)S(1)}, f32[128,128]{1,0:T(8,128)S(1)}, u32[]{:S(2)}, u32[]{:S(2)}) collective-permute-start(f32[128,128]{1,0:T(8,128)S(1)} %get-tuple-element.61), channel_id=1, source_target_pairs={{1,2},{3,4},{5,6},{7,8},{9,10},{11,12},{13,14},{15,16},{17,18},{19... | collective-permute-start | bytes 196616 | tf_op jit(solution)/shard_map/ppermute | solution.py:41
  34.0 0.3 collective-permute-start.7
  34.3 3.6 %shard_map.83 = (f32[4096,128]{1,0:T(8,128)S(1)}, f32[8,128]{1,0:T(8,128)S(1)}) custom-call(f32[8,128]{1,0:T(8,128)S(1)} %get-tuple-element.44.theta_ref, s32[6,1024]{1,0:T(8,128)S(1)} %copy-done.4, f32[4096,128]{1,0:T(8,128)S(1)} %get-tuple-element.63.field_ref.refs_6_, bf16[128,5120]{1,0:T(8,128)(2,1)S(1)} %get-tuple-element.64.layers_ref, ...), custom_call_target="tpu_custom_call" | custom-call | flops 1000000000 | bytes 4194304 | tf_op jit(solution)/shard_map/pallas_call | solution.py:47
  38.0 4.1 %shard_map.84 = (f32[4096,128]{1,0:T(8,128)S(1)}, f32[4096,128]{1,0:T(8,128)S(1)}, bf16[128,5120]{1,0:T(8,128)(2,1)S(1)}, f32[128,128]{1,0:T(8,128)S(1)}, f32[128,128]{1,0:T(8,128)S(1)}) custom-call(s32[8,128]{1,0:T(8,128)S(1)} %get-tuple-element.45.counts_ref.refs_1_, s32[6,1024]{1,0:T(8,128)S(1)} %copy-done.4, ...), custom_call_target="tpu_custom_call", output_to_operand_aliasing={{0}: (5, {})} | custom-call | flops 1000000000 | bytes 12582912 | tf_op jit(solution)/shard_map/pallas_call | solution.py:47
  42.1 3.3 %collective-permute-start.8 = (f32[128,128]{1,0:T(8,128)S(1)}, f32[128,128]{1,0:T(8,128)S(1)}, u32[]{:S(2)}, u32[]{:S(2)}) collective-permute-start(f32[128,128]{1,0:T(8,128)S(1)} %get-tuple-element.69), channel_id=1, source_target_pairs={{1,2},{3,4},{5,6},{7,8},{9,10},{11,12},{13,14},{15,16},{17,18},{19... | collective-permute-start | bytes 196616 | tf_op jit(solution)/shard_map/ppermute | solution.py:41
  45.4 0.3 collective-permute-start.9
  45.8 3.6 %shard_map.85 = (f32[4096,128]{1,0:T(8,128)S(1)}, f32[8,128]{1,0:T(8,128)S(1)}) custom-call(f32[8,128]{1,0:T(8,128)S(1)} %get-tuple-element.44.theta_ref, s32[6,1024]{1,0:T(8,128)S(1)} %copy-done.4, f32[4096,128]{1,0:T(8,128)S(1)} %get-tuple-element.71.field_ref.refs_7_, bf16[128,5120]{1,0:T(8,128)(2,1)S(1)} %get-tuple-element.72.layers_ref, ...), custom_call_target="tpu_custom_call" | custom-call | flops 1000000000 | bytes 4194304 | tf_op jit(solution)/shard_map/pallas_call | solution.py:47
  49.4 4.1 %shard_map.86 = (f32[4096,128]{1,0:T(8,128)S(1)}, f32[4096,128]{1,0:T(8,128)S(1)}, bf16[128,5120]{1,0:T(8,128)(2,1)S(1)}, f32[128,128]{1,0:T(8,128)S(1)}, f32[128,128]{1,0:T(8,128)S(1)}) custom-call(s32[8,128]{1,0:T(8,128)S(1)} %get-tuple-element.45.counts_ref.refs_1_, s32[6,1024]{1,0:T(8,128)S(1)} %copy-done.4, ...), custom_call_target="tpu_custom_call", output_to_operand_aliasing={{0}: (5, {})} | custom-call | flops 1000000000 | bytes 12582912 | tf_op jit(solution)/shard_map/pallas_call | solution.py:47
  53.5 5.5 %collective-permute-start.10 = (f32[128,128]{1,0:T(8,128)S(1)}, f32[128,128]{1,0:T(8,128)S(1)}, u32[]{:S(2)}, u32[]{:S(2)}) collective-permute-start(f32[128,128]{1,0:T(8,128)S(1)} %get-tuple-element.76), channel_id=1, source_target_pairs={{1,2},{3,4},{5,6},{7,8},{9,10},{11,12},{13,14},{15,16},{17,18},{19... | collective-permute-start | bytes 196616 | tf_op jit(solution)/shard_map/ppermute | solution.py:41
  59.0 0.1 collective-permute-start.11
  59.1 3.9 %shard_map.87 = (f32[4096,128]{1,0:T(8,128)S(1)}, f32[8,128]{1,0:T(8,128)S(1)}) custom-call(f32[8,128]{1,0:T(8,128)S(1)} %get-tuple-element.44.theta_ref, s32[6,1024]{1,0:T(8,128)S(1)} %copy-done.4, f32[4096,128]{1,0:T(8,128)S(1)} %get-tuple-element.78.field_ref.refs_8_, bf16[128,5120]{1,0:T(8,128)(2,1)S(1)} %get-tuple-element.79.layers_ref, ...), custom_call_target="tpu_custom_call" | custom-call | flops 1000000000 | bytes 4194304 | tf_op jit(solution)/shard_map/pallas_call | solution.py:47
  63.0 0.0 copy-start.3
  63.1 2.0 %shard_map.88 = (f32[4096,128]{1,0:T(8,128)S(1)}, f32[128,128]{1,0:T(8,128)S(1)}) custom-call(s32[8,128]{1,0:T(8,128)S(1)} %get-tuple-element.45.counts_ref.refs_1_, s32[6,1024]{1,0:T(8,128)S(1)} %copy-done.4, f32[128,128]{1,0:T(8,128)S(1)} %collective-permute-done.10.cross_ref, ...), custom_call_target="tpu_custom_call", output_to_operand_aliasing={{0}: (4, {})} | custom-call | flops 1000000000 | bytes 12582912 | tf_op jit(solution)/shard_map/pallas_call | solution.py:47
  65.0 30.2 %all_to_all.11 = f32[128,1,128]{2,1,0:T(1,128)S(1)} all-to-all(f32[128,1,128]{2,1,0:T(1,128)S(1)} %bitcast.7), channel_id=1, replica_groups=mesh['gx'=4,'gy'=4,'gz'=8] {'gx','gy','gz'}, dimensions={0} | all-to-all | bytes 131072 | tf_op jit(solution)/shard_map/all_to_all | solution.py:758
  95.2 3.1 %shard_map.89 = (f32[512,1024]{1,0:T(8,128)}, f32[512,1024]{1,0:T(8,128)}) custom-call(f32[8,128]{1,0:T(8,128)S(1)} %get-tuple-element.44.theta_ref, f32[128,128]{1,0:T(8,128)S(1)} %bitcast.6, f32[4096,128]{1,0:T(8,128)S(1)} %get-tuple-element.55.refs_0_, f32[4096,128]{1,0:T(8,128)S(1)} %get-tuple-element.65.refs_1_, ...), custom_call_target="tpu_custom_call" | custom-call | tf_op jit(solution)/shard_map/pallas_call | solution.py:47
  (22 shorter events, 0.1 us)
Async XLA Ops:
  0.6 7.7 %copy-start = (f32[512,1536]{1,0:T(8,128)S(1)}, f32[512,1536]{1,0:T(8,128)}, u32[]{:S(2)}) copy-start(f32[512,1536]{1,0:T(8,128)} %refs_3_.1) | copy-start | bytes 9437188
  0.6 0.8 copy-start.7
  3.6 9.0 %copy-start.4 = (s32[6,1024]{1,0:T(8,128)S(1)}, s32[6,1024]{1,0:T(8,128)}, u32[]{:S(2)}) copy-start(s32[6,1024]{1,0:T(8,128)} %codes_ref.17) | copy-start | bytes 73732
  3.6 9.0 %copy-start.5 = (f32[512,512]{1,0:T(8,128)S(1)}, f32[512,512]{1,0:T(8,128)}, u32[]{:S(2)}) copy-start(f32[512,512]{1,0:T(8,128)} %inverse_ref.1) | copy-start | bytes 3145732
  3.6 9.0 %copy-start.6 = (s32[2,256]{1,0:T(2,128)S(1)}, s32[2,256]{1,0:T(2,128)}, u32[]{:S(2)}) copy-start(s32[2,256]{1,0:T(2,128)} %send_ref.9) | copy-start | bytes 6148
  3.6 11.5 %collective-permute-start = (f32[1032,128]{1,0:T(8,128)S(1)}, f32[1032,128]{1,0:T(8,128)S(1)}, u32[]{:S(2)}, u32[]{:S(2)}) collective-permute-start(f32[1032,128]{1,0:T(8,128)S(1)} %get-tuple-element.46), channel_id=1, source_target_pairs={{1,2},{3,4},{5,6},{7,8},{9,10},{11,12},{13,14},{15,16},{17,18},{19... | collective-permute-start | bytes 1585160 | tf_op jit(solution)/shard_map/ppermute | solution.py:41
  8.2 6.9 %collective-permute-start.1 = (f32[1032,128]{1,0:T(8,128)S(1)}, f32[1032,128]{1,0:T(8,128)S(1)}, u32[]{:S(2)}, u32[]{:S(2)}) collective-permute-start(f32[1032,128]{1,0:T(8,128)S(1)} %get-tuple-element.47), channel_id=1, source_target_pairs={{0,1},{2,3},{4,5},{6,7},{8,9},{10,11},{12,13},{14,15},{16,17},{18,... | collective-permute-start | bytes 1585160 | tf_op jit(solution)/shard_map/ppermute | solution.py:41
  8.4 6.8 %copy-start.1 = (f32[512,1536]{1,0:T(8,128)S(1)}, f32[512,1536]{1,0:T(8,128)}, u32[]{:S(2)}) copy-start(f32[512,1536]{1,0:T(8,128)} %old_ref.4) | copy-start | bytes 9437188
  8.8 13.6 %collective-permute-start.4 = (f32[1024,128]{1,0:T(8,128)S(1)}, f32[1024,128]{1,0:T(8,128)S(1)}, u32[]{:S(2)}, u32[]{:S(2)}) collective-permute-start(f32[1024,128]{1,0:T(8,128)S(1)} %get-tuple-element.57), channel_id=1, source_target_pairs={{1,2},{3,4},{5,6},{7,8},{9,10},{11,12},{13,14},{15,16},{17,18},{19... | collective-permute-start | bytes 1572872 | tf_op jit(solution)/shard_map/ppermute | solution.py:41
  12.5 10.0 %collective-permute-start.5 = (f32[1024,128]{1,0:T(8,128)S(1)}, f32[1024,128]{1,0:T(8,128)S(1)}, u32[]{:S(2)}, u32[]{:S(2)}) collective-permute-start(f32[1024,128]{1,0:T(8,128)S(1)} %get-tuple-element.58), channel_id=1, source_target_pairs={{0,1},{2,3},{4,5},{6,7},{8,9},{10,11},{12,13},{14,15},{16,17},{18,... | collective-permute-start | bytes 1572872 | tf_op jit(solution)/shard_map/ppermute | solution.py:41
  18.5 7.9 %copy-start.2 = (f32[4096,128]{1,0:T(8,128)}, f32[4096,128]{1,0:T(8,128)S(1)}, u32[]{:S(2)}) copy-start(f32[4096,128]{1,0:T(8,128)S(1)} %get-tuple-element.52.field_ref.refs_5_) | copy-start | bytes 6291460
  18.5 7.9 %collective-permute-start.2 = (f32[128,128]{1,0:T(8,128)S(1)}, f32[128,128]{1,0:T(8,128)S(1)}, u32[]{:S(2)}, u32[]{:S(2)}) collective-permute-start(f32[128,128]{1,0:T(8,128)S(1)} %get-tuple-element.50), channel_id=1, source_target_pairs={{1,2},{3,4},{5,6},{7,8},{9,10},{11,12},{13,14},{15,16},{17,18},{19... | collective-permute-start | bytes 196616 | tf_op jit(solution)/shard_map/ppermute | solution.py:41
  22.2 4.2 %collective-permute-start.3 = (f32[128,128]{1,0:T(8,128)S(1)}, f32[128,128]{1,0:T(8,128)S(1)}, u32[]{:S(2)}, u32[]{:S(2)}) collective-permute-start(f32[128,128]{1,0:T(8,128)S(1)} %get-tuple-element.51), channel_id=1, source_target_pairs={{0,1},{2,3},{4,5},{6,7},{8,9},{10,11},{12,13},{14,15},{16,17},{18,... | collective-permute-start | bytes 196616 | tf_op jit(solution)/shard_map/ppermute | solution.py:41
  30.5 7.4 %collective-permute-start.6 = (f32[128,128]{1,0:T(8,128)S(1)}, f32[128,128]{1,0:T(8,128)S(1)}, u32[]{:S(2)}, u32[]{:S(2)}) collective-permute-start(f32[128,128]{1,0:T(8,128)S(1)} %get-tuple-element.61), channel_id=1, source_target_pairs={{1,2},{3,4},{5,6},{7,8},{9,10},{11,12},{13,14},{15,16},{17,18},{19... | collective-permute-start | bytes 196616 | tf_op jit(solution)/shard_map/ppermute | solution.py:41
  34.0 4.0 %collective-permute-start.7 = (f32[128,128]{1,0:T(8,128)S(1)}, f32[128,128]{1,0:T(8,128)S(1)}, u32[]{:S(2)}, u32[]{:S(2)}) collective-permute-start(f32[128,128]{1,0:T(8,128)S(1)} %get-tuple-element.62), channel_id=1, source_target_pairs={{0,1},{2,3},{4,5},{6,7},{8,9},{10,11},{12,13},{14,15},{16,17},{18,... | collective-permute-start | bytes 196616 | tf_op jit(solution)/shard_map/ppermute | solution.py:41
  42.1 7.3 %collective-permute-start.8 = (f32[128,128]{1,0:T(8,128)S(1)}, f32[128,128]{1,0:T(8,128)S(1)}, u32[]{:S(2)}, u32[]{:S(2)}) collective-permute-start(f32[128,128]{1,0:T(8,128)S(1)} %get-tuple-element.69), channel_id=1, source_target_pairs={{1,2},{3,4},{5,6},{7,8},{9,10},{11,12},{13,14},{15,16},{17,18},{19... | collective-permute-start | bytes 196616 | tf_op jit(solution)/shard_map/ppermute | solution.py:41
  45.4 3.9 %collective-permute-start.9 = (f32[128,128]{1,0:T(8,128)S(1)}, f32[128,128]{1,0:T(8,128)S(1)}, u32[]{:S(2)}, u32[]{:S(2)}) collective-permute-start(f32[128,128]{1,0:T(8,128)S(1)} %get-tuple-element.70), channel_id=1, source_target_pairs={{0,1},{2,3},{4,5},{6,7},{8,9},{10,11},{12,13},{14,15},{16,17},{18,... | collective-permute-start | bytes 196616 | tf_op jit(solution)/shard_map/ppermute | solution.py:41
  53.5 9.5 %collective-permute-start.10 = (f32[128,128]{1,0:T(8,128)S(1)}, f32[128,128]{1,0:T(8,128)S(1)}, u32[]{:S(2)}, u32[]{:S(2)}) collective-permute-start(f32[128,128]{1,0:T(8,128)S(1)} %get-tuple-element.76), channel_id=1, source_target_pairs={{1,2},{3,4},{5,6},{7,8},{9,10},{11,12},{13,14},{15,16},{17,18},{19... | collective-permute-start | bytes 196616 | tf_op jit(solution)/shard_map/ppermute | solution.py:41
  59.0 4.0 %collective-permute-start.11 = (f32[128,128]{1,0:T(8,128)S(1)}, f32[128,128]{1,0:T(8,128)S(1)}, u32[]{:S(2)}, u32[]{:S(2)}) collective-permute-start(f32[128,128]{1,0:T(8,128)S(1)} %get-tuple-element.77), channel_id=1, source_target_pairs={{0,1},{2,3},{4,5},{6,7},{8,9},{10,11},{12,13},{14,15},{16,17},{18,... | collective-permute-start | bytes 196616 | tf_op jit(solution)/shard_map/ppermute | solution.py:41
  63.0 32.2 %copy-start.3 = (f32[4096,128]{1,0:T(8,128)S(1)}, f32[4096,128]{1,0:T(8,128)}, u32[]{:S(2)}) copy-start(f32[4096,128]{1,0:T(8,128)} %copy-done.2) | copy-start | bytes 6291460

commit v8 on v7

--- a/solution.py
+++ b/solution.py
@@ -27,6 +27,9 @@
 PRODUCT = (0, 4, 5)
 SENT = (4, 5, 0, 3)
 SPLIT = (1,) + SENT
+SHELL = [(i, j) for i in range(BE) for j in range(BE) if i in (0, BE - 1) or j in (0, BE - 1)]
+CORE = [(i, j) for i in range(BE) for j in range(BE) if (i, j) not in SHELL]
+SHELL_ROWS = len(SHELL) * BE
 F32 = jnp.float32
 
 VMEM = pl.BlockSpec(memory_space=pltpu.VMEM)
@@ -181,7 +184,8 @@
 
 
 def prepare_kernel(
-    rank_ref, inverse_ref, codes_ref, send_ref, split_ref, theta_ref, sent_ref, taken_ref, local_ref
+    rank_ref, inverse_ref, codes_ref, send_ref,
+    split_ref, core_ref, theta_ref, sent_ref, taken_ref, local_ref,
 ):
     select(rank_ref[0] & 1, codes_ref, send_ref, sent_ref, taken_ref, local_ref)
     inverse = inverse_ref[...]
@@ -200,16 +204,30 @@
         scale = jnp.where(small, scale * 2.0**power, scale)
     scaled = inverse * scale
     high = scaled.astype(jnp.bfloat16)
-    split_ref[:, 0:BCELLS] = high
-    split_ref[:, BCELLS : 2 * BCELLS] = high
-    split_ref[:, 2 * BCELLS : 3 * BCELLS] = (scaled - high.astype(F32)).astype(jnp.bfloat16)
+    low = (scaled - high.astype(F32)).astype(jnp.bfloat16)
+    at = lax.broadcasted_iota(jnp.int32, (2 * FACE, BCELLS), 0)
+    cell = lax.broadcasted_iota(jnp.int32, (2 * FACE, BCELLS), 1)
+    wanted = jnp.where(at < FACE, at * BE, (at - FACE) * BE + BE - 1)
+    ends = jnp.where(cell == wanted, 1.0, 0.0).astype(jnp.bfloat16)
+
+    def tiles(value, which):
+        return [value[(i * BE + j) * BE : (i * BE + j + 1) * BE, :] for i, j in which]
+
+    for part, value in ((0, high), (2 * BCELLS, low)):
+        wide = value.astype(F32)
+        end_rows = jnp.dot(ends, value, preferred_element_type=F32)
+        shell = jnp.concatenate(tiles(wide, SHELL) + [end_rows], axis=0).astype(jnp.bfloat16)
+        core = jnp.concatenate(tiles(wide, CORE), axis=0).astype(jnp.bfloat16)
+        for column in (part, BCELLS) if part == 0 else (part,):
+            split_ref[:, column : column + BCELLS] = shell
+            core_ref[:, column : column + BCELLS] = core
     row = lax.broadcasted_iota(jnp.int32, (BCELLS, BCELLS), 0)
     column = lax.broadcasted_iota(jnp.int32, (BCELLS, BCELLS), 1)
     theta = jnp.sum(jnp.where(row == column, scaled, 0.0)) * (6.5 / BCELLS)
     theta_ref[...] = jnp.full((SUB, LANES), theta)
 
 
-def precondition(split_ref, field_ref, out_ref, pair):
+def precondition(split_ref, field_ref, pair):
     base = pair * 2 * BCELLS
     field = jnp.concatenate(
         [field_ref[base + half * BCELLS : base + (half + 1) * BCELLS, :] for half in range(2)],
@@ -218,9 +236,16 @@
     top = field.astype(jnp.bfloat16)
     rest = (field - top.astype(F32)).astype(jnp.bfloat16)
     stacked = jnp.concatenate([top, rest, top], axis=0)
-    found = jnp.dot(split_ref[...], stacked, preferred_element_type=F32)
-    out_ref[base : base + BCELLS, :] = found[:, :LANES]
-    out_ref[base + BCELLS : base + 2 * BCELLS, :] = found[:, LANES:]
+    return jnp.dot(split_ref[...], stacked, preferred_element_type=F32)
+
+
+def put_tiles(found, which, out_ref, pair):
+    for half in range(2):
+        for index, (i, j) in enumerate(which):
+            row = (2 * pair + half) * BCELLS + (i * BE + j) * BE
+            out_ref[row : row + SUB, :] = found[
+                index * SUB : (index + 1) * SUB, half * LANES : (half + 1) * LANES
+            ]
 
 
 def one_hot(code, out_ref, row, count, column):
@@ -258,8 +283,6 @@
 
 def whole_layer(field_ref, which, chunk):
     start = chunk * BCELLS
-    if which >= 4:
-        return field_ref[pl.ds(start + (which - 4) * (BE - 1), FACE, stride=BE), :]
     if which < 2:
         row = start + which * (BE - 1) * FACE
         return field_ref[row : row + FACE, :]
@@ -267,10 +290,18 @@
     return jnp.concatenate([field_ref[row : row + SUB, :] for row in rows], axis=0)
 
 
-def split_layers(field_ref, chunk, layers_ref):
-    for index, which in enumerate(SPLIT):
-        at = (index * CHUNKS + chunk) * LANES
-        layers_ref[:, at : at + LANES] = halves(whole_layer(field_ref, which, chunk))
+def split_layers(field_ref, ends, pair, layers_ref):
+    for half in range(2):
+        chunk = 2 * pair + half
+        for index, which in enumerate(SPLIT):
+            at = (index * CHUNKS + chunk) * LANES
+            if which >= 4:
+                value = ends[
+                    (which - 4) * FACE : (which - 3) * FACE, half * LANES : (half + 1) * LANES
+                ]
+            else:
+                value = whole_layer(field_ref, which, chunk)
+            layers_ref[:, at : at + LANES] = halves(value)
 
 
 def pack(field_ref, layers_ref, sent_ref, send_ref, odd, cross_ref, inside_ref):
@@ -349,17 +380,19 @@
                 faces_ref[base : base + SUB, :] = found[part]
 
 
-def local_kernel(known, theta_ref, codes_ref, field_ref, layers_ref, local_ref, *refs):
+def local_kernel(
+    known, theta_ref, codes_ref, old_field_ref, layers_ref, local_ref, core_ref, *refs
+):
     basis = refs[:known]
+    del old_field_ref
+    refs = refs[known:]
     faces_ref, beside_ref, sums_ref = refs[-3:]
     if known > 1:
-        diagonal_ref, gram_in_ref, out_ref, gram_ref = refs[known:-3]
+        diagonal_ref, gram_in_ref, out_ref, gram_ref, field_ref = refs[:5]
         gram_in = gram_in_ref[...]
     else:
-        counts_ref, before_ref, old_ref, cross_ref, inside_ref, out_ref, gram_ref, diagonal_ref = (
-            refs[1:9]
-        )
-        turned_ref = refs[9]
+        counts_ref, before_ref, old_ref, cross_ref, inside_ref = refs[:5]
+        out_ref, gram_ref, field_ref, diagonal_ref, turned_ref = refs[5:10]
         gram_in = jnp.zeros((SUB, LANES), F32)
         assemble(
             counts_ref, count_of(before_ref, 0), old_ref, cross_ref, inside_ref, diagonal_ref, turned_ref
@@ -399,6 +432,8 @@
                     old = newest if k == known - 1 else ref[rows, :]
                     sums[k] = sums[k] + newest * old
 
+    for pair in range(CHUNKS // 2):
+        put_tiles(precondition(core_ref, basis[-1], pair), CORE, field_ref, pair)
     gather_layers(0, codes_ref, field_ref, layers_ref, local_ref, faces_ref)
     for pair in range(CHUNKS // 2):
         if pair + 1 < CHUNKS // 2:
@@ -474,9 +509,9 @@
 ):
     for pair in range(CHUNKS // 2):
         before(pair)
-        precondition(split_ref, value_ref, field_ref, pair)
-        split_layers(field_ref, 2 * pair, layers_ref)
-        split_layers(field_ref, 2 * pair + 1, layers_ref)
+        found = precondition(split_ref, value_ref, pair)
+        put_tiles(found, SHELL, field_ref, pair)
+        split_layers(field_ref, found[SHELL_ROWS:, :], pair, layers_ref)
     pack(field_ref, layers_ref, sent_ref, send_ref, odd, cross_ref, inside_ref)
 
 
@@ -637,7 +672,8 @@
     field_type = of(CHUNKS * BCELLS)
     out_type = jax.ShapeDtypeStruct((BCELLS, BDEV), F32)
     halo_type = of(2 * FACE)
-    split_type = jax.ShapeDtypeStruct((BCELLS, 3 * BCELLS), jnp.bfloat16)
+    split_type = jax.ShapeDtypeStruct((SHELL_ROWS + 2 * FACE, 3 * BCELLS), jnp.bfloat16)
+    core_type = jax.ShapeDtypeStruct((BCELLS - SHELL_ROWS, 3 * BCELLS), jnp.bfloat16)
     turned = pltpu.VMEM((2, BCELLS, LANES), F32)
     layers = [
         pltpu.VMEM((CHUNKS * 6 * FACE, LANES), F32),
@@ -675,10 +711,11 @@
     )
     diagonal_cross = swapped(cross, True)
     diagonal_inside = swapped(inside, False)
-    split, theta, sent, taken, local = call(
+    split, core, theta, sent, taken, local = call(
         prepare_kernel,
         (
             split_type,
+            core_type,
             of(SUB),
             jax.ShapeDtypeStruct((len(SENT) * BDEV, 2 * HMAX), jnp.bfloat16),
             jax.ShapeDtypeStruct((2 * HMAX, len(PRODUCT) * BDEV), jnp.bfloat16),
@@ -686,7 +723,7 @@
         ),
         (rank, block_inverse, face_source, send_layers),
         [SMEM] + [VMEM] * 3,
-        (VMEM,) * 5,
+        (VMEM,) * 6,
     )
     before, rhs, field, packed, to_cross, to_inside = call(
         first_kernel,
@@ -701,12 +738,12 @@
     )
     diagonal = gram = None
     basis = [rhs]
-    fields = [field]
+    fields = []
     for known in range(1, BASIS):
         from_cross = swapped(to_cross, True)
         from_inside = swapped(to_inside, False)
-        args = [theta, face_source, field, packed, local] + basis
-        outs = [field_type, of(SUB)]
+        args = [theta, face_source, field, packed, local, core] + basis
+        outs = [field_type, of(SUB), field_type]
         if known > 1:
             args += [diagonal, gram]
             scratch = layers + [sums]
@@ -723,10 +760,12 @@
             scratch,
             flops=10**9,
             bytes_accessed=4 * MIB,
+            aliases={2: 2},
         )
-        partial, gram = found[:2]
+        partial, gram, field = found[:3]
+        fields.append(field)
         if known == 1:
-            diagonal = found[2]
+            diagonal = found[3]
         if known < BASIS - 1:
             value, field, packed, to_cross, to_inside = call(
                 next_kernel,
@@ -741,7 +780,6 @@
                 bytes_accessed=12 * MIB,
                 aliases={5: 0},
             )
-            fields.append(field)
         else:
             value, copies = call(
                 end_kernel,

time: 98.8 us -> 97.4 us (0.986)
  blocking collectives: 30.2 us -> 27.5 us
    all_to_all x1, blocking collectives: 30.2 us -> 27.5 us  [per_device(): lax.all_to_all(copies, AXES, split_axis=0, concat_axis=0, tiled=True)]
  transfers between devices with their start and end apart: 12 -> 12, of which waited for: 1 -> 1; matrix products, arithmetic and copies ran while one was open for 0% -> 0% of each run, Pallas kernels for 21% -> 24%
where the time goes in v8:
time: 97.4 us; the launch traced here: 97 us
  Pallas kernels  41.2 us (42%)
  blocking collectives  27.5 us (28%)
  starting transfers between devices  25.7 us (26%)
  between operations  1.22 us (1%)
    pallas_call x13, Pallas kernels, call(): pl.pallas_call(kernel, out_shape=outs, in_specs=in_specs, out_specs=out_s...  41.2 us
    all_to_all x1, blocking collectives, per_device(): lax.all_to_all(copies, AXES, split_axis=0, concat_axis=0, tiled=True)  27.5 us
    ppermute x12, starting transfers between devices, swapped(): lax.ppermute(value, AXES, pairs + [(high, low) for low, high in pairs])  25.7 us
  transfers between devices with their start and end apart: 12, of which 1 were waited for; matrix products, arithmetic and copies ran while one was open for 0% of the time, Pallas kernels for 24%

profile of v8, /device:TPU:1, one launch (start us, length us, event | category | flops | bytes accessed | tf_op | source)
XLA Modules:
  0.0 97.0 jit_solution(1835109225696232556)
XLA Ops:
  0.7 0.8 copy-done.7
  1.5 2.9 %shard_map.78 = (s32[8,128]{1,0:T(8,128)S(1)}, f32[1032,128]{1,0:T(8,128)}, f32[1032,128]{1,0:T(8,128)S(1)}) custom-call(s32[1]{0:T(128)} %bitcast.rank_ref, s32[12,128]{1,0:T(8,128)S(1)} %bitcast.8, f32[512,1536]{1,0:T(8,128)} %old_ref.4), custom_call_target="tpu_custom_call" | custom-call | tf_op jit(solution)/shard_map/pallas_call | solution.py:50
  4.4 0.0 copy-start.4
  4.4 0.0 copy-start.5
  4.4 0.0 copy-start.6
  4.4 4.6 %collective-permute-start = (f32[1032,128]{1,0:T(8,128)}, f32[1032,128]{1,0:T(8,128)S(1)}, u32[]{:S(2)}, u32[]{:S(2)}) collective-permute-start(f32[1032,128]{1,0:T(8,128)} %get-tuple-element.51), channel_id=1, source_target_pairs={{1,2},{3,4},{5,6},{7,8},{9,10},{11,12},{13,14},{15,16},{17,18},{19... | collective-permute-start | bytes 1585160 | tf_op jit(solution)/shard_map/ppermute | solution.py:44
  9.0 0.1 collective-permute-start.1
  9.2 0.5 shard_map.80
  9.6 3.6 %collective-permute-start.4 = (f32[1024,128]{1,0:T(8,128)S(1)}, f32[1024,128]{1,0:T(8,128)S(1)}, u32[]{:S(2)}, u32[]{:S(2)}) collective-permute-start(f32[1024,128]{1,0:T(8,128)S(1)} %get-tuple-element.63), channel_id=1, source_target_pairs={{1,2},{3,4},{5,6},{7,8},{9,10},{11,12},{13,14},{15,16},{17,18},{19... | collective-permute-start | bytes 1572872 | tf_op jit(solution)/shard_map/ppermute | solution.py:44
  13.3 0.1 collective-permute-start.5
  13.4 2.2 %shard_map.77 = (bf16[352,1536]{1,0:T(8,128)(2,1)S(1)}, bf16[288,1536]{1,0:T(8,128)(2,1)S(1)}, f32[8,128]{1,0:T(8,128)S(1)}, bf16[4096,512]{1,0:T(8,128)(2,1)S(1...) custom-call(s32[1]{0:T(128)} %bitcast.rank_ref, f32[512,512]{1,0:T(8,128)S(1)} %copy-done.5, ...), custom_call_target="tpu_custom_call" | custom-call | tf_op jit(solution)/shard_map/pallas_call | solution.py:50
  15.6 0.5 collective-permute-done.cross_ref
  16.1 2.8 %shard_map.79 = (s32[8,128]{1,0:T(8,128)S(1)}, f32[4096,128]{1,0:T(8,128)S(1)}, f32[4096,128]{1,0:T(8,128)S(1)}, bf16[128,5120]{1,0:T(8,128)(2,1)S(1)}, f32[128,128]{1,0:T(8,128)S(1)}, /*index=5*/f32[128,128]{1,0:T(8,128)S(1)}) custom-call(s32[8,128]{1,0:T(8,128)S(1)} %get-tuple-element.50.counts_ref.refs_1_, f32[512,1536]{1,0:T(8,128)S(1)} %copy-done.1, ...), custom_call_target="tpu_custom_call" | custom-call | flops 1000000000 | bytes 8388608 | tf_op jit(solution)/shard_map/pallas_call | solution.py:50
  18.9 3.6 %collective-permute-start.2 = (f32[128,128]{1,0:T(8,128)S(1)}, f32[128,128]{1,0:T(8,128)S(1)}, u32[]{:S(2)}, u32[]{:S(2)}) collective-permute-start(f32[128,128]{1,0:T(8,128)S(1)} %get-tuple-element.55), channel_id=1, source_target_pairs={{1,2},{3,4},{5,6},{7,8},{9,10},{11,12},{13,14},{15,16},{17,18},{19... | collective-permute-start | bytes 196616 | tf_op jit(solution)/shard_map/ppermute | solution.py:44
  22.6 0.3 collective-permute-start.3
  22.9 4.5 %shard_map.81 = (f32[4096,128]{1,0:T(8,128)S(1)}, f32[8,128]{1,0:T(8,128)S(1)}, f32[4096,128]{1,0:T(8,128)S(1)}, f32[4096,128]{1,0:T(8,128)S(1)}) custom-call(f32[8,128]{1,0:T(8,128)S(1)} %get-tuple-element.49.theta_ref, s32[6,1024]{1,0:T(8,128)S(1)} %copy-done.4, f32[4096,128]{1,0:T(8,128)S(1)} %get-tuple-element.57.old_field_ref, ...), custom_call_target="tpu_custom_call", output_to_operand_aliasing={{2}: (2, {})} | custom-call | flops 1000000000 | bytes 4194304 | tf_op jit(solution)/shard_map/pallas_call | solution.py:50
  27.3 0.0 copy-start.2
  27.4 3.2 %shard_map.82 = (f32[4096,128]{1,0:T(8,128)S(1)}, f32[4096,128]{1,0:T(8,128)S(1)}, bf16[128,5120]{1,0:T(8,128)(2,1)S(1)}, f32[128,128]{1,0:T(8,128)S(1)}, f32[128,128]{1,0:T(8,128)S(1)}) custom-call(s32[8,128]{1,0:T(8,128)S(1)} %get-tuple-element.50.counts_ref.refs_1_, s32[6,1024]{1,0:T(8,128)S(1)} %copy-done.4, ...), custom_call_target="tpu_custom_call", output_to_operand_aliasing={{0}: (5, {})} | custom-call | flops 1000000000 | bytes 12582912 | tf_op jit(solution)/shard_map/pallas_call | solution.py:50
  30.6 3.5 %collective-permute-start.6 = (f32[128,128]{1,0:T(8,128)S(1)}, f32[128,128]{1,0:T(8,128)S(1)}, u32[]{:S(2)}, u32[]{:S(2)}) collective-permute-start(f32[128,128]{1,0:T(8,128)S(1)} %get-tuple-element.67), channel_id=1, source_target_pairs={{1,2},{3,4},{5,6},{7,8},{9,10},{11,12},{13,14},{15,16},{17,18},{19... | collective-permute-start | bytes 196616 | tf_op jit(solution)/shard_map/ppermute | solution.py:44
  34.1 0.3 collective-permute-start.7
  34.4 4.3 %shard_map.83 = (f32[4096,128]{1,0:T(8,128)S(1)}, f32[8,128]{1,0:T(8,128)S(1)}, f32[4096,128]{1,0:T(8,128)S(1)}) custom-call(f32[8,128]{1,0:T(8,128)S(1)} %get-tuple-element.49.theta_ref, s32[6,1024]{1,0:T(8,128)S(1)} %copy-done.4, f32[4096,128]{1,0:T(8,128)S(1)} %get-tuple-element.69.old_field_ref, ...), custom_call_target="tpu_custom_call", output_to_operand_aliasing={{2}: (2, {})} | custom-call | flops 1000000000 | bytes 4194304 | tf_op jit(solution)/shard_map/pallas_call | solution.py:50
  38.7 3.2 %shard_map.84 = (f32[4096,128]{1,0:T(8,128)S(1)}, f32[4096,128]{1,0:T(8,128)S(1)}, bf16[128,5120]{1,0:T(8,128)(2,1)S(1)}, f32[128,128]{1,0:T(8,128)S(1)}, f32[128,128]{1,0:T(8,128)S(1)}) custom-call(s32[8,128]{1,0:T(8,128)S(1)} %get-tuple-element.50.counts_ref.refs_1_, s32[6,1024]{1,0:T(8,128)S(1)} %copy-done.4, ...), custom_call_target="tpu_custom_call", output_to_operand_aliasing={{0}: (5, {})} | custom-call | flops 1000000000 | bytes 12582912 | tf_op jit(solution)/shard_map/pallas_call | solution.py:50
  41.9 3.2 %collective-permute-start.8 = (f32[128,128]{1,0:T(8,128)S(1)}, f32[128,128]{1,0:T(8,128)S(1)}, u32[]{:S(2)}, u32[]{:S(2)}) collective-permute-start(f32[128,128]{1,0:T(8,128)S(1)} %get-tuple-element.75), channel_id=1, source_target_pairs={{1,2},{3,4},{5,6},{7,8},{9,10},{11,12},{13,14},{15,16},{17,18},{19... | collective-permute-start | bytes 196616 | tf_op jit(solution)/shard_map/ppermute | solution.py:44
  45.2 0.3 collective-permute-start.9
  45.5 4.5 %shard_map.85 = (f32[4096,128]{1,0:T(8,128)S(1)}, f32[8,128]{1,0:T(8,128)S(1)}, f32[4096,128]{1,0:T(8,128)S(1)}) custom-call(f32[8,128]{1,0:T(8,128)S(1)} %get-tuple-element.49.theta_ref, s32[6,1024]{1,0:T(8,128)S(1)} %copy-done.4, f32[4096,128]{1,0:T(8,128)S(1)} %get-tuple-element.77.old_field_ref, ...), custom_call_target="tpu_custom_call", output_to_operand_aliasing={{2}: (2, {})} | custom-call | flops 1000000000 | bytes 4194304 | tf_op jit(solution)/shard_map/pallas_call | solution.py:50
  50.0 3.2 %shard_map.86 = (f32[4096,128]{1,0:T(8,128)S(1)}, f32[4096,128]{1,0:T(8,128)S(1)}, bf16[128,5120]{1,0:T(8,128)(2,1)S(1)}, f32[128,128]{1,0:T(8,128)S(1)}, f32[128,128]{1,0:T(8,128)S(1)}) custom-call(s32[8,128]{1,0:T(8,128)S(1)} %get-tuple-element.50.counts_ref.refs_1_, s32[6,1024]{1,0:T(8,128)S(1)} %copy-done.4, ...), custom_call_target="tpu_custom_call", output_to_operand_aliasing={{0}: (5, {})} | custom-call | flops 1000000000 | bytes 12582912 | tf_op jit(solution)/shard_map/pallas_call | solution.py:50
  53.3 5.6 %collective-permute-start.10 = (f32[128,128]{1,0:T(8,128)S(1)}, f32[128,128]{1,0:T(8,128)S(1)}, u32[]{:S(2)}, u32[]{:S(2)}) collective-permute-start(f32[128,128]{1,0:T(8,128)S(1)} %get-tuple-element.82), channel_id=1, source_target_pairs={{1,2},{3,4},{5,6},{7,8},{9,10},{11,12},{13,14},{15,16},{17,18},{19... | collective-permute-start | bytes 196616 | tf_op jit(solution)/shard_map/ppermute | solution.py:44
  58.9 0.4 collective-permute-start.11
  59.3 4.9 %shard_map.87 = (f32[4096,128]{1,0:T(8,128)S(1)}, f32[8,128]{1,0:T(8,128)S(1)}, f32[4096,128]{1,0:T(8,128)S(1)}) custom-call(f32[8,128]{1,0:T(8,128)S(1)} %get-tuple-element.49.theta_ref, s32[6,1024]{1,0:T(8,128)S(1)} %copy-done.4, f32[4096,128]{1,0:T(8,128)S(1)} %get-tuple-element.84.old_field_ref, ...), custom_call_target="tpu_custom_call", output_to_operand_aliasing={{2}: (2, {})} | custom-call | flops 1000000000 | bytes 4194304 | tf_op jit(solution)/shard_map/pallas_call | solution.py:50
  64.2 2.0 %shard_map.88 = (f32[4096,128]{1,0:T(8,128)S(1)}, f32[128,128]{1,0:T(8,128)S(1)}) custom-call(s32[8,128]{1,0:T(8,128)S(1)} %get-tuple-element.50.counts_ref.refs_1_, s32[6,1024]{1,0:T(8,128)S(1)} %copy-done.4, f32[128,128]{1,0:T(8,128)S(1)} %collective-permute-done.10.cross_ref, ...), custom_call_target="tpu_custom_call", output_to_operand_aliasing={{0}: (4, {})} | custom-call | flops 1000000000 | bytes 12582912 | tf_op jit(solution)/shard_map/pallas_call | solution.py:50
  66.2 27.5 %all_to_all.11 = f32[128,1,128]{2,1,0:T(1,128)S(1)} all-to-all(f32[128,1,128]{2,1,0:T(1,128)S(1)} %bitcast.7), channel_id=1, replica_groups=mesh['gx'=4,'gy'=4,'gz'=8] {'gx','gy','gz'}, dimensions={0} | all-to-all | bytes 131072 | tf_op jit(solution)/shard_map/all_to_all | solution.py:796
  93.7 3.1 %shard_map.89 = (f32[512,1024]{1,0:T(8,128)}, f32[512,1024]{1,0:T(8,128)}) custom-call(f32[8,128]{1,0:T(8,128)S(1)} %get-tuple-element.49.theta_ref, f32[128,128]{1,0:T(8,128)S(1)} %bitcast.6, f32[4096,128]{1,0:T(8,128)S(1)} %get-tuple-element.61.refs_0_, f32[4096,128]{1,0:T(8,128)S(1)} %get-tuple-element.71.refs_1_, ...), custom_call_target="tpu_custom_call" | custom-call | tf_op jit(solution)/shard_map/pallas_call | solution.py:50
  (22 shorter events, 0.1 us)
Async XLA Ops:
  0.6 8.5 %copy-start = (f32[512,1536]{1,0:T(8,128)S(1)}, f32[512,1536]{1,0:T(8,128)}, u32[]{:S(2)}) copy-start(f32[512,1536]{1,0:T(8,128)} %refs_3_.1) | copy-start | bytes 9437188
  0.6 0.8 copy-start.7
  4.4 9.0 %copy-start.4 = (s32[6,1024]{1,0:T(8,128)S(1)}, s32[6,1024]{1,0:T(8,128)}, u32[]{:S(2)}) copy-start(s32[6,1024]{1,0:T(8,128)} %codes_ref.17) | copy-start | bytes 73732
  4.4 9.0 %copy-start.5 = (f32[512,512]{1,0:T(8,128)S(1)}, f32[512,512]{1,0:T(8,128)}, u32[]{:S(2)}) copy-start(f32[512,512]{1,0:T(8,128)} %inverse_ref.1) | copy-start | bytes 3145732
  4.4 9.0 %copy-start.6 = (s32[2,256]{1,0:T(2,128)S(1)}, s32[2,256]{1,0:T(2,128)}, u32[]{:S(2)}) copy-start(s32[2,256]{1,0:T(2,128)} %send_ref.9) | copy-start | bytes 6148
  4.4 11.8 %collective-permute-start = (f32[1032,128]{1,0:T(8,128)}, f32[1032,128]{1,0:T(8,128)S(1)}, u32[]{:S(2)}, u32[]{:S(2)}) collective-permute-start(f32[1032,128]{1,0:T(8,128)} %get-tuple-element.51), channel_id=1, source_target_pairs={{1,2},{3,4},{5,6},{7,8},{9,10},{11,12},{13,14},{15,16},{17,18},{19... | collective-permute-start | bytes 1585160 | tf_op jit(solution)/shard_map/ppermute | solution.py:44
  9.0 7.1 %collective-permute-start.1 = (f32[1032,128]{1,0:T(8,128)S(1)}, f32[1032,128]{1,0:T(8,128)S(1)}, u32[]{:S(2)}, u32[]{:S(2)}) collective-permute-start(f32[1032,128]{1,0:T(8,128)S(1)} %get-tuple-element.52), channel_id=1, source_target_pairs={{0,1},{2,3},{4,5},{6,7},{8,9},{10,11},{12,13},{14,15},{16,17},{18,... | collective-permute-start | bytes 1585160 | tf_op jit(solution)/shard_map/ppermute | solution.py:44
  9.1 7.0 %copy-start.1 = (f32[512,1536]{1,0:T(8,128)S(1)}, f32[512,1536]{1,0:T(8,128)}, u32[]{:S(2)}) copy-start(f32[512,1536]{1,0:T(8,128)} %old_ref.4) | copy-start | bytes 9437188
  9.6 13.2 %collective-permute-start.4 = (f32[1024,128]{1,0:T(8,128)S(1)}, f32[1024,128]{1,0:T(8,128)S(1)}, u32[]{:S(2)}, u32[]{:S(2)}) collective-permute-start(f32[1024,128]{1,0:T(8,128)S(1)} %get-tuple-element.63), channel_id=1, source_target_pairs={{1,2},{3,4},{5,6},{7,8},{9,10},{11,12},{13,14},{15,16},{17,18},{19... | collective-permute-start | bytes 1572872 | tf_op jit(solution)/shard_map/ppermute | solution.py:44
  13.3 9.6 %collective-permute-start.5 = (f32[1024,128]{1,0:T(8,128)S(1)}, f32[1024,128]{1,0:T(8,128)S(1)}, u32[]{:S(2)}, u32[]{:S(2)}) collective-permute-start(f32[1024,128]{1,0:T(8,128)S(1)} %get-tuple-element.64), channel_id=1, source_target_pairs={{0,1},{2,3},{4,5},{6,7},{8,9},{10,11},{12,13},{14,15},{16,17},{18,... | collective-permute-start | bytes 1572872 | tf_op jit(solution)/shard_map/ppermute | solution.py:44
  18.9 8.4 %collective-permute-start.2 = (f32[128,128]{1,0:T(8,128)S(1)}, f32[128,128]{1,0:T(8,128)S(1)}, u32[]{:S(2)}, u32[]{:S(2)}) collective-permute-start(f32[128,128]{1,0:T(8,128)S(1)} %get-tuple-element.55), channel_id=1, source_target_pairs={{1,2},{3,4},{5,6},{7,8},{9,10},{11,12},{13,14},{15,16},{17,18},{19... | collective-permute-start | bytes 196616 | tf_op jit(solution)/shard_map/ppermute | solution.py:44
  22.6 4.8 %collective-permute-start.3 = (f32[128,128]{1,0:T(8,128)S(1)}, f32[128,128]{1,0:T(8,128)S(1)}, u32[]{:S(2)}, u32[]{:S(2)}) collective-permute-start(f32[128,128]{1,0:T(8,128)S(1)} %get-tuple-element.56), channel_id=1, source_target_pairs={{0,1},{2,3},{4,5},{6,7},{8,9},{10,11},{12,13},{14,15},{16,17},{18,... | collective-permute-start | bytes 196616 | tf_op jit(solution)/shard_map/ppermute | solution.py:44
  27.3 3.3 %copy-start.2 = (f32[4096,128]{1,0:T(8,128)}, f32[4096,128]{1,0:T(8,128)S(1)}, u32[]{:S(2)}) copy-start(f32[4096,128]{1,0:T(8,128)S(1)} %get-tuple-element.92.refs_5_) | copy-start | bytes 6291460
  30.6 8.1 %collective-permute-start.6 = (f32[128,128]{1,0:T(8,128)S(1)}, f32[128,128]{1,0:T(8,128)S(1)}, u32[]{:S(2)}, u32[]{:S(2)}) collective-permute-start(f32[128,128]{1,0:T(8,128)S(1)} %get-tuple-element.67), channel_id=1, source_target_pairs={{1,2},{3,4},{5,6},{7,8},{9,10},{11,12},{13,14},{15,16},{17,18},{19... | collective-permute-start | bytes 196616 | tf_op jit(solution)/shard_map/ppermute | solution.py:44
  34.1 4.6 %collective-permute-start.7 = (f32[128,128]{1,0:T(8,128)S(1)}, f32[128,128]{1,0:T(8,128)S(1)}, u32[]{:S(2)}, u32[]{:S(2)}) collective-permute-start(f32[128,128]{1,0:T(8,128)S(1)} %get-tuple-element.68), channel_id=1, source_target_pairs={{0,1},{2,3},{4,5},{6,7},{8,9},{10,11},{12,13},{14,15},{16,17},{18,... | collective-permute-start | bytes 196616 | tf_op jit(solution)/shard_map/ppermute | solution.py:44
  41.9 8.1 %collective-permute-start.8 = (f32[128,128]{1,0:T(8,128)S(1)}, f32[128,128]{1,0:T(8,128)S(1)}, u32[]{:S(2)}, u32[]{:S(2)}) collective-permute-start(f32[128,128]{1,0:T(8,128)S(1)} %get-tuple-element.75), channel_id=1, source_target_pairs={{1,2},{3,4},{5,6},{7,8},{9,10},{11,12},{13,14},{15,16},{17,18},{19... | collective-permute-start | bytes 196616 | tf_op jit(solution)/shard_map/ppermute | solution.py:44
  45.2 4.8 %collective-permute-start.9 = (f32[128,128]{1,0:T(8,128)S(1)}, f32[128,128]{1,0:T(8,128)S(1)}, u32[]{:S(2)}, u32[]{:S(2)}) collective-permute-start(f32[128,128]{1,0:T(8,128)S(1)} %get-tuple-element.76), channel_id=1, source_target_pairs={{0,1},{2,3},{4,5},{6,7},{8,9},{10,11},{12,13},{14,15},{16,17},{18,... | collective-permute-start | bytes 196616 | tf_op jit(solution)/shard_map/ppermute | solution.py:44
  53.3 10.9 %collective-permute-start.10 = (f32[128,128]{1,0:T(8,128)S(1)}, f32[128,128]{1,0:T(8,128)S(1)}, u32[]{:S(2)}, u32[]{:S(2)}) collective-permute-start(f32[128,128]{1,0:T(8,128)S(1)} %get-tuple-element.82), channel_id=1, source_target_pairs={{1,2},{3,4},{5,6},{7,8},{9,10},{11,12},{13,14},{15,16},{17,18},{19... | collective-permute-start | bytes 196616 | tf_op jit(solution)/shard_map/ppermute | solution.py:44
  58.9 5.3 %collective-permute-start.11 = (f32[128,128]{1,0:T(8,128)S(1)}, f32[128,128]{1,0:T(8,128)S(1)}, u32[]{:S(2)}, u32[]{:S(2)}) collective-permute-start(f32[128,128]{1,0:T(8,128)S(1)} %get-tuple-element.83), channel_id=1, source_target_pairs={{0,1},{2,3},{4,5},{6,7},{8,9},{10,11},{12,13},{14,15},{16,17},{18,... | collective-permute-start | bytes 196616 | tf_op jit(solution)/shard_map/ppermute | solution.py:44
  64.2 29.5 %copy-start.3 = (f32[4096,128]{1,0:T(8,128)S(1)}, f32[4096,128]{1,0:T(8,128)}, u32[]{:S(2)}) copy-start(f32[4096,128]{1,0:T(8,128)} %copy-done.2) | copy-start | bytes 6291460
